TPU v7x, 512 devices: a whole 4x8x8 slice. The times are simulated.
512 devices in a mesh: seq: 64 (over y, z_lo, core), dp: 8 (over z_hi, x).
Axes of the slice: x: 4, y: 8, z: 8 (z_hi: 2, z_lo: 4; z = z_hi * 4 + z_lo), core: 2. Of those that a mesh axis runs over, the one named last changes fastest.
Arguments:
- query_rows: bfloat16 [8, 64, 256, 1024], P('dp', 'seq'), may hold values from -8 to 8
- key_rows: bfloat16 [8, 64, 256, 1024], P('dp', 'seq'), may hold values from -8 to 8
- value_rows: bfloat16 [8, 64, 256, 1024], P('dp', 'seq'), may hold values from -6 to 6
- upstream: bfloat16 [8, 64, 256, 1024], P('dp', 'seq'), may hold values from -6 to 6
- input_weights: bfloat16 [1024, 3072], P('seq'), may hold values from -0.1875 to 0.1875
- output_weight: bfloat16 [1024, 1024], P('seq'), may hold values from -0.1875 to 0.1875
Outputs:
- input_gradient: bfloat16 [8, 64, 256, 1024], P('dp', 'seq')
- weight_gradient: float32 [1024, 1024], P('seq')
All inputs are finite; a program needn't handle non-finite values.
Results may differ from a plain program's by a relative error of at most 0.0067.
Values may be sent and summed in bfloat16 or wider, within the bound.
No kernel may reach another device: no remote copies, remote signals or barrier semaphores. Data moves between devices by JAX's collectives and lax.ppermute only.
A program may use at most 64 MiB of HBM per device.

v0:
```python
import math

import jax
import jax.numpy as jnp
from jax import lax
from jax.sharding import PartitionSpec as P

HEAD_DIM = 64
CLIP_LEN = 32


def attention_grads(query_block, key_block, value_block, context_grad):
    frame_count = query_block.shape[1]
    patch_count = query_block.shape[2]
    head_count = query_block.shape[3] // HEAD_DIM
    layout = (frame_count // CLIP_LEN, CLIP_LEN, patch_count, head_count, HEAD_DIM)
    score_scale = 1.0 / math.sqrt(HEAD_DIM)
    query_heads = query_block.reshape(layout)
    key_heads = key_block.reshape(layout)
    value_heads = value_block.reshape(layout)
    grad_heads = context_grad.reshape(layout)
    scores = (
        jnp.einsum("ctphe,csphe->cphts", query_heads, key_heads, preferred_element_type=jnp.float32)
        * score_scale
    )
    attention = jax.nn.softmax(scores, axis=-1)
    attention_b = attention.astype(jnp.bfloat16)
    context = jnp.einsum(
        "cphts,csphe->ctphe", attention_b, value_heads, preferred_element_type=jnp.float32
    )
    grad_scores = jnp.einsum(
        "ctphe,csphe->cphts", grad_heads, value_heads, preferred_element_type=jnp.float32
    )
    row_total = jnp.sum(attention * grad_scores, axis=-1, keepdims=True)
    score_grad = (attention * (grad_scores - row_total) * score_scale).astype(jnp.bfloat16)
    grad_query = jnp.einsum(
        "cphts,csphe->ctphe", score_grad, key_heads, preferred_element_type=jnp.float32
    )
    grad_key = jnp.einsum(
        "cphts,ctphe->csphe", score_grad, query_heads, preferred_element_type=jnp.float32
    )
    grad_value = jnp.einsum(
        "cphts,ctphe->csphe", attention_b, grad_heads, preferred_element_type=jnp.float32
    )
    shape_back = query_block.shape
    return (
        context.astype(jnp.bfloat16).reshape(shape_back),
        grad_query.astype(jnp.bfloat16).reshape(shape_back),
        grad_key.astype(jnp.bfloat16).reshape(shape_back),
        grad_value.astype(jnp.bfloat16).reshape(shape_back),
    )


def on_device(query_rows, key_rows, value_rows, upstream, input_weights, output_weight):
    feature_width = query_rows.shape[3]
    seq_count = lax.axis_size("seq")
    group_tokens = query_rows.shape[1] * seq_count * query_rows.shape[2]
    factor = 1.0 / (lax.axis_size("dp") * math.sqrt(group_tokens))
    contract_last = (((1,), (1,)), ((), ()))
    full_input, full_output = (
        lax.all_gather(input_weights, "seq", axis=0, tiled=True),
        lax.all_gather(output_weight, "seq", axis=0, tiled=True),
    )
    flat = upstream.reshape(-1, feature_width)
    result = lax.dot_general(flat, full_output, contract_last, preferred_element_type=jnp.float32)
    context_grad = result.astype(jnp.bfloat16).reshape(upstream.shape)
    moved = (
        lax.all_to_all(query_rows, "seq", split_axis=2, concat_axis=1, tiled=True),
        lax.all_to_all(key_rows, "seq", split_axis=2, concat_axis=1, tiled=True),
        lax.all_to_all(value_rows, "seq", split_axis=2, concat_axis=1, tiled=True),
        lax.all_to_all(context_grad, "seq", split_axis=2, concat_axis=1, tiled=True),
    )
    results = attention_grads(moved[0], moved[1], moved[2], moved[3])
    returned = (
        lax.all_to_all(results[0], "seq", split_axis=1, concat_axis=2, tiled=True),
        lax.all_to_all(results[1], "seq", split_axis=1, concat_axis=2, tiled=True),
        lax.all_to_all(results[2], "seq", split_axis=1, concat_axis=2, tiled=True),
        lax.all_to_all(results[3], "seq", split_axis=1, concat_axis=2, tiled=True),
    )
    grad_query = returned[1]
    total = lax.dot_general(
        grad_query.reshape(-1, feature_width),
        full_input[:, :feature_width],
        contract_last,
        preferred_element_type=jnp.float32,
    )
    total = total + lax.dot_general(
        returned[2].reshape(-1, feature_width),
        full_input[:, feature_width : 2 * feature_width],
        contract_last,
        preferred_element_type=jnp.float32,
    )
    total = total + lax.dot_general(
        returned[3].reshape(-1, feature_width),
        full_input[:, 2 * feature_width :],
        contract_last,
        preferred_element_type=jnp.float32,
    )
    input_gradient = total.astype(jnp.bfloat16).reshape(grad_query.shape)
    context_flat = returned[0].reshape(-1, feature_width)
    grad_flat = upstream.reshape(-1, feature_width)
    share = lax.psum_scatter(
        lax.dot_general(
            context_flat, grad_flat, (((0,), (0,)), ((), ())), preferred_element_type=jnp.float32
        ),
        "seq",
        scatter_dimension=0,
        tiled=True,
    )
    weight_gradient = lax.psum(share, "dp") * factor
    return (input_gradient, weight_gradient)


def solution(mesh):
    return jax.shard_map(
        on_device,
        mesh=mesh,
        in_specs=(
            P("dp", "seq", None, None),
            P("dp", "seq", None, None),
            P("dp", "seq", None, None),
            P("dp", "seq", None, None),
            P("seq", None),
            P("seq", None),
        ),
        out_specs=(P("dp", "seq", None, None), P("seq", None)),
        check_vma=False,
    )
```

profile of v0, /device:TPU:1, one launch (start us, length us, event | category | flops | bytes accessed | tf_op | source)
XLA Modules:
  0.0 788.5 jit_solution(18000172852631370204)
XLA Ops:
  7.2 1.9 copy.135
  9.1 0.5 broadcast.26
  9.6 3.7 reduce.10
  13.3 1.1 reshape.112
  14.4 14.6 %all-to-all-start = ((bf16[64,2,2048]{2,1,0:T(2,128)(2,1)}), bf16[64,2,2048]{2,1,0:T(2,128)(2,1)S(1)}, u32[]{:S(2)}, u32[]{:S(2)}) async-start(bf16[64,2,2048]{2,1,0:T(2,128)(2,1)} %reshape.112), calls=%async_computation | async-start | bytes 1048576 | tf_op jit(solution)/shard_map/all_to_all | solution.py:68
  29.0 0.8 copy.134
  29.9 3.8 reduce.9
  33.6 1.1 reshape.110
  34.8 12.0 %all-to-all-done = bf16[64,2,2048]{2,1,0:T(2,128)(2,1)S(1)} async-done(((bf16[64,2,2048]{2,1,0:T(2,128)(2,1)}), bf16[64,2,2048]{2,1,0:T(2,128)(2,1)S(1)}, u32[]{:S(2)}, u32[]{:S(2)}) %all-to-all-start) | async-done | bytes 524320 | tf_op jit(solution)/shard_map/all_to_all | solution.py:68
  46.8 5.9 all-to-all-start.1
  52.6 0.8 copy.132
  53.5 3.7 reduce.11
  57.2 1.1 reshape.114
  58.3 11.9 %all-to-all-done.1 = bf16[64,2,2048]{2,1,0:T(2,128)(2,1)S(1)} async-done(((bf16[64,2,2048]{2,1,0:T(2,128)(2,1)}), bf16[64,2,2048]{2,1,0:T(2,128)(2,1)S(1)}, u32[]{:S(2)}, u32[]{:S(2)}) %all-to-all-start.1) | async-done | bytes 524320 | tf_op jit(solution)/shard_map/all_to_all | solution.py:69
  70.2 5.6 all-to-all-start.3
  75.9 0.5 reshape.113
  76.4 3.0 bitcast_reduce_fusion.1
  79.4 1.6 reshape.85
  81.1 0.5 reshape.111
  81.6 3.0 bitcast_reduce_fusion.2
  84.6 0.7 reshape.86
  85.3 8.2 %all-to-all-done.3 = bf16[64,2,2048]{2,1,0:T(2,128)(2,1)S(1)} async-done(((bf16[64,2,2048]{2,1,0:T(2,128)(2,1)}), bf16[64,2,2048]{2,1,0:T(2,128)(2,1)S(1)}, u32[]{:S(2)}, u32[]{:S(2)}) %all-to-all-start.3) | async-done | bytes 524320 | tf_op jit(solution)/shard_map/all_to_all | solution.py:70
  93.5 0.7 reshape.115
  94.3 3.0 bitcast_reduce_fusion
  97.3 0.7 reshape.90
  98.0 4.4 fusion.80
  102.4 2.5 fusion.24
  104.9 0.4 copy.91
  105.3 0.6 reshape.103
  106.0 23.1 %all_to_all.32 = bf16[1,64,4,1024]{3,2,0,1:T(4,128)(2,1)S(1)} all-to-all(bf16[1,64,4,1024]{3,2,0,1:T(4,128)(2,1)S(1)} %reshape.103), channel_id=1, replica_groups=mesh['seq'=64,'dp'=8] {'seq'}, dimensions={1} | all-to-all | bytes 1048576 | tf_op jit(solution)/shard_map/all_to_all | solution.py:75
  129.2 2.7 fusion.58
  131.9 0.7 all-gather.3.cloned.1.call-update
  132.7 279.7 %reduce-scatter.2.cloned.1.call-done = f32[16,1024]{1,0:T(8,128)} async-done(((f32[1024,1024]{1,0:T(8,128)}), f32[16,1024]{1,0:T(8,128)}) %reduce-scatter.2.cloned.1.call-update) | async-done | bytes 65552 | tf_op jit(solution)/shard_map/reduce_scatter | solution.py:102
  412.4 0.4 all-gather.5.cloned.1.call-start
  412.9 121.9 %all-gather.3.cloned.1.call-done = bf16[1024,1024]{1,0:T(8,128)(2,1)} async-done(((bf16[16,1024]{1,0:T(8,128)(2,1)}), bf16[1024,1024]{1,0:T(8,128)(2,1)}) %all-gather.3.cloned.1.call-update) | async-done | bytes 2097168 | tf_op jit(solution)/shard_map/all_gather | solution.py:62
  534.9 2.3 fusion.41
  537.2 0.8 copy.133
  538.0 3.7 reduce.8
  541.7 0.3 reshape.108
  542.1 24.7 %all_to_all.33 = bf16[64,2,2048]{2,1,0:T(2,128)(2,1)S(1)} all-to-all(bf16[64,2,2048]{2,1,0:T(2,128)(2,1)S(1)} %reshape.108), channel_id=1, replica_groups=mesh['seq'=64,'dp'=8] {'seq'}, dimensions={0} | all-to-all | bytes 1048576 | tf_op jit(solution)/shard_map/all_to_all | solution.py:71
  566.7 0.5 reshape.109
  567.3 3.0 bitcast_reduce_fusion.3
  570.3 0.7 reshape.89
  571.0 2.8 fusion.49
  573.8 6.1 fusion.26
  579.8 1.7 copy.89
  581.6 1.4 reshape.101
  583.0 5.7 all-to-all-start.5
  588.6 5.8 fusion.29
  594.5 1.7 copy.88
  596.2 1.5 reshape.100
  597.7 8.7 %all-to-all-done.5 = bf16[1,64,4,1024]{3,2,0,1:T(4,128)(2,1)S(1)} async-done(((bf16[1,64,4,1024]{3,2,0,1:T(4,128)(2,1)}), bf16[1,64,4,1024]{3,2,0,1:T(4,128)(2,1)S(1)}, u32[]{:S(2)}, u32[]{:S(2)}) %all-to-all-start.5) | async-done | bytes 524320 | tf_op jit(solution)/shard_map/all_to_all | solution.py:77
  606.4 5.6 all-to-all-start.4
  612.0 2.4 fusion.25
  614.4 0.4 copy.90
  614.8 1.4 reshape.102
  616.2 13.8 %all-to-all-done.4 = bf16[1,64,4,1024]{3,2,0,1:T(4,128)(2,1)S(1)} async-done(((bf16[1,64,4,1024]{3,2,0,1:T(4,128)(2,1)}), bf16[1,64,4,1024]{3,2,0,1:T(4,128)(2,1)S(1)}, u32[]{:S(2)}, u32[]{:S(2)}) %all-to-all-start.4) | async-done | bytes 524320 | tf_op jit(solution)/shard_map/all_to_all | solution.py:76
  630.1 5.4 all-to-all-start.6
  635.7 17.5 %all-to-all-done.6 = bf16[1,64,4,1024]{3,2,0,1:T(4,128)(2,1)S(1)} async-done(((bf16[1,64,4,1024]{3,2,0,1:T(4,128)(2,1)}), bf16[1,64,4,1024]{3,2,0,1:T(4,128)(2,1)S(1)}, u32[]{:S(2)}, u32[]{:S(2)}) %all-to-all-start.6) | async-done | bytes 524320 | tf_op jit(solution)/shard_map/all_to_all | solution.py:78
  653.3 1.5 broadcast_multiply_fusion
  654.8 119.1 %all-gather.5.cloned.1.call-done = bf16[1024,3072]{1,0:T(8,128)(2,1)} async-done(((bf16[16,3072]{1,0:T(8,128)(2,1)}), bf16[1024,3072]{1,0:T(8,128)(2,1)}) %all-gather.5.cloned.1.call-update) | async-done | bytes 6291472 | tf_op jit(solution)/shard_map/all_gather | solution.py:61
  773.9 2.3 fusion.2
  776.3 2.3 fusion.4
  778.6 3.2 fusion.42
  (25 shorter events, 0.8 us)
Async XLA Ops:
  7.2 122.0 %copy-start = (bf16[1,1,256,1024]{3,2,1,0:T(8,128)(2,1)S(1)}, bf16[1,1,256,1024]{3,2,1,0:T(8,128)(2,1)}, u32[]{:S(2)}) copy-start(bf16[1,1,256,1024]{3,2,1,0:T(8,128)(2,1)} %param.9) | copy-start | bytes 1572868
  9.1 19.9 %copy-start.5 = (bf16[1,1,256,1024]{3,2,1,0:T(8,128)(2,1)S(1)}, bf16[1,1,256,1024]{3,2,1,0:T(8,128)(2,1)}, u32[]{:S(2)}) copy-start(bf16[1,1,256,1024]{3,2,1,0:T(8,128)(2,1)} %param.7) | copy-start | bytes 1572868
  14.4 32.3 %all-to-all-start = ((bf16[64,2,2048]{2,1,0:T(2,128)(2,1)}), bf16[64,2,2048]{2,1,0:T(2,128)(2,1)S(1)}, u32[]{:S(2)}, u32[]{:S(2)}) async-start(bf16[64,2,2048]{2,1,0:T(2,128)(2,1)} %reshape.112), calls=%async_computation | async-start | bytes 1048576 | tf_op jit(solution)/shard_map/all_to_all | solution.py:68
  29.9 22.8 %copy-start.6 = (bf16[1,1,256,1024]{3,2,1,0:T(8,128)(2,1)S(1)}, bf16[1,1,256,1024]{3,2,1,0:T(8,128)(2,1)}, u32[]{:S(2)}) copy-start(bf16[1,1,256,1024]{3,2,1,0:T(8,128)(2,1)} %param.8) | copy-start | bytes 1572868
  46.8 23.5 %all-to-all-start.1 = ((bf16[64,2,2048]{2,1,0:T(2,128)(2,1)}), bf16[64,2,2048]{2,1,0:T(2,128)(2,1)S(1)}, u32[]{:S(2)}, u32[]{:S(2)}) async-start(bf16[64,2,2048]{2,1,0:T(2,128)(2,1)} %reshape.110), calls=%async_computation.1 | async-start | bytes 1048576 | tf_op jit(solution)/shard_map/all_to_all | solution.py:69
  70.2 23.3 %all-to-all-start.3 = ((bf16[64,2,2048]{2,1,0:T(2,128)(2,1)}), bf16[64,2,2048]{2,1,0:T(2,128)(2,1)S(1)}, u32[]{:S(2)}, u32[]{:S(2)}) async-start(bf16[64,2,2048]{2,1,0:T(2,128)(2,1)} %reshape.114), calls=%async_computation.3 | async-start | bytes 1048576 | tf_op jit(solution)/shard_map/all_to_all | solution.py:70
  75.8 336.5 %reduce-scatter.2.cloned.1.call-start = ((), (), s32[]{:S(2)}) async-start(), calls=%async_computation.11 | async-start | bytes 4259840 | tf_op jit(solution)/shard_map/reduce_scatter | solution.py:102
  85.3 12.7 %copy-start.3 = (bf16[2,32,4,16,64]{4,3,2,1,0:T(8,128)(2,1)}, bf16[2,32,4,16,64]{4,3,2,1,0:T(8,128)(2,1)S(1)}, u32[]{:S(2)}) copy-start(bf16[2,32,4,16,64]{4,3,2,1,0:T(8,128)(2,1)S(1)} %reshape.86) | copy-start | bytes 1572868
  131.9 403.0 %all-gather.3.cloned.1.call-start = ((), (), s32[]{:S(2)}) async-start(), calls=%async_computation.9 | async-start | bytes 2129920 | tf_op jit(solution)/shard_map/all_gather | solution.py:62
  132.6 520.7 %all-reduce.2.cloned.1.call-start = ((), (), s32[]{:S(2)}) async-start(), calls=%async_computation.12 | async-start | bytes 131072 | tf_op jit(solution)/shard_map/psum | solution.py:110
  412.4 361.6 %all-gather.5.cloned.1.call-start = ((), (), s32[]{:S(2)}) async-start(), calls=%async_computation.10 | async-start | bytes 6389760 | tf_op jit(solution)/shard_map/all_gather | solution.py:61
  570.9 2.8 copy-start.1
  579.8 8.8 %copy-start.4 = (bf16[2,32,4,16,64]{4,3,2,1,0:T(8,128)(2,1)S(1)}, bf16[2,32,4,16,64]{4,3,2,1,0:T(8,128)(2,1)}, u32[]{:S(2)}) copy-start(bf16[2,32,4,16,64]{4,3,2,1,0:T(8,128)(2,1)} %copy-done.3) | copy-start | bytes 1572868
  583.0 23.4 %all-to-all-start.5 = ((bf16[1,64,4,1024]{3,2,0,1:T(4,128)(2,1)}), bf16[1,64,4,1024]{3,2,0,1:T(4,128)(2,1)S(1)}, u32[]{:S(2)}, u32[]{:S(2)}) async-start(bf16[1,64,4,1024]{3,2,0,1:T(4,128)(2,1)} %reshape.101), calls=%async_computation.5 | async-start | bytes 1048576 | tf_op jit(solution)/shard_map/all_to_all | solution.py:77
  594.5 17.5 %copy-start.2 = (bf16[2,32,4,16,64]{4,3,2,1,0:T(8,128)(2,1)S(1)}, bf16[2,32,4,16,64]{4,3,2,1,0:T(8,128)(2,1)}, u32[]{:S(2)}) copy-start(bf16[2,32,4,16,64]{4,3,2,1,0:T(8,128)(2,1)} %copy-done.1) | copy-start | bytes 1572868
  606.4 23.7 %all-to-all-start.4 = ((bf16[1,64,4,1024]{3,2,0,1:T(4,128)(2,1)}), bf16[1,64,4,1024]{3,2,0,1:T(4,128)(2,1)S(1)}, u32[]{:S(2)}, u32[]{:S(2)}) async-start(bf16[1,64,4,1024]{3,2,0,1:T(4,128)(2,1)} %reshape.100), calls=%async_computation.4 | async-start | bytes 1048576 | tf_op jit(solution)/shard_map/all_to_all | solution.py:76
  630.1 23.1 %all-to-all-start.6 = ((bf16[1,64,4,1024]{3,2,0,1:T(4,128)(2,1)}), bf16[1,64,4,1024]{3,2,0,1:T(4,128)(2,1)S(1)}, u32[]{:S(2)}, u32[]{:S(2)}) async-start(bf16[1,64,4,1024]{3,2,0,1:T(4,128)(2,1)} %reshape.102), calls=%async_computation.6 | async-start | bytes 1048576 | tf_op jit(solution)/shard_map/all_to_all | solution.py:78
Sparse Core Ops, SparseCore 0:
  132.0 280.2 reduce-scatter.1
  414.7 120.0 all-gather.2
  538.0 107.1 all-reduce.1
  647.2 126.6 all-gather.4
where the time goes:
time: 797 us; the launch traced here: 789 us
  waiting for transfers between devices  594 us (75%)
  blocking collectives  47.8 us (6%)
  starting transfers between devices  43.2 us (5%)
  matrix products  36.8 us (5%)
  local copies, waits for them, and re-layouts  36.3 us (5%)
  other arithmetic  16.3 us (2%)
  between operations  14.4 us (2%)
    reduce_scatter x1, waiting for transfers between devices, on_device(): lax.psum_scatter(lax.dot_general(context_flat, grad_flat, (((0,), (0,)),...  280 us
    all_gather x1, waiting for transfers between devices, on_device(): lax.all_gather(output_weight, 'seq', axis=0, tiled=True)  122 us
    all_gather x1, waiting for transfers between devices, on_device(): lax.all_gather(input_weights, 'seq', axis=0, tiled=True)  119 us
    all_to_all x1, blocking collectives, on_device(): lax.all_to_all(context_grad, 'seq', split_axis=2, concat_axis=1, tiled=True)  24.7 us
    all_to_all x1, blocking collectives, on_device(): lax.all_to_all(results[0], 'seq', split_axis=1, concat_axis=2, tiled=True)  23.1 us
    all_to_all x1, waiting for transfers between devices, on_device(): lax.all_to_all(results[3], 'seq', split_axis=1, concat_axis=2, tiled=True)  17.5 us
  transfers between devices with their start and end apart: 10, of which 9 were waited for; matrix products, arithmetic and copies ran while one was open for 8% of the time, Pallas kernels for 0%

commit v1 on v0

v1 whole, which is shorter than its diff:
```python
import functools
import math

import jax
import jax.numpy as jnp
from jax import lax
from jax.experimental import pallas as pl
from jax.experimental.pallas import tpu as pltpu
from jax.sharding import Mesh
from jax.sharding import PartitionSpec as P

D = 1024
HEAD_DIM = 64
CLIP_LEN = 32
PATCH_BLOCK = 8
ROWS = CLIP_LEN * PATCH_BLOCK
PAIR = 2 * HEAD_DIM
SLICE = 256
CLIP_AXES = ("yl", "zl", "c")
Y_AXES = ("yh", "yl")
Z_AXES = ("zl", "zh")
NEG = -1e30


def ring(size, shift):
    return [(i, (i + shift) % size) for i in range(size)]


def z_ring(shift):
    def at(z):
        return (z % 4) * 2 + z // 4

    return [(at(z), at((z + shift) % 8)) for z in range(8)]


def dot(a, b, contract):
    return lax.dot_general(a, b, (contract, ((), ())), preferred_element_type=jnp.float32)


NN = ((1,), (0,))
NT = ((1,), (1,))
TN = ((0,), (0,))


def weight_rows(own, sibling, z_at, core, columns):
    parts = []
    for z_lo in range(4):
        step = lax.rem(z_lo - z_at + 4, 4)
        mine, other = own[step, 0][:, columns], sibling[step, 0][:, columns]
        first = core == 0
        parts.append(jnp.where(first, mine, other))
        parts.append(jnp.where(first, other, mine))
    return jnp.concatenate(parts, axis=0)


def attention_kernel(place, q_ref, k_ref, v_ref, u_ref, *refs):
    pieces, (g_ref, dw_ref, bias) = refs[:8], refs[8:]
    pair = pl.program_id(0)
    x_at, z_at, core = place[0], place[1], place[2]

    @pl.when(pair == 0)
    def _():
        row = lax.broadcasted_iota(jnp.int32, (ROWS, ROWS), 0)
        col = lax.broadcasted_iota(jnp.int32, (ROWS, ROWS), 1)
        bias[...] = jnp.where(lax.rem(row - col + ROWS, PATCH_BLOCK) == 0, 0.0, NEG)

    cg = jnp.zeros((ROWS, PAIR), jnp.float32)
    for d in range(4):
        w = weight_rows(pieces[d], pieces[4 + d], z_at, core, slice(None))
        at = pl.multiple_of(lax.rem(x_at + d, 4) * SLICE, SLICE)
        cg = cg + dot(u_ref[:, pl.ds(at, SLICE)], w, NT)
    cg = cg.astype(jnp.bfloat16)
    q, k, v = q_ref[...], k_ref[...], v_ref[...]
    first = lax.broadcasted_iota(jnp.int32, (ROWS, PAIR), 1) < HEAD_DIM
    zero = jnp.zeros((), jnp.bfloat16)
    context = grad_q = grad_k = grad_v = jnp.zeros((ROWS, PAIR), jnp.float32)
    for head in range(2):

        def only(a):
            return jnp.where(first, a, zero) if head == 0 else jnp.where(first, zero, a)

        q_h, k_h, v_h, cg_h = only(q), only(k), only(v), only(cg)
        scores = dot(q, k_h, NT) + bias[...]
        top = jnp.max(scores, axis=1, keepdims=True)
        e = jnp.exp2((scores - top) * (math.log2(math.e) / math.sqrt(HEAD_DIM)))
        attention = e * (1.0 / jnp.sum(e, axis=1, keepdims=True))
        attention_b = attention.astype(jnp.bfloat16)
        grad_scores = dot(cg, v_h, NT)
        total = jnp.sum(attention * grad_scores, axis=1, keepdims=True)
        score_grad = (attention * (grad_scores - total) * (1.0 / math.sqrt(HEAD_DIM))).astype(
            jnp.bfloat16
        )
        context = context + dot(attention_b, v_h, NN)
        grad_q = grad_q + dot(score_grad, k_h, NN)
        grad_k = grad_k + dot(score_grad, q_h, TN)
        grad_v = grad_v + dot(attention_b, cg_h, TN)
    for i, g in enumerate((grad_q, grad_k, grad_v)):
        at = pl.multiple_of(i * D + pair * PAIR, PAIR)
        g_ref[:, pl.ds(at, PAIR)] = g.astype(jnp.bfloat16)
    dw = dot(context.astype(jnp.bfloat16), u_ref[...], TN).astype(jnp.bfloat16)
    dw = dw.reshape(4, 2, 16, D)
    for c in range(2):
        rows = dw[:, c].reshape(64, D)
        for x in range(4):
            dw_ref[c, x, 0] = rows[:, x * SLICE : (x + 1) * SLICE]


def attention_call(place, moved, pieces):
    def column(base):
        return pl.BlockSpec((ROWS, PAIR), lambda i, s: (0, base + i))

    grid_spec = pltpu.PrefetchScalarGridSpec(
        num_scalar_prefetch=1,
        grid=(8,),
        in_specs=[
            column(0),
            column(8),
            column(16),
            pl.BlockSpec((ROWS, D), lambda i, s: (0, 3)),
        ]
        + [pl.BlockSpec((4, 1, 16, SLICE), lambda i, s: (0, i, 0, 3))] * 8,
        out_specs=[
            pl.BlockSpec((ROWS, 3 * D), lambda i, s: (0, 0)),
            pl.BlockSpec((2, 4, 1, 64, SLICE), lambda i, s: (0, 0, i, 0, 0)),
        ],
        scratch_shapes=[pltpu.VMEM((ROWS, ROWS), jnp.float32)],
    )
    return pl.pallas_call(
        attention_kernel,
        grid_spec=grid_spec,
        out_shape=[
            jax.ShapeDtypeStruct((ROWS, 3 * D), jnp.bfloat16),
            jax.ShapeDtypeStruct((2, 4, 8, 64, SLICE), jnp.bfloat16),
        ],
        compiler_params=pltpu.CompilerParams(vmem_limit_bytes=40 * 2**20),
        cost_estimate=pl.CostEstimate(
            flops=5 * 10**9, bytes_accessed=8 * 2**20, transcendentals=2**20
        ),
        name="attention_grads",
    )(place, moved, moved, moved, moved, *pieces)


def projection_kernel(place, g_ref, *refs):
    pieces, o_ref = refs[:8], refs[8]
    x_at, z_at, core = place[0], place[1], place[2]
    total = jnp.zeros((ROWS, PAIR), jnp.float32)
    for d in range(4):
        w = weight_rows(pieces[d], pieces[4 + d], z_at, core, slice(0, 3 * SLICE))
        at = pl.multiple_of(lax.rem(x_at + d, 4) * (3 * SLICE), 3 * SLICE)
        total = total + dot(g_ref[:, pl.ds(at, 3 * SLICE)], w, NT)
    o_ref[...] = total.astype(jnp.bfloat16)


def projection_call(place, grads, pieces):
    grid_spec = pltpu.PrefetchScalarGridSpec(
        num_scalar_prefetch=1,
        grid=(8,),
        in_specs=[pl.BlockSpec((ROWS, 3 * D), lambda i, s: (0, 0))]
        + [pl.BlockSpec((4, 1, 16, D), lambda i, s: (0, i, 0, 0))] * 8,
        out_specs=pl.BlockSpec((ROWS, PAIR), lambda i, s: (0, i)),
    )
    return pl.pallas_call(
        projection_kernel,
        grid_spec=grid_spec,
        out_shape=jax.ShapeDtypeStruct((ROWS, D), jnp.bfloat16),
        compiler_params=pltpu.CompilerParams(vmem_limit_bytes=40 * 2**20),
        cost_estimate=pl.CostEstimate(
            flops=2 * 10**9, bytes_accessed=8 * 2**20, transcendentals=0
        ),
        name="input_projection",
    )(place, grads, *pieces)


def spread(block, axes, perms):
    half = block.shape[0] // 2
    after = lax.ppermute(block, axes, perms(-1))
    before = lax.ppermute(block, axes, perms(1))
    far_a = lax.ppermute(before[:half], axes, perms(1))
    far_b = lax.ppermute(after[half:], axes, perms(-1))
    return [block, after, jnp.concatenate([far_a, far_b], axis=0), before]


def gather_weights(input_weights, output_weight):
    x_at = lax.axis_index("x")
    mine = jnp.concatenate(
        [
            lax.dynamic_slice(input_weights, (0, x_at * 3 * SLICE), (16, 3 * SLICE)),
            lax.dynamic_slice(output_weight, (0, x_at * SLICE), (16, SLICE)),
        ],
        axis=1,
    )
    rows = lax.all_to_all(
        jnp.broadcast_to(mine[None], (8, 16, D)), Y_AXES, 0, 0, tiled=True
    )
    plane = jnp.stack(spread(rows, Z_AXES, z_ring), axis=0)
    own = spread(plane, "x", functools.partial(ring, 4))
    return own + [lax.ppermute(piece, "c", ring(2, 1)) for piece in own]


def sum_weight_grad(partial, factor):
    x_at = lax.axis_index("x")
    pair = lax.all_to_all(partial, "c", 0, 0, tiled=True)
    pair = (pair[0].astype(jnp.float32) + pair[1].astype(jnp.float32)).astype(jnp.bfloat16)

    def for_x(shift):
        return lax.dynamic_index_in_dim(pair, lax.rem(x_at + shift, 4), 0, keepdims=False)

    row = for_x(0).astype(jnp.float32)
    for shift in (2, 1, 3):
        row = row + lax.ppermute(for_x(shift), "x", ring(4, shift)).astype(jnp.float32)
    row = row.astype(jnp.bfloat16).reshape(32, 16, SLICE)
    plane = lax.all_to_all(row, ("yh", "yl", "zl"), 0, 0, tiled=True)
    plane = jnp.sum(plane.astype(jnp.float32), axis=0)
    every = lax.all_to_all(
        jnp.broadcast_to(plane[None], (8, 16, SLICE)), ("zh", "x"), 0, 0, tiled=True
    )
    every = (every[:4] + every[4:]) * factor
    return jnp.swapaxes(every, 0, 1).reshape(16, D)


def on_device(query_rows, key_rows, value_rows, upstream, input_weights, output_weight):
    factor = 1.0 / (8 * math.sqrt(16384))
    place = jnp.stack([lax.axis_index("x"), lax.axis_index("zl"), lax.axis_index("c")]).astype(
        jnp.int32
    )
    pieces = gather_weights(input_weights, output_weight)
    sent = jnp.concatenate(
        [a.reshape(CLIP_LEN, PATCH_BLOCK, D) for a in (query_rows, key_rows, value_rows, upstream)],
        axis=2,
    )
    moved = lax.all_to_all(sent, CLIP_AXES, 0, 0, tiled=True).reshape(ROWS, 4 * D)
    grads, partial = attention_call(place, moved, pieces)
    result = projection_call(place, grads, pieces).reshape(CLIP_LEN, PATCH_BLOCK, D)
    input_gradient = lax.all_to_all(result, CLIP_AXES, 0, 0, tiled=True)
    weight_gradient = sum_weight_grad(partial, factor)
    return (input_gradient.reshape(query_rows.shape), weight_gradient)


def solution(mesh):
    axes = ("yh", "yl", "zl", "c", "zh", "x")
    fine = Mesh(mesh.devices.reshape(2, 4, 4, 2, 2, 4), axes)
    seq, dp = ("yh", "yl", "zl", "c"), ("zh", "x")
    rows = P(dp, seq, None, None)
    return jax.shard_map(
        on_device,
        mesh=fine,
        in_specs=(rows, rows, rows, rows, P(seq, None), P(seq, None)),
        out_specs=(rows, P(seq, None)),
        check_vma=False,
    )
```

time: 797 us -> 248 us (0.31)
  waiting for transfers between devices: 594 us -> 81.7 us
  starting transfers between devices: 43.2 us -> 107 us
  matrix products: 36.8 us -> 0 us
  local copies, waits for them, and re-layouts: 36.3 us -> 9.59 us
  blocking collectives: 47.8 us -> 21.6 us
  Pallas kernels: 0 us -> 21.5 us
  between operations: 14.4 us -> 0.96 us
  other arithmetic: 16.3 us -> 5.04 us
    reduce_scatter x1 -> x0, waiting for transfers between devices: 280 us -> none  [on_device(): lax.psum_scatter(lax.dot_general(context_flat, grad_flat, (((0,), (0,)),...]
    all_gather x2 -> x0, waiting for transfers between devices: 241 us -> none  [the longest x1 122 us: on_device(): lax.all_gather(output_weight, 'seq', axis=0, tiled=True)]
    ppermute x0 -> x15, starting transfers between devices: none -> 74.2 us  [the longest x2 27.6 us: spread(): far_b = lax.ppermute(after[half:], axes, perms(-1))]
    ppermute x0 -> x15, waiting for transfers between devices: none -> 59.7 us  [the longest x2 20.7 us: spread(): after = lax.ppermute(block, axes, perms(-1))]
    all_to_all x6 -> x4, waiting for transfers between devices: 72.1 us -> 22 us  [the longest x1 15.6 us: on_device(): input_gradient = lax.all_to_all(result, CLIP_AXES, 0, 0, tiled=True)]
    dot_general x10 -> x0, matrix products: 32.4 us -> none  [the longest x1 6.06 us: attention_grads(): jnp.einsum('cphts,ctphe->csphe', score_grad, query_heads, preferred_eleme...]
    all_to_all x2, blocking collectives: 47.8 us -> 21.6 us  [the longest x1 16.2 us: sum_weight_grad(): plane = lax.all_to_all(row, ('yh', 'yl', 'zl'), 0, 0, tiled=True)]
    pallas_call x0 -> x2, Pallas kernels: none -> 21.5 us  [the longest x1 13.1 us: attention_call(): pl.pallas_call(attention_kernel, grid_spec=grid_spec, out_shape=[jax.Shap...]
  transfers between devices with their start and end apart: 10 -> 19, of which waited for: 9 -> 9; matrix products, arithmetic and copies ran while one was open for 8% -> 2% of each run, Pallas kernels for 0% -> 3%
where the time goes in v1:
time: 248 us; the launch traced here: 247 us
  starting transfers between devices  107 us (43%)
  waiting for transfers between devices  81.7 us (33%)
  blocking collectives  21.6 us (9%)
  Pallas kernels  21.5 us (9%)
  local copies, waits for them, and re-layouts  9.59 us (4%)
  other arithmetic  5.04 us (2%)
    ppermute x2, starting transfers between devices, spread(): far_b = lax.ppermute(after[half:], axes, perms(-1))  27.6 us
    ppermute x2, waiting for transfers between devices, spread(): after = lax.ppermute(block, axes, perms(-1))  20.7 us
    ppermute x2, waiting for transfers between devices, spread(): before = lax.ppermute(block, axes, perms(1))  19.5 us
    all_to_all x1, blocking collectives, sum_weight_grad(): plane = lax.all_to_all(row, ('yh', 'yl', 'zl'), 0, 0, tiled=True)  16.2 us
    all_to_all x1, waiting for transfers between devices, on_device(): input_gradient = lax.all_to_all(result, CLIP_AXES, 0, 0, tiled=True)  15.6 us
    ppermute x4, starting transfers between devices, gather_weights(): return own + [lax.ppermute(piece, 'c', ring(2, 1)) for piece in own]  13.1 us
    pallas_call x1, Pallas kernels, attention_call(): pl.pallas_call(attention_kernel, grid_spec=grid_spec, out_shape=[jax.Shap...  13.1 us
    ppermute x2, starting transfers between devices, spread(): after = lax.ppermute(block, axes, perms(-1))  11.5 us
  transfers between devices with their start and end apart: 19, of which 9 were waited for; matrix products, arithmetic and copies ran while one was open for 2% of the time, Pallas kernels for 3%

profile of v1, /device:TPU:1, one launch (start us, length us, event | category | flops | bytes accessed | tf_op | source)
XLA Modules:
  0.0 246.9 jit_solution(2972987499800949406)
XLA Ops:
  0.6 0.0 copy-start
  0.7 0.7 constant_dynamic-slice_fusion
  1.4 0.1 copy-done
  1.5 0.7 broadcast_in_dim.4
  2.3 7.7 %all-to-all-start.1 = ((bf16[8,16,1024]{2,1,0:T(8,128)(2,1)}), bf16[8,16,1024]{2,1,0:T(8,128)(2,1)S(1)}, u32[]{:S(2)}, u32[]{:S(2)}) async-start(bf16[8,16,1024]{2,1,0:T(8,128)(2,1)} %broadcast_in_dim.4), calls=%async_computation.1 | async-start | bytes 524288 | tf_op jit(solution)/shard_map/all_to_all | solution.py:192
  9.9 3.0 %pad_maximum_fusion = bf16[32,8,4096]{2,1,0:T(8,128)(2,1)} fusion(bf16[32,8,1024]{2,1,0:T(8,128)(2,1)} %bitcast.35, bf16[32,8,1024]{2,1,0:T(8,128)(2,1)} %bitcast.36, bf16[32,8,1024]{2,1,0:T(8,128)(2,1)} %bitcast.37, bf16[32,8,1024]{2,1,0:T(8,128)(2,1)} %bitcast.38), kind=kLoop, calls=%fused_computation | loop fusion | flops 8388608 | bytes 4194304 | tf_op jit(solution)/shard_map/concatenate | solution.py:227
  12.9 6.4 %all-to-all-done.1 = bf16[8,16,1024]{2,1,0:T(8,128)(2,1)S(1)} async-done(((bf16[8,16,1024]{2,1,0:T(8,128)(2,1)}), bf16[8,16,1024]{2,1,0:T(8,128)(2,1)S(1)}, u32[]{:S(2)}, u32[]{:S(2)}) %all-to-all-start.1) | async-done | bytes 262176 | tf_op jit(solution)/shard_map/all_to_all | solution.py:192
  19.3 10.9 %all-to-all-start = ((bf16[32,8,4096]{2,1,0:T(8,128)(2,1)}), bf16[32,8,4096]{2,1,0:T(8,128)(2,1)}, u32[]{:S(2)}, u32[]{:S(2)}) async-start(bf16[32,8,4096]{2,1,0:T(8,128)(2,1)} %pad_maximum_fusion), calls=%async_computation | async-start | bytes 4194304 | tf_op jit(solution)/shard_map/all_to_all | solution.py:231
  30.2 8.1 %collective-permute-start = (bf16[8,16,1024]{2,1,0:T(8,128)(2,1)S(1)}, bf16[8,16,1024]{2,1,0:T(8,128)(2,1)S(1)}, u32[]{:S(2)}, u32[]{:S(2)}) collective-permute-start(bf16[8,16,1024]{2,1,0:T(8,128)(2,1)S(1)} %all-to-all-done.1), channel_id=1, source_target_pairs={{0,52},{16,0},{32,16},{48,32},{4,48},{20,4},{36,20},{52,36},{1,53}... | collective-permute-start | bytes 786440 | tf_op jit(solution)/shard_map/ppermute | solution.py:176
  38.4 1.9 collective-permute-start.1
  40.3 20.6 %collective-permute-done = bf16[8,16,1024]{2,1,0:T(8,128)(2,1)S(1)} collective-permute-done((bf16[8,16,1024]{2,1,0:T(8,128)(2,1)S(1)}, bf16[8,16,1024]{2,1,0:T(8,128)(2,1)S(1)}, u32[]{:S(2)}, u32[]{:S(2)}) %collective-permute-start) | collective-permute-done | bytes 262176 | tf_op jit(solution)/shard_map/ppermute | solution.py:176
  61.0 23.0 %collective-permute-start.3 = (bf16[4,16,1024]{2,1,0:T(8,128)(2,1)S(1)}, bf16[4,16,1024]{2,1,0:T(8,128)(2,1)S(1)}, u32[]{:S(2)}, u32[]{:S(2)}) collective-permute-start(bf16[4,16,1024]{2,1,0:T(8,128)(2,1)S(1)} %slice.33), channel_id=1, source_target_pairs={{0,52},{16,0},{32,16},{48,32},{4,48},{20,4},{36,20},{52,36},{1,53}... | collective-permute-start | bytes 393224 | tf_op jit(solution)/shard_map/ppermute | solution.py:179
  84.0 0.0 collective-permute-done.1
  84.0 4.8 %collective-permute-start.2 = (bf16[4,16,1024]{2,1,0:T(8,128)(2,1)S(1)}, bf16[4,16,1024]{2,1,0:T(8,128)(2,1)S(1)}, u32[]{:S(2)}, u32[]{:S(2)}) collective-permute-start(bf16[4,16,1024]{2,1,0:T(8,128)(2,1)S(1)} %slice.32), channel_id=1, source_target_pairs={{0,16},{16,32},{32,48},{48,4},{4,20},{20,36},{36,52},{52,0},{1,17}... | collective-permute-start | bytes 393224 | tf_op jit(solution)/shard_map/ppermute | solution.py:178
  88.8 1.0 collective-permute-done.3
  89.8 4.8 %collective-permute-done.2 = bf16[4,16,1024]{2,1,0:T(8,128)(2,1)S(1)} collective-permute-done((bf16[4,16,1024]{2,1,0:T(8,128)(2,1)S(1)}, bf16[4,16,1024]{2,1,0:T(8,128)(2,1)S(1)}, u32[]{:S(2)}, u32[]{:S(2)}) %collective-permute-start.2) | collective-permute-done | bytes 131104 | tf_op jit(solution)/shard_map/ppermute | solution.py:178
  94.7 0.1 pad_maximum_fusion.1.refs_0_
  94.8 3.1 %collective-permute-start.5 = (bf16[4,8,16,1024]{3,2,1,0:T(8,128)(2,1)S(1)}, bf16[4,8,16,1024]{3,2,1,0:T(8,128)(2,1)S(1)}, u32[]{:S(2)}, u32[]{:S(2)}) collective-permute-start(bf16[4,8,16,1024]{3,2,1,0:T(8,128)(2,1)S(1)} %pad_maximum_fusion.1.refs_0_), channel_id=1, source_target_pairs={{0,1},{1,2},{2,3},{3,0},{4,5},{5,6},{6,7},{7,4},{8,9},{9,10},{10,1... | collective-permute-start | bytes 3145736 | tf_op jit(solution)/shard_map/ppermute | solution.py:177
  97.9 3.4 %collective-permute-start.4 = (bf16[4,8,16,1024]{3,2,1,0:T(8,128)(2,1)S(1)}, bf16[4,8,16,1024]{3,2,1,0:T(8,128)(2,1)S(1)}, u32[]{:S(2)}, u32[]{:S(2)}) collective-permute-start(bf16[4,8,16,1024]{3,2,1,0:T(8,128)(2,1)S(1)} %pad_maximum_fusion.1.refs_0_), channel_id=1, source_target_pairs={{0,3},{1,0},{2,1},{3,2},{4,7},{5,4},{6,5},{7,6},{8,11},{9,8},{10,9... | collective-permute-start | bytes 3145736 | tf_op jit(solution)/shard_map/ppermute | solution.py:176
  101.3 19.5 %collective-permute-done.5.refs_3_ = bf16[4,8,16,1024]{3,2,1,0:T(8,128)(2,1)S(1)} collective-permute-done((bf16[4,8,16,1024]{3,2,1,0:T(8,128)(2,1)S(1)}, bf16[4,8,16,1024]{3,2,1,0:T(8,128)(2,1)S(1)}, u32[]{:S(2)}, u32[]{:S(2)}) %collective-permute-start.5) | collective-permute-done | bytes 1048608 | tf_op jit(solution)/shard_map/ppermute | solution.py:177
  120.8 1.9 collective-permute-start.6
  122.8 0.0 collective-permute-done.4.refs_1_
  122.8 4.6 %collective-permute-start.7 = (bf16[2,8,16,1024]{3,2,1,0:T(8,128)(2,1)S(1)}, bf16[2,8,16,1024]{3,2,1,0:T(8,128)(2,1)S(1)}, u32[]{:S(2)}, u32[]{:S(2)}) collective-permute-start(bf16[2,8,16,1024]{3,2,1,0:T(8,128)(2,1)S(1)} %slice.35), channel_id=1, source_target_pairs={{0,3},{1,0},{2,1},{3,2},{4,7},{5,4},{6,5},{7,6},{8,11},{9,8},{10,9... | collective-permute-start | bytes 1572872 | tf_op jit(solution)/shard_map/ppermute | solution.py:179
  127.4 5.2 %collective-permute-start.8 = (bf16[4,8,16,1024]{3,2,1,0:T(8,128)(2,1)S(1)}, bf16[4,8,16,1024]{3,2,1,0:T(8,128)(2,1)}, u32[]{:S(2)}, u32[]{:S(2)}) collective-permute-start(bf16[4,8,16,1024]{3,2,1,0:T(8,128)(2,1)S(1)} %pad_maximum_fusion.1.refs_0_), channel_id=1, source_target_pairs={{0,8},{8,0},{1,9},{9,1},{2,10},{10,2},{3,11},{11,3},{4,12},{12,4},... | collective-permute-start | bytes 3145736 | tf_op jit(solution)/shard_map/ppermute | solution.py:197
  132.6 1.9 collective-permute-start.9
  134.5 2.4 collective-permute-start.11
  136.9 0.0 collective-permute-done.6
  136.9 0.9 constant_dynamic-update-slice_fusion.1
  137.8 0.0 collective-permute-done.7
  137.8 0.8 constant_dynamic-update-slice_fusion.refs_2_
  138.7 3.6 %collective-permute-start.10 = (bf16[4,8,16,1024]{3,2,1,0:T(8,128)(2,1)}, bf16[4,8,16,1024]{3,2,1,0:T(8,128)(2,1)}, u32[]{:S(2)}, u32[]{:S(2)}) collective-permute-start(bf16[4,8,16,1024]{3,2,1,0:T(8,128)(2,1)} %constant_dynamic-update-slice_fusion.refs_2_), channel_id=1, source_target_pairs={{0,8},{8,0},{1,9},{9,1},{2,10},{10,2},{3,11},{11,3},{4,12},{12,4},... | collective-permute-start | bytes 3145736 | tf_op jit(solution)/shard_map/ppermute | solution.py:197
  142.3 0.1 pad_add_fusion.place
  142.4 0.0 collective-permute-done.8.refs_4_
  142.4 0.0 collective-permute-done.9.refs_5_
  142.4 0.0 collective-permute-done.11.refs_7_
  142.4 2.5 %collective-permute-done.10.refs_6_ = bf16[4,8,16,1024]{3,2,1,0:T(8,128)(2,1)} collective-permute-done((bf16[4,8,16,1024]{3,2,1,0:T(8,128)(2,1)}, bf16[4,8,16,1024]{3,2,1,0:T(8,128)(2,1)}, u32[]{:S(2)}, u32[]{:S(2)}) %collective-permute-start.10) | collective-permute-done | bytes 1048608 | tf_op jit(solution)/shard_map/ppermute | solution.py:197
  144.9 0.0 all-to-all-done
  144.9 13.1 %attention_grads.1 = (bf16[256,3072]{1,0:T(8,128)(2,1)S(1)}, bf16[2,4,8,64,256]{4,3,2,1,0:T(8,128)(2,1)S(1)}) custom-call(s32[3]{0:T(128)S(1)} %pad_add_fusion.place, bf16[256,4096]{1,0:T(8,128)(2,1)} %bitcast.7.q_ref.k_ref.v_ref.u_ref, bf16[256,4096]{1,0:T(8,128)(2,1)} %bitcast.7.q_ref.k_ref.v_ref.u_ref, bf16[256,4096]{1,0:T(8,128)(2,1)} %bitcast.7.q_ref.k_ref.v_ref.u_ref, ...), custom_call_target="tpu_custom_call" | custom-call | flops 5000000000 | bytes 8388608 | tf_op jit(solution)/shard_map/attention_grads/pallas_call | solution.py:128
  157.9 0.0 copy-start.2
  157.9 5.4 %all_to_all.30 = bf16[2,4,8,64,256]{4,3,2,1,0:T(8,128)(2,1)S(1)} all-to-all(bf16[2,4,8,64,256]{4,3,2,1,0:T(8,128)(2,1)S(1)} %get-tuple-element.5), channel_id=1, replica_groups=mesh['yh'=2,'yl'=4,'zl'=4,'c'=2,'zh'=2,'x'=4] {'c'}, dimensions={0} | all-to-all | bytes 4194304 | tf_op jit(solution)/shard_map/all_to_all | solution.py:202
  163.4 0.0 copy-done.2
  163.4 0.4 add_convert_fusion
  163.8 0.0 copy-start.4
  163.8 1.0 copy-done.4
  164.8 0.9 dynamic-slice_bitcast_fusion.2
  165.6 5.3 %collective-permute-start.14 = (bf16[8,64,256]{2,1,0:T(8,128)(2,1)}, bf16[8,64,256]{2,1,0:T(8,128)(2,1)}, u32[]{:S(2)}, u32[]{:S(2)}) collective-permute-start(bf16[8,64,256]{2,1,0:T(8,128)(2,1)} %get-tuple-element.7), channel_id=1, source_target_pairs={{0,3},{1,0},{2,1},{3,2},{4,7},{5,4},{6,5},{7,6},{8,11},{9,8},{10,9... | collective-permute-start | bytes 786440 | tf_op jit(solution)/shard_map/ppermute | solution.py:210
  170.9 1.9 collective-permute-start.13
  172.9 3.1 %collective-permute-start.12 = (bf16[8,64,256]{2,1,0:T(8,128)(2,1)S(1)}, bf16[8,64,256]{2,1,0:T(8,128)(2,1)}, u32[]{:S(2)}, u32[]{:S(2)}) collective-permute-start(bf16[8,64,256]{2,1,0:T(8,128)(2,1)S(1)} %get-tuple-element.6), channel_id=1, source_target_pairs={{0,2},{1,3},{2,0},{3,1},{4,6},{5,7},{6,4},{7,5},{8,10},{9,11},{10,... | collective-permute-start | bytes 786440 | tf_op jit(solution)/shard_map/ppermute | solution.py:210
  176.0 0.6 collective-permute-done.14
  176.6 10.6 %collective-permute-done.13 = bf16[8,64,256]{2,1,0:T(8,128)(2,1)} collective-permute-done((bf16[8,64,256]{2,1,0:T(8,128)(2,1)}, bf16[8,64,256]{2,1,0:T(8,128)(2,1)}, u32[]{:S(2)}, u32[]{:S(2)}) %collective-permute-start.13) | collective-permute-done | bytes 262176 | tf_op jit(solution)/shard_map/ppermute | solution.py:210
  187.2 0.0 collective-permute-done.12
  187.2 1.3 fusion.2
  188.5 16.2 %all_to_all.31 = bf16[32,16,256]{2,1,0:T(8,128)(2,1)S(1)} all-to-all(bf16[32,16,256]{2,1,0:T(8,128)(2,1)S(1)} %bitcast.31), channel_id=1, replica_groups=mesh['yh'=2,'yl'=4,'zl'=4,'c'=2,'zh'=2,'x'=4] {'yh','yl','zl'}, dimensions={0} | all-to-all | bytes 524288 | tf_op jit(solution)/shard_map/all_to_all | solution.py:212
  204.7 0.7 broadcast_in_dim.5
  205.4 6.6 %all-to-all-start.5 = ((f32[8,16,256]{2,1,0:T(8,128)}), f32[8,16,256]{2,1,0:T(8,128)S(1)}, u32[]{:S(2)}, u32[]{:S(2)}) async-start(f32[8,16,256]{2,1,0:T(8,128)} %broadcast_in_dim.5), calls=%async_computation.5 | async-start | bytes 262144 | tf_op jit(solution)/shard_map/all_to_all | solution.py:214
  212.0 1.4 copy-done.3
  213.4 8.5 %input_projection.1 = bf16[256,1024]{1,0:T(8,128)(2,1)S(1)} custom-call(s32[3]{0:T(128)S(1)} %pad_add_fusion.place, bf16[256,3072]{1,0:T(8,128)(2,1)S(1)} %copy-done.3, bf16[4,8,16,1024]{3,2,1,0:T(8,128)(2,1)S(1)} %pad_maximum_fusion.1.refs_0_, bf16[4,8,16,1024]{3,2,1,0:T(8,128)(2,1)S(1)} %collective-permute-done.4.refs_1_, ...), custom_call_target="tpu_custom_call" | custom-call | flops 2000000000 | bytes 8388608 | tf_op jit(solution)/shard_map/input_projection/pallas_call | solution.py:162
  221.9 0.0 copy-start.1
  222.0 0.8 copy-done.1
  222.7 0.0 all-to-all-done.5
  222.7 7.1 %all-to-all-start.2 = ((bf16[32,8,1024]{2,1,0:T(8,128)(2,1)}), bf16[32,8,1024]{2,1,0:T(8,128)(2,1)S(1)}, u32[]{:S(2)}, u32[]{:S(2)}) async-start(bf16[32,8,1024]{2,1,0:T(8,128)(2,1)} %bitcast.29), calls=%async_computation.2 | async-start | bytes 1048576 | tf_op jit(solution)/shard_map/all_to_all | solution.py:234
  229.9 0.6 copy.9
  230.5 15.6 %all-to-all-done.2 = bf16[32,8,1024]{2,1,0:T(8,128)(2,1)S(1)} async-done(((bf16[32,8,1024]{2,1,0:T(8,128)(2,1)}), bf16[32,8,1024]{2,1,0:T(8,128)(2,1)S(1)}, u32[]{:S(2)}, u32[]{:S(2)}) %all-to-all-start.2) | async-done | bytes 524320 | tf_op jit(solution)/shard_map/all_to_all | solution.py:234
  246.1 0.8 copy.12
  (10 shorter events, 0.2 us)
Async XLA Ops:
  0.6 0.9 copy-start
  2.3 17.1 %all-to-all-start.1 = ((bf16[8,16,1024]{2,1,0:T(8,128)(2,1)}), bf16[8,16,1024]{2,1,0:T(8,128)(2,1)S(1)}, u32[]{:S(2)}, u32[]{:S(2)}) async-start(bf16[8,16,1024]{2,1,0:T(8,128)(2,1)} %broadcast_in_dim.4), calls=%async_computation.1 | async-start | bytes 524288 | tf_op jit(solution)/shard_map/all_to_all | solution.py:192
  19.3 125.5 %all-to-all-start = ((bf16[32,8,4096]{2,1,0:T(8,128)(2,1)}), bf16[32,8,4096]{2,1,0:T(8,128)(2,1)}, u32[]{:S(2)}, u32[]{:S(2)}) async-start(bf16[32,8,4096]{2,1,0:T(8,128)(2,1)} %pad_maximum_fusion), calls=%async_computation | async-start | bytes 4194304 | tf_op jit(solution)/shard_map/all_to_all | solution.py:231
  30.2 30.7 %collective-permute-start = (bf16[8,16,1024]{2,1,0:T(8,128)(2,1)S(1)}, bf16[8,16,1024]{2,1,0:T(8,128)(2,1)S(1)}, u32[]{:S(2)}, u32[]{:S(2)}) collective-permute-start(bf16[8,16,1024]{2,1,0:T(8,128)(2,1)S(1)} %all-to-all-done.1), channel_id=1, source_target_pairs={{0,52},{16,0},{32,16},{48,32},{4,48},{20,4},{36,20},{52,36},{1,53}... | collective-permute-start | bytes 786440 | tf_op jit(solution)/shard_map/ppermute | solution.py:176
  38.4 45.6 %collective-permute-start.1 = (bf16[8,16,1024]{2,1,0:T(8,128)(2,1)S(1)}, bf16[8,16,1024]{2,1,0:T(8,128)(2,1)S(1)}, u32[]{:S(2)}, u32[]{:S(2)}) collective-permute-start(bf16[8,16,1024]{2,1,0:T(8,128)(2,1)S(1)} %all-to-all-done.1), channel_id=1, source_target_pairs={{0,16},{16,32},{32,48},{48,4},{4,20},{20,36},{36,52},{52,0},{1,17}... | collective-permute-start | bytes 786440 | tf_op jit(solution)/shard_map/ppermute | solution.py:177
  61.0 28.8 %collective-permute-start.3 = (bf16[4,16,1024]{2,1,0:T(8,128)(2,1)S(1)}, bf16[4,16,1024]{2,1,0:T(8,128)(2,1)S(1)}, u32[]{:S(2)}, u32[]{:S(2)}) collective-permute-start(bf16[4,16,1024]{2,1,0:T(8,128)(2,1)S(1)} %slice.33), channel_id=1, source_target_pairs={{0,52},{16,0},{32,16},{48,32},{4,48},{20,4},{36,20},{52,36},{1,53}... | collective-permute-start | bytes 393224 | tf_op jit(solution)/shard_map/ppermute | solution.py:179
  84.0 10.6 %collective-permute-start.2 = (bf16[4,16,1024]{2,1,0:T(8,128)(2,1)S(1)}, bf16[4,16,1024]{2,1,0:T(8,128)(2,1)S(1)}, u32[]{:S(2)}, u32[]{:S(2)}) collective-permute-start(bf16[4,16,1024]{2,1,0:T(8,128)(2,1)S(1)} %slice.32), channel_id=1, source_target_pairs={{0,16},{16,32},{32,48},{48,4},{4,20},{20,36},{36,52},{52,0},{1,17}... | collective-permute-start | bytes 393224 | tf_op jit(solution)/shard_map/ppermute | solution.py:178
  94.8 26.0 %collective-permute-start.5 = (bf16[4,8,16,1024]{3,2,1,0:T(8,128)(2,1)S(1)}, bf16[4,8,16,1024]{3,2,1,0:T(8,128)(2,1)S(1)}, u32[]{:S(2)}, u32[]{:S(2)}) collective-permute-start(bf16[4,8,16,1024]{3,2,1,0:T(8,128)(2,1)S(1)} %pad_maximum_fusion.1.refs_0_), channel_id=1, source_target_pairs={{0,1},{1,2},{2,3},{3,0},{4,5},{5,6},{6,7},{7,4},{8,9},{9,10},{10,1... | collective-permute-start | bytes 3145736 | tf_op jit(solution)/shard_map/ppermute | solution.py:177
  97.9 24.8 %collective-permute-start.4 = (bf16[4,8,16,1024]{3,2,1,0:T(8,128)(2,1)S(1)}, bf16[4,8,16,1024]{3,2,1,0:T(8,128)(2,1)S(1)}, u32[]{:S(2)}, u32[]{:S(2)}) collective-permute-start(bf16[4,8,16,1024]{3,2,1,0:T(8,128)(2,1)S(1)} %pad_maximum_fusion.1.refs_0_), channel_id=1, source_target_pairs={{0,3},{1,0},{2,1},{3,2},{4,7},{5,4},{6,5},{7,6},{8,11},{9,8},{10,9... | collective-permute-start | bytes 3145736 | tf_op jit(solution)/shard_map/ppermute | solution.py:176
  120.8 16.1 %collective-permute-start.6 = (bf16[2,8,16,1024]{3,2,1,0:T(8,128)(2,1)S(1)}, bf16[2,8,16,1024]{3,2,1,0:T(8,128)(2,1)S(1)}, u32[]{:S(2)}, u32[]{:S(2)}) collective-permute-start(bf16[2,8,16,1024]{3,2,1,0:T(8,128)(2,1)S(1)} %slice.34), channel_id=1, source_target_pairs={{0,1},{1,2},{2,3},{3,0},{4,5},{5,6},{6,7},{7,4},{8,9},{9,10},{10,1... | collective-permute-start | bytes 1572872 | tf_op jit(solution)/shard_map/ppermute | solution.py:178
  122.8 15.0 %collective-permute-start.7 = (bf16[2,8,16,1024]{3,2,1,0:T(8,128)(2,1)S(1)}, bf16[2,8,16,1024]{3,2,1,0:T(8,128)(2,1)S(1)}, u32[]{:S(2)}, u32[]{:S(2)}) collective-permute-start(bf16[2,8,16,1024]{3,2,1,0:T(8,128)(2,1)S(1)} %slice.35), channel_id=1, source_target_pairs={{0,3},{1,0},{2,1},{3,2},{4,7},{5,4},{6,5},{7,6},{8,11},{9,8},{10,9... | collective-permute-start | bytes 1572872 | tf_op jit(solution)/shard_map/ppermute | solution.py:179
  127.4 15.0 %collective-permute-start.8 = (bf16[4,8,16,1024]{3,2,1,0:T(8,128)(2,1)S(1)}, bf16[4,8,16,1024]{3,2,1,0:T(8,128)(2,1)}, u32[]{:S(2)}, u32[]{:S(2)}) collective-permute-start(bf16[4,8,16,1024]{3,2,1,0:T(8,128)(2,1)S(1)} %pad_maximum_fusion.1.refs_0_), channel_id=1, source_target_pairs={{0,8},{8,0},{1,9},{9,1},{2,10},{10,2},{3,11},{11,3},{4,12},{12,4},... | collective-permute-start | bytes 3145736 | tf_op jit(solution)/shard_map/ppermute | solution.py:197
  132.6 9.8 %collective-permute-start.9 = (bf16[4,8,16,1024]{3,2,1,0:T(8,128)(2,1)S(1)}, bf16[4,8,16,1024]{3,2,1,0:T(8,128)(2,1)}, u32[]{:S(2)}, u32[]{:S(2)}) collective-permute-start(bf16[4,8,16,1024]{3,2,1,0:T(8,128)(2,1)S(1)} %collective-permute-done.4.refs_1_), channel_id=1, source_target_pairs={{0,8},{8,0},{1,9},{9,1},{2,10},{10,2},{3,11},{11,3},{4,12},{12,4},... | collective-permute-start | bytes 3145736 | tf_op jit(solution)/shard_map/ppermute | solution.py:197
  134.5 7.9 %collective-permute-start.11 = (bf16[4,8,16,1024]{3,2,1,0:T(8,128)(2,1)S(1)}, bf16[4,8,16,1024]{3,2,1,0:T(8,128)(2,1)}, u32[]{:S(2)}, u32[]{:S(2)}) collective-permute-start(bf16[4,8,16,1024]{3,2,1,0:T(8,128)(2,1)S(1)} %collective-permute-done.5.refs_3_), channel_id=1, source_target_pairs={{0,8},{8,0},{1,9},{9,1},{2,10},{10,2},{3,11},{11,3},{4,12},{12,4},... | collective-permute-start | bytes 3145736 | tf_op jit(solution)/shard_map/ppermute | solution.py:197
  138.7 6.2 %collective-permute-start.10 = (bf16[4,8,16,1024]{3,2,1,0:T(8,128)(2,1)}, bf16[4,8,16,1024]{3,2,1,0:T(8,128)(2,1)}, u32[]{:S(2)}, u32[]{:S(2)}) collective-permute-start(bf16[4,8,16,1024]{3,2,1,0:T(8,128)(2,1)} %constant_dynamic-update-slice_fusion.refs_2_), channel_id=1, source_target_pairs={{0,8},{8,0},{1,9},{9,1},{2,10},{10,2},{3,11},{11,3},{4,12},{12,4},... | collective-permute-start | bytes 3145736 | tf_op jit(solution)/shard_map/ppermute | solution.py:197
  157.9 5.4 %copy-start.2 = (bf16[256,3072]{1,0:T(8,128)(2,1)}, bf16[256,3072]{1,0:T(8,128)(2,1)S(1)}, u32[]{:S(2)}) copy-start(bf16[256,3072]{1,0:T(8,128)(2,1)S(1)} %get-tuple-element.4.g_ref) | copy-start | bytes 4718596
  163.8 1.0 copy-start.4
  165.6 10.9 %collective-permute-start.14 = (bf16[8,64,256]{2,1,0:T(8,128)(2,1)}, bf16[8,64,256]{2,1,0:T(8,128)(2,1)}, u32[]{:S(2)}, u32[]{:S(2)}) collective-permute-start(bf16[8,64,256]{2,1,0:T(8,128)(2,1)} %get-tuple-element.7), channel_id=1, source_target_pairs={{0,3},{1,0},{2,1},{3,2},{4,7},{5,4},{6,5},{7,6},{8,11},{9,8},{10,9... | collective-permute-start | bytes 786440 | tf_op jit(solution)/shard_map/ppermute | solution.py:210
  170.9 16.2 %collective-permute-start.13 = (bf16[8,64,256]{2,1,0:T(8,128)(2,1)}, bf16[8,64,256]{2,1,0:T(8,128)(2,1)}, u32[]{:S(2)}, u32[]{:S(2)}) collective-permute-start(bf16[8,64,256]{2,1,0:T(8,128)(2,1)} %get-tuple-element.8), channel_id=1, source_target_pairs={{0,1},{1,2},{2,3},{3,0},{4,5},{5,6},{6,7},{7,4},{8,9},{9,10},{10,1... | collective-permute-start | bytes 786440 | tf_op jit(solution)/shard_map/ppermute | solution.py:210
  172.9 14.3 %collective-permute-start.12 = (bf16[8,64,256]{2,1,0:T(8,128)(2,1)S(1)}, bf16[8,64,256]{2,1,0:T(8,128)(2,1)}, u32[]{:S(2)}, u32[]{:S(2)}) collective-permute-start(bf16[8,64,256]{2,1,0:T(8,128)(2,1)S(1)} %get-tuple-element.6), channel_id=1, source_target_pairs={{0,2},{1,3},{2,0},{3,1},{4,6},{5,7},{6,4},{7,5},{8,10},{9,11},{10,... | collective-permute-start | bytes 786440 | tf_op jit(solution)/shard_map/ppermute | solution.py:210
  205.4 17.3 %all-to-all-start.5 = ((f32[8,16,256]{2,1,0:T(8,128)}), f32[8,16,256]{2,1,0:T(8,128)S(1)}, u32[]{:S(2)}, u32[]{:S(2)}) async-start(f32[8,16,256]{2,1,0:T(8,128)} %broadcast_in_dim.5), calls=%async_computation.5 | async-start | bytes 262144 | tf_op jit(solution)/shard_map/all_to_all | solution.py:214
  212.0 1.4 copy-start.3
  221.9 0.8 copy-start.1
  222.7 23.4 %all-to-all-start.2 = ((bf16[32,8,1024]{2,1,0:T(8,128)(2,1)}), bf16[32,8,1024]{2,1,0:T(8,128)(2,1)S(1)}, u32[]{:S(2)}, u32[]{:S(2)}) async-start(bf16[32,8,1024]{2,1,0:T(8,128)(2,1)} %bitcast.29), calls=%async_computation.2 | async-start | bytes 1048576 | tf_op jit(solution)/shard_map/all_to_all | solution.py:234

commit v2 on v1

v2 whole, which is shorter than its diff:
```python
import math

import jax
import jax.numpy as jnp
from jax import lax
from jax.experimental import pallas as pl
from jax.experimental.pallas import tpu as pltpu
from jax.sharding import Mesh
from jax.sharding import PartitionSpec as P

D = 1024
HEAD_DIM = 64
CLIP_LEN = 32
PATCH_BLOCK = 8
ROWS = CLIP_LEN * PATCH_BLOCK
SLICE = 256
CLIP_AXES = ("yl", "zl", "c")
PLANE_AXES = ("yh", "yl", "zl")
NEG = -1e30
NN = ((1,), (0,))
NT = ((1,), (1,))


def ring(size, shift):
    return [(i, (i + shift) % size) for i in range(size)]


def dot(a, b, contract):
    return lax.dot_general(a, b, (contract, ((), ())), preferred_element_type=jnp.float32)

def weight_rows(own, sibling, core, columns):
    first = core == 0
    parts = []
    for at in range(8):
        mine, other = own[at, :, columns], sibling[at, :, columns]
        parts.append(jnp.where(first, mine, other))
        parts.append(jnp.where(first, other, mine))
    return jnp.concatenate(parts, axis=0)


def head_only(block, head):
    lane = lax.broadcasted_iota(jnp.int32, block.shape, 1)
    keep = (lane >= head * HEAD_DIM) & (lane < (head + 1) * HEAD_DIM)
    return jnp.where(keep, block, jnp.zeros((), block.dtype))


def forward_kernel(place, q_ref, k_ref, v_ref, u_ref, attention_ref, keep_ref, send_ref, bias):
    core = place[1]

    @pl.when(pl.program_id(0) == 0)
    def _():
        row = lax.broadcasted_iota(jnp.int32, (ROWS, ROWS), 0)
        col = lax.broadcasted_iota(jnp.int32, (ROWS, ROWS), 1)
        bias[...] = jnp.where(lax.rem(row - col + ROWS, PATCH_BLOCK) == 0, 0.0, NEG)

    q, k = q_ref[...], k_ref[...]
    v_t = v_ref[...].T
    context_t = []
    for head in range(4):
        scores = dot(q, head_only(k, head), NT) + bias[...]
        top = jnp.max(scores, axis=1, keepdims=True)
        e = jnp.exp2((scores - top) * (math.log2(math.e) / math.sqrt(HEAD_DIM)))
        attention = e * (1.0 / jnp.sum(e, axis=1, keepdims=True))
        attention_ref[head] = attention
        rows = v_t[head * HEAD_DIM : (head + 1) * HEAD_DIM]
        context_t.append(dot(rows, attention.astype(jnp.bfloat16), NT).astype(jnp.bfloat16))
    context_t = jnp.concatenate(context_t, axis=0)
    dw = dot(context_t, u_ref[...], NN).astype(jnp.bfloat16)
    dw = dw.reshape(8, 2, 16, D)
    halves = dw[:, 0].reshape(128, D), dw[:, 1].reshape(128, D)
    keep = jnp.where(core == 0, halves[0], halves[1])
    send = jnp.where(core == 0, halves[1], halves[0])
    for x in range(4):
        keep_ref[x] = keep[:, x * SLICE : (x + 1) * SLICE]
        send_ref[x] = send[:, x * SLICE : (x + 1) * SLICE]


def forward_call(place, moved):
    def column(base):
        return pl.BlockSpec((ROWS, SLICE), lambda i, s: (0, base + i))

    shares = pl.BlockSpec((4, 128, SLICE), lambda i, s: (0, i, 0))
    return pl.pallas_call(
        forward_kernel,
        grid_spec=pltpu.PrefetchScalarGridSpec(
            num_scalar_prefetch=1,
            grid=(4,),
            in_specs=[
                column(0),
                column(4),
                column(8),
                pl.BlockSpec((ROWS, D), lambda i, s: (0, 3)),
            ],
            out_specs=[pl.BlockSpec((4, ROWS, ROWS), lambda i, s: (i, 0, 0)), shares, shares],
            scratch_shapes=[pltpu.VMEM((ROWS, ROWS), jnp.float32)],
        ),
        out_shape=[
            pltpu.HBM((16, ROWS, ROWS), jnp.float32),
            jax.ShapeDtypeStruct((4, 512, SLICE), jnp.bfloat16),
            jax.ShapeDtypeStruct((4, 512, SLICE), jnp.bfloat16),
        ],
        compiler_params=pltpu.CompilerParams(vmem_limit_bytes=20 * 2**20),
        cost_estimate=pl.CostEstimate(
            flops=2 * 10**9, bytes_accessed=8 * 2**20, transcendentals=2**20
        ),
        name="attention_and_weight_grad",
    )(place, moved, moved, moved, moved)


def backward_kernel(place, attention_ref, q_ref, k_ref, v_ref, u_ref, *refs):
    pieces, g_ref = refs[:8], refs[8]
    x_at, core = place[0], place[1]
    cg = jnp.zeros((ROWS, SLICE), jnp.float32)
    for d in range(4):
        w = weight_rows(pieces[d], pieces[4 + d], core, slice(None))
        at = pl.multiple_of(lax.rem(x_at + d, 4) * SLICE, SLICE)
        cg = cg + dot(u_ref[:, pl.ds(at, SLICE)], w, NT)
    cg = cg.astype(jnp.bfloat16)
    v = v_ref[...]
    q_t, k_t, cg_t = q_ref[...].T, k_ref[...].T, cg.T
    for head in range(4):
        rows = slice(head * HEAD_DIM, (head + 1) * HEAD_DIM)
        attention = attention_ref[head]
        attention_b = attention.astype(jnp.bfloat16)
        grad_scores = dot(cg, head_only(v, head), NT)
        total = jnp.sum(attention * grad_scores, axis=1, keepdims=True)
        score_grad = attention * (grad_scores - total) * (1.0 / math.sqrt(HEAD_DIM))
        score_grad = score_grad.astype(jnp.bfloat16)
        g_ref[0, rows] = dot(k_t[rows], score_grad, NT).astype(jnp.bfloat16)
        g_ref[1, rows] = dot(q_t[rows], score_grad, NN).astype(jnp.bfloat16)
        g_ref[2, rows] = dot(cg_t[rows], attention_b, NN).astype(jnp.bfloat16)


def backward_call(place, attention, moved, pieces):
    def column(base):
        return pl.BlockSpec((ROWS, SLICE), lambda i, s: (0, base + i))

    return pl.pallas_call(
        backward_kernel,
        grid_spec=pltpu.PrefetchScalarGridSpec(
            num_scalar_prefetch=1,
            grid=(4,),
            in_specs=[
                pl.BlockSpec((4, ROWS, ROWS), lambda i, s: (i, 0, 0)),
                column(0),
                column(4),
                column(8),
                pl.BlockSpec((ROWS, D), lambda i, s: (0, 3)),
            ]
            + [pl.BlockSpec((8, 16, SLICE), lambda i, s: (i, 0, 3))] * 8,
            out_specs=pl.BlockSpec((3, SLICE, ROWS), lambda i, s: (0, i, 0)),
        ),
        out_shape=pltpu.HBM((3, D, ROWS), jnp.bfloat16),
        compiler_params=pltpu.CompilerParams(vmem_limit_bytes=20 * 2**20),
        cost_estimate=pl.CostEstimate(
            flops=3 * 10**9, bytes_accessed=10 * 2**20, transcendentals=0
        ),
        name="attention_grads",
    )(place, attention, moved, moved, moved, moved, *pieces)


def projection_kernel(place, g_ref, *refs):
    pieces, o_ref = refs[:8], refs[8]
    x_at, core = place[0], place[1]
    width = 3 * SLICE
    total = jnp.zeros((SLICE, ROWS), jnp.float32)
    for d in range(4):
        w = weight_rows(pieces[d], pieces[4 + d], core, slice(0, width))
        at = pl.multiple_of(lax.rem(x_at + d, 4) * width, width)
        total = total + dot(w, g_ref[pl.ds(at, width)], NN)
    o_ref[...] = total.astype(jnp.bfloat16).T


def projection_call(place, grads, pieces):
    return pl.pallas_call(
        projection_kernel,
        grid_spec=pltpu.PrefetchScalarGridSpec(
            num_scalar_prefetch=1,
            grid=(4,),
            in_specs=[pl.BlockSpec((3 * D, ROWS), lambda i, s: (0, 0))]
            + [pl.BlockSpec((8, 16, D), lambda i, s: (i, 0, 0))] * 8,
            out_specs=pl.BlockSpec((ROWS, SLICE), lambda i, s: (0, i)),
        ),
        out_shape=jax.ShapeDtypeStruct((ROWS, D), jnp.bfloat16),
        compiler_params=pltpu.CompilerParams(vmem_limit_bytes=20 * 2**20),
        cost_estimate=pl.CostEstimate(
            flops=2 * 10**9, bytes_accessed=8 * 2**20, transcendentals=0
        ),
        name="input_projection",
    )(place, grads.reshape(3 * D, ROWS), *pieces)


def gather_plane(input_weights, output_weight):
    x_at = lax.axis_index("x")
    mine = jnp.concatenate(
        [
            lax.dynamic_slice(input_weights, (0, x_at * 3 * SLICE), (16, 3 * SLICE)),
            lax.dynamic_slice(output_weight, (0, x_at * SLICE), (16, SLICE)),
        ],
        axis=1,
    )
    return lax.all_to_all(jnp.broadcast_to(mine[None], (32, 16, D)), PLANE_AXES, 0, 0, tiled=True)


def swap_cores(block):
    return lax.ppermute(block, "c", ring(2, 1))


def spread_x(plane):
    half = plane.shape[0] // 2
    after = lax.ppermute(plane, "x", ring(4, -1))
    before = lax.ppermute(plane, "x", ring(4, 1))
    far_a = lax.ppermute(before[:half], "x", ring(4, 1))
    far_b = lax.ppermute(after[half:], "x", ring(4, -1))
    own = [plane, after, jnp.concatenate([far_a, far_b], axis=0), before]
    return own + [swap_cores(piece) for piece in own]


def sum_cores(keep, send):
    return (keep.astype(jnp.float32) + swap_cores(send).astype(jnp.float32)).astype(jnp.bfloat16)


def gather_x(share):
    x_at = lax.axis_index("x")
    result = jnp.zeros((16, D), jnp.float32)
    for shift in range(4):
        columns = share if shift == 0 else lax.ppermute(share, "x", ring(4, -shift))
        at = lax.rem(x_at + shift, 4) * SLICE
        result = lax.dynamic_update_slice(result, columns, (0, at))
    return result


def on_device(query_rows, key_rows, value_rows, upstream, input_weights, output_weight):
    factor = 1.0 / (8 * math.sqrt(16384))
    place = jnp.stack([lax.axis_index(a) for a in ("x", "c")]).astype(jnp.int32)
    plane = gather_plane(input_weights, output_weight)
    sent = jnp.concatenate(
        [a.reshape(CLIP_LEN, PATCH_BLOCK, D) for a in (query_rows, key_rows, value_rows, upstream)],
        axis=2,
    )
    sent, plane = lax.optimization_barrier((sent, plane))
    moved = lax.all_to_all(sent, CLIP_AXES, 0, 0, tiled=True).reshape(ROWS, 4 * D)
    moved, pieces = lax.optimization_barrier((moved, spread_x(plane)))
    attention, keep, send = forward_call(place, moved)
    attention, steps = lax.optimization_barrier((attention, sum_cores(keep, send)))
    steps = lax.all_to_all(steps, "x", 0, 0, tiled=True)
    grads = backward_call(place, attention, moved, pieces)
    grads, steps = lax.optimization_barrier((grads, steps))
    share = jnp.sum(steps.astype(jnp.float32), axis=0).astype(jnp.bfloat16)
    share = lax.all_to_all(share.reshape(32, 16, SLICE), PLANE_AXES, 0, 0, tiled=True)
    result = projection_call(place, grads, pieces).reshape(CLIP_LEN, PATCH_BLOCK, D)
    share = jnp.sum(share.astype(jnp.float32), axis=0) * factor
    share = share + lax.ppermute(share, "zh", ring(2, 1))
    result, share = lax.optimization_barrier((result, share))
    input_gradient = lax.all_to_all(result, CLIP_AXES, 0, 0, tiled=True)
    weight_gradient = gather_x(share)
    return (input_gradient.reshape(query_rows.shape), weight_gradient)


def solution(mesh):
    axes = ("yh", "yl", "zl", "c", "zh", "x")
    fine = Mesh(mesh.devices.reshape(2, 4, 4, 2, 2, 4), axes)
    seq, dp = ("yh", "yl", "zl", "c"), ("zh", "x")
    rows = P(dp, seq, None, None)
    return jax.shard_map(
        on_device,
        mesh=fine,
        in_specs=(rows, rows, rows, rows, P(seq, None), P(seq, None)),
        out_specs=(rows, P(seq, None)),
        check_vma=False,
    )
```

time: 248 us -> 196 us (0.79)
  starting transfers between devices: 107 us -> 76.4 us
  waiting for transfers between devices: 81.7 us -> 61.8 us
  blocking collectives: 21.6 us -> 18.4 us
    ppermute x15 -> x13, starting transfers between devices: 74.2 us -> 43.3 us  [the longest x5 14.3 us: swap_cores(): return lax.ppermute(block, 'c', ring(2, 1))]
    ppermute x15 -> x13, waiting for transfers between devices: 59.7 us -> 31.1 us  [the longest x1 21.2 us: spread_x(): before = lax.ppermute(plane, 'x', ring(4, 1))]
    all_to_all x2, waiting for transfers between devices: 6.4 us -> 26.6 us  [the longest x1 25.1 us: gather_plane(): lax.all_to_all(jnp.broadcast_to(mine[None], (32, 16, D)), PLANE_AXES, 0,...]
    all_to_all x1, waiting for transfers between devices: 15.6 us -> 3.98 us  [on_device(): input_gradient = lax.all_to_all(result, CLIP_AXES, 0, 0, tiled=True)]
    all_to_all x2, starting transfers between devices: 14.3 us -> 18.1 us  [the longest x1 13.5 us: gather_plane(): lax.all_to_all(jnp.broadcast_to(mine[None], (32, 16, D)), PLANE_AXES, 0,...]
    all_to_all x1, starting transfers between devices: 10.9 us -> 7.44 us  [on_device(): lax.all_to_all(sent, CLIP_AXES, 0, 0, tiled=True).reshape(ROWS, 4 * D)]
    all_to_all x2 -> x1, blocking collectives: 21.6 us -> 18.4 us  [on_device(): lax.all_to_all(share.reshape(32, 16, SLICE), PLANE_AXES, 0, 0, tiled=True)]
    pallas_call x2 -> x3, Pallas kernels: 21.5 us -> 23 us  [the longest x1 10.9 us: backward_call(): pl.pallas_call(backward_kernel, grid_spec=pltpu.PrefetchScalarGridSpec(nu...]
  transfers between devices with their start and end apart: 19 -> 17, of which waited for: 9 -> 9; matrix products, arithmetic and copies ran while one was open for 2% -> 3% of each run, Pallas kernels for 3% -> 9%
where the time goes in v2:
time: 196 us; the launch traced here: 194 us
  starting transfers between devices  76.4 us (39%)
  waiting for transfers between devices  61.8 us (32%)
  Pallas kernels  23 us (12%)
  blocking collectives  18.4 us (9%)
  local copies, waits for them, and re-layouts  9.56 us (5%)
  other arithmetic  4.41 us (2%)
    all_to_all x1, waiting for transfers between devices, gather_plane(): lax.all_to_all(jnp.broadcast_to(mine[None], (32, 16, D)), PLANE_AXES, 0,...  25.1 us
    ppermute x1, waiting for transfers between devices, spread_x(): before = lax.ppermute(plane, 'x', ring(4, 1))  21.2 us
    all_to_all x1, blocking collectives, on_device(): lax.all_to_all(share.reshape(32, 16, SLICE), PLANE_AXES, 0, 0, tiled=True)  18.4 us
    ppermute x5, starting transfers between devices, swap_cores(): return lax.ppermute(block, 'c', ring(2, 1))  14.3 us
    all_to_all x1, starting transfers between devices, gather_plane(): lax.all_to_all(jnp.broadcast_to(mine[None], (32, 16, D)), PLANE_AXES, 0,...  13.5 us
    pallas_call x1, Pallas kernels, backward_call(): pl.pallas_call(backward_kernel, grid_spec=pltpu.PrefetchScalarGridSpec(nu...  10.9 us
    ppermute x3, starting transfers between devices, gather_x(): columns = share if shift == 0 else lax.ppermute(share, 'x', ring(4, -shift))  8.11 us
    ppermute x1, starting transfers between devices, on_device(): share = share + lax.ppermute(share, 'zh', ring(2, 1))  7.94 us
  transfers between devices with their start and end apart: 17, of which 9 were waited for; matrix products, arithmetic and copies ran while one was open for 3% of the time, Pallas kernels for 9%

profile of v2, /device:TPU:1, one launch (start us, length us, event | category | flops | bytes accessed | tf_op | source)
XLA Modules:
  0.0 194.4 jit_solution(10929751952782193375)
XLA Ops:
  0.6 0.0 copy-start
  0.6 0.0 copy-start.6
  0.7 0.0 copy-start.5
  0.7 0.0 copy-start.4
  0.7 0.0 copy-start.3
  0.7 0.8 copy-done
  1.5 0.7 constant_dynamic-slice_fusion
  2.2 1.1 broadcast_in_dim.4
  3.4 13.5 %all-to-all-start = ((bf16[32,16,1024]{2,1,0:T(8,128)(2,1)}), bf16[32,16,1024]{2,1,0:T(8,128)(2,1)S(1)}, u32[]{:S(2)}, u32[]{:S(2)}) async-start(bf16[32,16,1024]{2,1,0:T(8,128)(2,1)} %broadcast_in_dim.4), calls=%async_computation | async-start | bytes 2097152 | tf_op jit(solution)/shard_map/all_to_all | solution.py:202
  16.8 0.0 copy-done.6
  16.8 0.0 copy-done.5
  16.9 0.0 copy-done.4
  16.9 0.0 copy-done.3
  16.9 1.5 pad_maximum_fusion
  18.4 25.1 %all-to-all-done.refs_0_ = bf16[32,16,1024]{2,1,0:T(8,128)(2,1)S(1)} async-done(((bf16[32,16,1024]{2,1,0:T(8,128)(2,1)}), bf16[32,16,1024]{2,1,0:T(8,128)(2,1)S(1)}, u32[]{:S(2)}, u32[]{:S(2)}) %all-to-all-start) | async-done | bytes 1048608 | tf_op jit(solution)/shard_map/all_to_all | solution.py:202
  43.5 7.4 %all-to-all-start.1 = ((bf16[32,8,4096]{2,1,0:T(8,128)(2,1)}), bf16[32,8,4096]{2,1,0:T(8,128)(2,1)S(1)}, u32[]{:S(2)}, u32[]{:S(2)}) async-start(bf16[32,8,4096]{2,1,0:T(8,128)(2,1)} %pad_maximum_fusion), calls=%async_computation.1 | async-start | bytes 4194304 | tf_op jit(solution)/shard_map/all_to_all | solution.py:242
  50.9 3.1 %collective-permute-start.1 = (bf16[32,16,1024]{2,1,0:T(8,128)(2,1)S(1)}, bf16[32,16,1024]{2,1,0:T(8,128)(2,1)}, u32[]{:S(2)}, u32[]{:S(2)}) collective-permute-start(bf16[32,16,1024]{2,1,0:T(8,128)(2,1)S(1)} %all-to-all-done.refs_0_), channel_id=1, source_target_pairs={{0,1},{1,2},{2,3},{3,0},{4,5},{5,6},{6,7},{7,4},{8,9},{9,10},{10,1... | collective-permute-start | bytes 3145736 | tf_op jit(solution)/shard_map/ppermute | solution.py:212
  54.0 3.4 %collective-permute-start = (bf16[32,16,1024]{2,1,0:T(8,128)(2,1)S(1)}, bf16[32,16,1024]{2,1,0:T(8,128)(2,1)}, u32[]{:S(2)}, u32[]{:S(2)}) collective-permute-start(bf16[32,16,1024]{2,1,0:T(8,128)(2,1)S(1)} %all-to-all-done.refs_0_), channel_id=1, source_target_pairs={{0,3},{1,0},{2,1},{3,2},{4,7},{5,4},{6,5},{7,6},{8,11},{9,8},{10,9... | collective-permute-start | bytes 3145736 | tf_op jit(solution)/shard_map/ppermute | solution.py:211
  57.4 21.2 %collective-permute-done.1.refs_3_ = bf16[32,16,1024]{2,1,0:T(8,128)(2,1)} collective-permute-done((bf16[32,16,1024]{2,1,0:T(8,128)(2,1)S(1)}, bf16[32,16,1024]{2,1,0:T(8,128)(2,1)}, u32[]{:S(2)}, u32[]{:S(2)}) %collective-permute-start.1) | collective-permute-done | bytes 1048608 | tf_op jit(solution)/shard_map/ppermute | solution.py:212
  78.6 1.1 slice.8
  79.7 1.9 collective-permute-start.2
  81.7 0.0 collective-permute-done.refs_1_
  81.7 1.1 slice.9
  82.8 4.6 %collective-permute-start.3 = (bf16[16,16,1024]{2,1,0:T(8,128)(2,1)S(1)}, bf16[16,16,1024]{2,1,0:T(8,128)(2,1)S(1)}, u32[]{:S(2)}, u32[]{:S(2)}) collective-permute-start(bf16[16,16,1024]{2,1,0:T(8,128)(2,1)S(1)} %slice.9), channel_id=1, source_target_pairs={{0,3},{1,0},{2,1},{3,2},{4,7},{5,4},{6,5},{7,6},{8,11},{9,8},{10,9... | collective-permute-start | bytes 1572872 | tf_op jit(solution)/shard_map/ppermute | solution.py:214
  87.3 3.5 %collective-permute-start.4 = (bf16[32,16,1024]{2,1,0:T(8,128)(2,1)S(1)}, bf16[32,16,1024]{2,1,0:T(8,128)(2,1)}, u32[]{:S(2)}, u32[]{:S(2)}) collective-permute-start(bf16[32,16,1024]{2,1,0:T(8,128)(2,1)S(1)} %all-to-all-done.refs_0_), channel_id=1, source_target_pairs={{0,8},{8,0},{1,9},{9,1},{2,10},{10,2},{3,11},{11,3},{4,12},{12,4},... | collective-permute-start | bytes 3145736 | tf_op jit(solution)/shard_map/ppermute | solution.py:206
  90.9 1.9 collective-permute-start.5
  92.8 2.4 %collective-permute-start.7 = (bf16[32,16,1024]{2,1,0:T(8,128)(2,1)}, bf16[32,16,1024]{2,1,0:T(8,128)(2,1)}, u32[]{:S(2)}, u32[]{:S(2)}) collective-permute-start(bf16[32,16,1024]{2,1,0:T(8,128)(2,1)} %collective-permute-done.1.refs_3_), channel_id=1, source_target_pairs={{0,8},{8,0},{1,9},{9,1},{2,10},{10,2},{3,11},{11,3},{4,12},{12,4},... | collective-permute-start | bytes 3145736 | tf_op jit(solution)/shard_map/ppermute | solution.py:206
  95.2 0.0 collective-permute-done.2
  95.2 0.9 constant_dynamic-update-slice_fusion.1
  96.1 1.1 collective-permute-done.3
  97.2 0.8 constant_dynamic-update-slice_fusion.refs_2_
  98.0 4.1 %collective-permute-start.6 = (bf16[32,16,1024]{2,1,0:T(8,128)(2,1)}, bf16[32,16,1024]{2,1,0:T(8,128)(2,1)}, u32[]{:S(2)}, u32[]{:S(2)}) collective-permute-start(bf16[32,16,1024]{2,1,0:T(8,128)(2,1)} %constant_dynamic-update-slice_fusion.refs_2_), channel_id=1, source_target_pairs={{0,8},{8,0},{1,9},{9,1},{2,10},{10,2},{3,11},{11,3},{4,12},{12,4},... | collective-permute-start | bytes 3145736 | tf_op jit(solution)/shard_map/ppermute | solution.py:206
  102.2 0.1 pad_add_fusion.place
  102.3 0.0 collective-permute-done.4.refs_4_
  102.3 0.0 collective-permute-done.5.refs_5_
  102.3 0.0 collective-permute-done.7.refs_7_
  102.3 2.5 %collective-permute-done.6.refs_6_ = bf16[32,16,1024]{2,1,0:T(8,128)(2,1)} collective-permute-done((bf16[32,16,1024]{2,1,0:T(8,128)(2,1)}, bf16[32,16,1024]{2,1,0:T(8,128)(2,1)}, u32[]{:S(2)}, u32[]{:S(2)}) %collective-permute-start.6) | collective-permute-done | bytes 1048608 | tf_op jit(solution)/shard_map/ppermute | solution.py:206
  104.8 0.0 all-to-all-done.1
  104.8 5.9 %attention_and_weight_grad.1 = (f32[16,256,256]{2,1,0:T(8,128)}, bf16[4,512,256]{2,1,0:T(8,128)(2,1)S(1)}, bf16[4,512,256]{2,1,0:T(8,128)(2,1)S(1)}) custom-call(s32[2]{0:T(128)S(1)} %pad_add_fusion.place, bf16[256,4096]{1,0:T(8,128)(2,1)S(1)} %bitcast.11, bf16[256,4096]{1,0:T(8,128)(2,1)S(1)} %bitcast.12, bf16[256,4096]{1,0:T(8,128)(2,1)S(1)} %bitcast.13, ...), custom_call_target="tpu_custom_call" | custom-call | flops 2000000000 | bytes 8388608 | tf_op jit(solution)/shard_map/attention_and_weight_grad/pallas_call | solution.py:83
  110.7 2.3 %collective-permute-start.8 = (bf16[4,512,256]{2,1,0:T(8,128)(2,1)S(1)}, bf16[4,512,256]{2,1,0:T(8,128)(2,1)S(1)}, u32[]{:S(2)}, u32[]{:S(2)}) collective-permute-start(bf16[4,512,256]{2,1,0:T(8,128)(2,1)S(1)} %get-tuple-element.27), channel_id=1, source_target_pairs={{0,8},{8,0},{1,9},{9,1},{2,10},{10,2},{3,11},{11,3},{4,12},{12,4},... | collective-permute-start | bytes 3145736 | tf_op jit(solution)/shard_map/ppermute | solution.py:206
  113.0 2.3 %collective-permute-done.8 = bf16[4,512,256]{2,1,0:T(8,128)(2,1)S(1)} collective-permute-done((bf16[4,512,256]{2,1,0:T(8,128)(2,1)S(1)}, bf16[4,512,256]{2,1,0:T(8,128)(2,1)S(1)}, u32[]{:S(2)}, u32[]{:S(2)}) %collective-permute-start.8) | collective-permute-done | bytes 1048608 | tf_op jit(solution)/shard_map/ppermute | solution.py:206
  115.2 1.3 add_convert_fusion
  116.5 4.7 %all-to-all-start.2 = ((bf16[4,512,256]{2,1,0:T(8,128)(2,1)}), bf16[4,512,256]{2,1,0:T(8,128)(2,1)}, u32[]{:S(2)}, u32[]{:S(2)}) async-start(bf16[4,512,256]{2,1,0:T(8,128)(2,1)} %add_convert_fusion), calls=%async_computation.2 | async-start | bytes 2097152 | tf_op jit(solution)/shard_map/all_to_all | solution.py:246
  121.2 0.0 copy-start.2
  121.2 2.2 %copy-done.2 = f32[16,256,256]{2,1,0:T(8,128)S(1)} copy-done((f32[16,256,256]{2,1,0:T(8,128)S(1)}, f32[16,256,256]{2,1,0:T(8,128)}, u32[]{:S(2)}) %copy-start.2) | copy-done | bytes 4194328
  123.4 10.9 %attention_grads.1 = bf16[3,1024,256]{2,1,0:T(8,128)(2,1)} custom-call(s32[2]{0:T(128)S(1)} %pad_add_fusion.place, f32[16,256,256]{2,1,0:T(8,128)S(1)} %copy-done.2, bf16[256,4096]{1,0:T(8,128)(2,1)S(1)} %bitcast.15, bf16[256,4096]{1,0:T(8,128)(2,1)S(1)} %bitcast.16, bf16[256,4096]{1,0:T(8,128)(2,1)S(1)} %bitcast.17, bf16[256,4096]{1,0:T(8,128)(2,1)S(1)} %bitcast.18, ...), custom_call_target="tpu_custom_call" | custom-call | flops 3000000000 | bytes 10485760 | tf_op jit(solution)/shard_map/attention_grads/pallas_call | solution.py:138
  134.2 0.0 copy-start.1
  134.2 1.6 all-to-all-done.2
  135.8 1.5 reduce_sum.21
  137.3 18.4 %all_to_all.25 = bf16[32,16,256]{2,1,0:T(8,128)(2,1)S(1)} all-to-all(bf16[32,16,256]{2,1,0:T(8,128)(2,1)S(1)} %bitcast.21), channel_id=1, replica_groups=mesh['yh'=2,'yl'=4,'zl'=4,'c'=2,'zh'=2,'x'=4] {'yh','yl','zl'}, dimensions={0} | all-to-all | bytes 524288 | tf_op jit(solution)/shard_map/all_to_all | solution.py:250
  155.7 7.9 %collective-permute-start.9 = (f32[16,256]{1,0:T(8,128)S(1)}, f32[16,256]{1,0:T(8,128)S(1)}, u32[]{:S(2)}, u32[]{:S(2)}) collective-permute-start(f32[16,256]{1,0:T(8,128)S(1)} %broadcast_multiply_fusion), channel_id=1, source_target_pairs={{0,4},{4,0},{1,5},{5,1},{2,6},{6,2},{3,7},{7,3},{8,12},{12,8},{9,1... | collective-permute-start | bytes 49160 | tf_op jit(solution)/shard_map/ppermute | solution.py:253
  163.7 0.0 copy-done.1
  163.7 6.2 %input_projection.1 = bf16[256,1024]{1,0:T(8,128)(2,1)} custom-call(s32[2]{0:T(128)S(1)} %pad_add_fusion.place, bf16[3072,256]{1,0:T(8,128)(2,1)S(1)} %bitcast.19, bf16[32,16,1024]{2,1,0:T(8,128)(2,1)S(1)} %all-to-all-done.refs_0_, bf16[32,16,1024]{2,1,0:T(8,128)(2,1)} %collective-permute-done.refs_1_, ...), custom_call_target="tpu_custom_call" | custom-call | flops 2000000000 | bytes 8388608 | tf_op jit(solution)/shard_map/input_projection/pallas_call | solution.py:175
  169.9 0.0 collective-permute-done.9
  169.9 7.5 %all-to-all-start.4 = ((bf16[32,8,1024]{2,1,0:T(8,128)(2,1)}), bf16[32,8,1024]{2,1,0:T(8,128)(2,1)S(1)}, u32[]{:S(2)}, u32[]{:S(2)}) async-start(bf16[32,8,1024]{2,1,0:T(8,128)(2,1)} %bitcast.8), calls=%async_computation.4 | async-start | bytes 1048576 | tf_op jit(solution)/shard_map/all_to_all | solution.py:255
  177.5 3.1 %collective-permute-start.10 = (f32[16,256]{1,0:T(8,128)S(1)}, f32[16,256]{1,0:T(8,128)S(1)}, u32[]{:S(2)}, u32[]{:S(2)}) collective-permute-start(f32[16,256]{1,0:T(8,128)S(1)} %fusion), channel_id=1, source_target_pairs={{0,3},{1,0},{2,1},{3,2},{4,7},{5,4},{6,5},{7,6},{8,11},{9,8},{10,9... | collective-permute-start | bytes 49160 | tf_op jit(solution)/shard_map/ppermute | solution.py:227
  180.6 3.1 %collective-permute-start.11 = (f32[16,256]{1,0:T(8,128)S(1)}, f32[16,256]{1,0:T(8,128)S(1)}, u32[]{:S(2)}, u32[]{:S(2)}) collective-permute-start(f32[16,256]{1,0:T(8,128)S(1)} %fusion), channel_id=1, source_target_pairs={{0,2},{1,3},{2,0},{3,1},{4,6},{5,7},{6,4},{7,5},{8,10},{9,11},{10,... | collective-permute-start | bytes 49160 | tf_op jit(solution)/shard_map/ppermute | solution.py:227
  183.7 1.9 collective-permute-start.12
  185.6 0.0 collective-permute-done.10
  185.6 1.2 collective-permute-done.11
  186.8 2.8 %collective-permute-done.12 = f32[16,256]{1,0:T(8,128)S(1)} collective-permute-done((f32[16,256]{1,0:T(8,128)S(1)}, f32[16,256]{1,0:T(8,128)S(1)}, u32[]{:S(2)}, u32[]{:S(2)}) %collective-permute-start.12) | collective-permute-done | bytes 16416 | tf_op jit(solution)/shard_map/ppermute | solution.py:227
  189.7 4.0 %all-to-all-done.4 = bf16[32,8,1024]{2,1,0:T(8,128)(2,1)S(1)} async-done(((bf16[32,8,1024]{2,1,0:T(8,128)(2,1)}), bf16[32,8,1024]{2,1,0:T(8,128)(2,1)S(1)}, u32[]{:S(2)}, u32[]{:S(2)}) %all-to-all-start.4) | async-done | bytes 524320 | tf_op jit(solution)/shard_map/all_to_all | solution.py:255
  193.6 0.8 copy.14
  194.4 0.0 copy-done.7
  (11 shorter events, 0.1 us)
Async XLA Ops:
  0.6 0.9 copy-start
  0.6 16.2 %copy-start.6 = (bf16[1,1,256,1024]{3,2,1,0:T(8,128)(2,1)S(1)}, bf16[1,1,256,1024]{3,2,1,0:T(8,128)(2,1)}, u32[]{:S(2)}) copy-start(bf16[1,1,256,1024]{3,2,1,0:T(8,128)(2,1)} %param.6) | copy-start | bytes 1572868
  0.7 16.2 %copy-start.5 = (bf16[1,1,256,1024]{3,2,1,0:T(8,128)(2,1)S(1)}, bf16[1,1,256,1024]{3,2,1,0:T(8,128)(2,1)}, u32[]{:S(2)}) copy-start(bf16[1,1,256,1024]{3,2,1,0:T(8,128)(2,1)} %param.7) | copy-start | bytes 1572868
  0.7 16.2 %copy-start.4 = (bf16[1,1,256,1024]{3,2,1,0:T(8,128)(2,1)S(1)}, bf16[1,1,256,1024]{3,2,1,0:T(8,128)(2,1)}, u32[]{:S(2)}) copy-start(bf16[1,1,256,1024]{3,2,1,0:T(8,128)(2,1)} %param.8) | copy-start | bytes 1572868
  0.7 16.2 %copy-start.3 = (bf16[1,1,256,1024]{3,2,1,0:T(8,128)(2,1)S(1)}, bf16[1,1,256,1024]{3,2,1,0:T(8,128)(2,1)}, u32[]{:S(2)}) copy-start(bf16[1,1,256,1024]{3,2,1,0:T(8,128)(2,1)} %param.9) | copy-start | bytes 1572868
  3.4 40.1 %all-to-all-start = ((bf16[32,16,1024]{2,1,0:T(8,128)(2,1)}), bf16[32,16,1024]{2,1,0:T(8,128)(2,1)S(1)}, u32[]{:S(2)}, u32[]{:S(2)}) async-start(bf16[32,16,1024]{2,1,0:T(8,128)(2,1)} %broadcast_in_dim.4), calls=%async_computation | async-start | bytes 2097152 | tf_op jit(solution)/shard_map/all_to_all | solution.py:202
  43.5 61.3 %all-to-all-start.1 = ((bf16[32,8,4096]{2,1,0:T(8,128)(2,1)}), bf16[32,8,4096]{2,1,0:T(8,128)(2,1)S(1)}, u32[]{:S(2)}, u32[]{:S(2)}) async-start(bf16[32,8,4096]{2,1,0:T(8,128)(2,1)} %pad_maximum_fusion), calls=%async_computation.1 | async-start | bytes 4194304 | tf_op jit(solution)/shard_map/all_to_all | solution.py:242
  50.9 27.7 %collective-permute-start.1 = (bf16[32,16,1024]{2,1,0:T(8,128)(2,1)S(1)}, bf16[32,16,1024]{2,1,0:T(8,128)(2,1)}, u32[]{:S(2)}, u32[]{:S(2)}) collective-permute-start(bf16[32,16,1024]{2,1,0:T(8,128)(2,1)S(1)} %all-to-all-done.refs_0_), channel_id=1, source_target_pairs={{0,1},{1,2},{2,3},{3,0},{4,5},{5,6},{6,7},{7,4},{8,9},{9,10},{10,1... | collective-permute-start | bytes 3145736 | tf_op jit(solution)/shard_map/ppermute | solution.py:212
  54.0 27.6 %collective-permute-start = (bf16[32,16,1024]{2,1,0:T(8,128)(2,1)S(1)}, bf16[32,16,1024]{2,1,0:T(8,128)(2,1)}, u32[]{:S(2)}, u32[]{:S(2)}) collective-permute-start(bf16[32,16,1024]{2,1,0:T(8,128)(2,1)S(1)} %all-to-all-done.refs_0_), channel_id=1, source_target_pairs={{0,3},{1,0},{2,1},{3,2},{4,7},{5,4},{6,5},{7,6},{8,11},{9,8},{10,9... | collective-permute-start | bytes 3145736 | tf_op jit(solution)/shard_map/ppermute | solution.py:211
  79.7 15.5 %collective-permute-start.2 = (bf16[16,16,1024]{2,1,0:T(8,128)(2,1)S(1)}, bf16[16,16,1024]{2,1,0:T(8,128)(2,1)S(1)}, u32[]{:S(2)}, u32[]{:S(2)}) collective-permute-start(bf16[16,16,1024]{2,1,0:T(8,128)(2,1)S(1)} %slice.8), channel_id=1, source_target_pairs={{0,1},{1,2},{2,3},{3,0},{4,5},{5,6},{6,7},{7,4},{8,9},{9,10},{10,1... | collective-permute-start | bytes 1572872 | tf_op jit(solution)/shard_map/ppermute | solution.py:213
  82.8 14.4 %collective-permute-start.3 = (bf16[16,16,1024]{2,1,0:T(8,128)(2,1)S(1)}, bf16[16,16,1024]{2,1,0:T(8,128)(2,1)S(1)}, u32[]{:S(2)}, u32[]{:S(2)}) collective-permute-start(bf16[16,16,1024]{2,1,0:T(8,128)(2,1)S(1)} %slice.9), channel_id=1, source_target_pairs={{0,3},{1,0},{2,1},{3,2},{4,7},{5,4},{6,5},{7,6},{8,11},{9,8},{10,9... | collective-permute-start | bytes 1572872 | tf_op jit(solution)/shard_map/ppermute | solution.py:214
  87.3 14.9 %collective-permute-start.4 = (bf16[32,16,1024]{2,1,0:T(8,128)(2,1)S(1)}, bf16[32,16,1024]{2,1,0:T(8,128)(2,1)}, u32[]{:S(2)}, u32[]{:S(2)}) collective-permute-start(bf16[32,16,1024]{2,1,0:T(8,128)(2,1)S(1)} %all-to-all-done.refs_0_), channel_id=1, source_target_pairs={{0,8},{8,0},{1,9},{9,1},{2,10},{10,2},{3,11},{11,3},{4,12},{12,4},... | collective-permute-start | bytes 3145736 | tf_op jit(solution)/shard_map/ppermute | solution.py:206
  90.9 11.4 %collective-permute-start.5 = (bf16[32,16,1024]{2,1,0:T(8,128)(2,1)}, bf16[32,16,1024]{2,1,0:T(8,128)(2,1)}, u32[]{:S(2)}, u32[]{:S(2)}) collective-permute-start(bf16[32,16,1024]{2,1,0:T(8,128)(2,1)} %collective-permute-done.refs_1_), channel_id=1, source_target_pairs={{0,8},{8,0},{1,9},{9,1},{2,10},{10,2},{3,11},{11,3},{4,12},{12,4},... | collective-permute-start | bytes 3145736 | tf_op jit(solution)/shard_map/ppermute | solution.py:206
  92.8 9.5 %collective-permute-start.7 = (bf16[32,16,1024]{2,1,0:T(8,128)(2,1)}, bf16[32,16,1024]{2,1,0:T(8,128)(2,1)}, u32[]{:S(2)}, u32[]{:S(2)}) collective-permute-start(bf16[32,16,1024]{2,1,0:T(8,128)(2,1)} %collective-permute-done.1.refs_3_), channel_id=1, source_target_pairs={{0,8},{8,0},{1,9},{9,1},{2,10},{10,2},{3,11},{11,3},{4,12},{12,4},... | collective-permute-start | bytes 3145736 | tf_op jit(solution)/shard_map/ppermute | solution.py:206
  98.0 6.8 %collective-permute-start.6 = (bf16[32,16,1024]{2,1,0:T(8,128)(2,1)}, bf16[32,16,1024]{2,1,0:T(8,128)(2,1)}, u32[]{:S(2)}, u32[]{:S(2)}) collective-permute-start(bf16[32,16,1024]{2,1,0:T(8,128)(2,1)} %constant_dynamic-update-slice_fusion.refs_2_), channel_id=1, source_target_pairs={{0,8},{8,0},{1,9},{9,1},{2,10},{10,2},{3,11},{11,3},{4,12},{12,4},... | collective-permute-start | bytes 3145736 | tf_op jit(solution)/shard_map/ppermute | solution.py:206
  110.7 4.5 %collective-permute-start.8 = (bf16[4,512,256]{2,1,0:T(8,128)(2,1)S(1)}, bf16[4,512,256]{2,1,0:T(8,128)(2,1)S(1)}, u32[]{:S(2)}, u32[]{:S(2)}) collective-permute-start(bf16[4,512,256]{2,1,0:T(8,128)(2,1)S(1)} %get-tuple-element.27), channel_id=1, source_target_pairs={{0,8},{8,0},{1,9},{9,1},{2,10},{10,2},{3,11},{11,3},{4,12},{12,4},... | collective-permute-start | bytes 3145736 | tf_op jit(solution)/shard_map/ppermute | solution.py:206
  116.5 19.3 %all-to-all-start.2 = ((bf16[4,512,256]{2,1,0:T(8,128)(2,1)}), bf16[4,512,256]{2,1,0:T(8,128)(2,1)}, u32[]{:S(2)}, u32[]{:S(2)}) async-start(bf16[4,512,256]{2,1,0:T(8,128)(2,1)} %add_convert_fusion), calls=%async_computation.2 | async-start | bytes 2097152 | tf_op jit(solution)/shard_map/all_to_all | solution.py:246
  121.2 2.2 %copy-start.2 = (f32[16,256,256]{2,1,0:T(8,128)S(1)}, f32[16,256,256]{2,1,0:T(8,128)}, u32[]{:S(2)}) copy-start(f32[16,256,256]{2,1,0:T(8,128)} %get-tuple-element.28.attention_ref) | copy-start | bytes 12582916
  134.2 29.4 %copy-start.1 = (bf16[3,1024,256]{2,1,0:T(8,128)(2,1)S(1)}, bf16[3,1024,256]{2,1,0:T(8,128)(2,1)}, u32[]{:S(2)}) copy-start(bf16[3,1024,256]{2,1,0:T(8,128)(2,1)} %attention_grads.1) | copy-start | bytes 4718596
  155.7 14.2 %collective-permute-start.9 = (f32[16,256]{1,0:T(8,128)S(1)}, f32[16,256]{1,0:T(8,128)S(1)}, u32[]{:S(2)}, u32[]{:S(2)}) collective-permute-start(f32[16,256]{1,0:T(8,128)S(1)} %broadcast_multiply_fusion), channel_id=1, source_target_pairs={{0,4},{4,0},{1,5},{5,1},{2,6},{6,2},{3,7},{7,3},{8,12},{12,8},{9,1... | collective-permute-start | bytes 49160 | tf_op jit(solution)/shard_map/ppermute | solution.py:253
  169.9 23.7 %all-to-all-start.4 = ((bf16[32,8,1024]{2,1,0:T(8,128)(2,1)}), bf16[32,8,1024]{2,1,0:T(8,128)(2,1)S(1)}, u32[]{:S(2)}, u32[]{:S(2)}) async-start(bf16[32,8,1024]{2,1,0:T(8,128)(2,1)} %bitcast.8), calls=%async_computation.4 | async-start | bytes 1048576 | tf_op jit(solution)/shard_map/all_to_all | solution.py:255
  177.5 8.2 %collective-permute-start.10 = (f32[16,256]{1,0:T(8,128)S(1)}, f32[16,256]{1,0:T(8,128)S(1)}, u32[]{:S(2)}, u32[]{:S(2)}) collective-permute-start(f32[16,256]{1,0:T(8,128)S(1)} %fusion), channel_id=1, source_target_pairs={{0,3},{1,0},{2,1},{3,2},{4,7},{5,4},{6,5},{7,6},{8,11},{9,8},{10,9... | collective-permute-start | bytes 49160 | tf_op jit(solution)/shard_map/ppermute | solution.py:227
  180.6 6.3 %collective-permute-start.11 = (f32[16,256]{1,0:T(8,128)S(1)}, f32[16,256]{1,0:T(8,128)S(1)}, u32[]{:S(2)}, u32[]{:S(2)}) collective-permute-start(f32[16,256]{1,0:T(8,128)S(1)} %fusion), channel_id=1, source_target_pairs={{0,2},{1,3},{2,0},{3,1},{4,6},{5,7},{6,4},{7,5},{8,10},{9,11},{10,... | collective-permute-start | bytes 49160 | tf_op jit(solution)/shard_map/ppermute | solution.py:227
  183.7 6.0 %collective-permute-start.12 = (f32[16,256]{1,0:T(8,128)S(1)}, f32[16,256]{1,0:T(8,128)S(1)}, u32[]{:S(2)}, u32[]{:S(2)}) collective-permute-start(f32[16,256]{1,0:T(8,128)S(1)} %fusion), channel_id=1, source_target_pairs={{0,1},{1,2},{2,3},{3,0},{4,5},{5,6},{6,7},{7,4},{8,9},{9,10},{10,1... | collective-permute-start | bytes 49160 | tf_op jit(solution)/shard_map/ppermute | solution.py:227
  189.6 4.8 %copy-start.7 = (f32[16,1024]{1,0:T(8,128)}, f32[16,1024]{1,0:T(8,128)S(1)}, u32[]{:S(2)}) copy-start(f32[16,1024]{1,0:T(8,128)S(1)} %constant_dynamic-update-slice_fusion.2) | copy-start | bytes 196612

commit v3 on v2

--- a/solution.py
+++ b/solution.py
@@ -55,31 +55,32 @@
 
     q, k = q_ref[...], k_ref[...]
     v_t = v_ref[...].T
-    context_t = []
-    for head in range(4):
-        scores = dot(q, head_only(k, head), NT) + bias[...]
-        top = jnp.max(scores, axis=1, keepdims=True)
-        e = jnp.exp2((scores - top) * (math.log2(math.e) / math.sqrt(HEAD_DIM)))
+    scores = [dot(q, head_only(k, head), NT) for head in range(4)]
+    weights = []
+    for head in range(4):
+        masked = scores[head] + bias[...]
+        top = jnp.max(masked, axis=1, keepdims=True)
+        e = jnp.exp2((masked - top) * (math.log2(math.e) / math.sqrt(HEAD_DIM)))
         attention = e * (1.0 / jnp.sum(e, axis=1, keepdims=True))
         attention_ref[head] = attention
+        weights.append(attention.astype(jnp.bfloat16))
+    context_t = []
+    for head in range(4):
         rows = v_t[head * HEAD_DIM : (head + 1) * HEAD_DIM]
-        context_t.append(dot(rows, attention.astype(jnp.bfloat16), NT).astype(jnp.bfloat16))
+        context_t.append(dot(rows, weights[head], NT).astype(jnp.bfloat16))
     context_t = jnp.concatenate(context_t, axis=0)
     dw = dot(context_t, u_ref[...], NN).astype(jnp.bfloat16)
     dw = dw.reshape(8, 2, 16, D)
     halves = dw[:, 0].reshape(128, D), dw[:, 1].reshape(128, D)
-    keep = jnp.where(core == 0, halves[0], halves[1])
-    send = jnp.where(core == 0, halves[1], halves[0])
-    for x in range(4):
-        keep_ref[x] = keep[:, x * SLICE : (x + 1) * SLICE]
-        send_ref[x] = send[:, x * SLICE : (x + 1) * SLICE]
+    keep_ref[...] = jnp.where(core == 0, halves[0], halves[1])
+    send_ref[...] = jnp.where(core == 0, halves[1], halves[0])
 
 
 def forward_call(place, moved):
     def column(base):
         return pl.BlockSpec((ROWS, SLICE), lambda i, s: (0, base + i))
 
-    shares = pl.BlockSpec((4, 128, SLICE), lambda i, s: (0, i, 0))
+    shares = pl.BlockSpec((128, D), lambda i, s: (i, 0))
     return pl.pallas_call(
         forward_kernel,
         grid_spec=pltpu.PrefetchScalarGridSpec(
@@ -96,8 +97,8 @@
         ),
         out_shape=[
             pltpu.HBM((16, ROWS, ROWS), jnp.float32),
-            jax.ShapeDtypeStruct((4, 512, SLICE), jnp.bfloat16),
-            jax.ShapeDtypeStruct((4, 512, SLICE), jnp.bfloat16),
+            jax.ShapeDtypeStruct((512, D), jnp.bfloat16),
+            jax.ShapeDtypeStruct((512, D), jnp.bfloat16),
         ],
         compiler_params=pltpu.CompilerParams(vmem_limit_bytes=20 * 2**20),
         cost_estimate=pl.CostEstimate(
@@ -118,16 +119,18 @@
     cg = cg.astype(jnp.bfloat16)
     v = v_ref[...]
     q_t, k_t, cg_t = q_ref[...].T, k_ref[...].T, cg.T
+    grad_scores = [dot(cg, head_only(v, head), NT) for head in range(4)]
+    score_grads = []
+    for head in range(4):
+        attention = attention_ref[head]
+        total = jnp.sum(attention * grad_scores[head], axis=1, keepdims=True)
+        score_grad = attention * (grad_scores[head] - total) * (1.0 / math.sqrt(HEAD_DIM))
+        score_grads.append(score_grad.astype(jnp.bfloat16))
     for head in range(4):
         rows = slice(head * HEAD_DIM, (head + 1) * HEAD_DIM)
-        attention = attention_ref[head]
-        attention_b = attention.astype(jnp.bfloat16)
-        grad_scores = dot(cg, head_only(v, head), NT)
-        total = jnp.sum(attention * grad_scores, axis=1, keepdims=True)
-        score_grad = attention * (grad_scores - total) * (1.0 / math.sqrt(HEAD_DIM))
-        score_grad = score_grad.astype(jnp.bfloat16)
-        g_ref[0, rows] = dot(k_t[rows], score_grad, NT).astype(jnp.bfloat16)
-        g_ref[1, rows] = dot(q_t[rows], score_grad, NN).astype(jnp.bfloat16)
+        attention_b = attention_ref[head].astype(jnp.bfloat16)
+        g_ref[0, rows] = dot(k_t[rows], score_grads[head], NT).astype(jnp.bfloat16)
+        g_ref[1, rows] = dot(q_t[rows], score_grads[head], NN).astype(jnp.bfloat16)
         g_ref[2, rows] = dot(cg_t[rows], attention_b, NN).astype(jnp.bfloat16)
 
 
@@ -220,14 +223,10 @@
     return (keep.astype(jnp.float32) + swap_cores(send).astype(jnp.float32)).astype(jnp.bfloat16)
 
 
-def gather_x(share):
-    x_at = lax.axis_index("x")
-    result = jnp.zeros((16, D), jnp.float32)
-    for shift in range(4):
-        columns = share if shift == 0 else lax.ppermute(share, "x", ring(4, -shift))
-        at = lax.rem(x_at + shift, 4) * SLICE
-        result = lax.dynamic_update_slice(result, columns, (0, at))
-    return result
+def sum_groups(share):
+    for bit in (1, 2):
+        share = share + lax.ppermute(share, "x", [(i, i ^ bit) for i in range(4)])
+    return share + lax.ppermute(share, "zh", ring(2, 1))
 
 
 def on_device(query_rows, key_rows, value_rows, upstream, input_weights, output_weight):
@@ -242,18 +241,13 @@
     moved = lax.all_to_all(sent, CLIP_AXES, 0, 0, tiled=True).reshape(ROWS, 4 * D)
     moved, pieces = lax.optimization_barrier((moved, spread_x(plane)))
     attention, keep, send = forward_call(place, moved)
-    attention, steps = lax.optimization_barrier((attention, sum_cores(keep, send)))
-    steps = lax.all_to_all(steps, "x", 0, 0, tiled=True)
+    attention, share = lax.optimization_barrier((attention, sum_cores(keep, send)))
+    share = lax.all_to_all(share.reshape(32, 16, D), PLANE_AXES, 0, 0, tiled=True)
     grads = backward_call(place, attention, moved, pieces)
-    grads, steps = lax.optimization_barrier((grads, steps))
-    share = jnp.sum(steps.astype(jnp.float32), axis=0).astype(jnp.bfloat16)
-    share = lax.all_to_all(share.reshape(32, 16, SLICE), PLANE_AXES, 0, 0, tiled=True)
     result = projection_call(place, grads, pieces).reshape(CLIP_LEN, PATCH_BLOCK, D)
-    share = jnp.sum(share.astype(jnp.float32), axis=0) * factor
-    share = share + lax.ppermute(share, "zh", ring(2, 1))
     result, share = lax.optimization_barrier((result, share))
     input_gradient = lax.all_to_all(result, CLIP_AXES, 0, 0, tiled=True)
-    weight_gradient = gather_x(share)
+    weight_gradient = sum_groups(jnp.sum(share.astype(jnp.float32), axis=0) * factor)
     return (input_gradient.reshape(query_rows.shape), weight_gradient)
 
 

time: 196 us -> 186 us (0.949); the launches traced: 194 us -> 182 us
  blocking collectives: 18.4 us -> 0 us
  waiting for transfers between devices: 61.8 us -> 68.5 us
  Pallas kernels: 23 us -> 18.8 us
  starting transfers between devices: 76.4 us -> 78.7 us
    all_to_all x1 -> x0, blocking collectives: 18.4 us -> none  [on_device(): lax.all_to_all(share.reshape(32, 16, SLICE), PLANE_AXES, 0, 0, tiled=True)]
    all_to_all x1, waiting for transfers between devices: 1.58 us -> 9.97 us  [on_device(): lax.all_to_all(share.reshape(32, 16, D), PLANE_AXES, 0, 0, tiled=True)]
    all_to_all x1, waiting for transfers between devices: 3.98 us -> 0.01 us  [on_device(): input_gradient = lax.all_to_all(result, CLIP_AXES, 0, 0, tiled=True)]
    pallas_call x1, Pallas kernels: 10.9 us -> 7.22 us  [backward_call(): pl.pallas_call(backward_kernel, grid_spec=pltpu.PrefetchScalarGridSpec(nu...]
    all_to_all x1, starting transfers between devices: 4.68 us -> 7.64 us  [on_device(): lax.all_to_all(share.reshape(32, 16, D), PLANE_AXES, 0, 0, tiled=True)]
    ppermute x4 -> x3, waiting for transfers between devices: 4 us -> 6.33 us  [the longest x2 4.59 us: sum_groups(): share = share + lax.ppermute(share, 'x', [(i, i ^ bit) for i in range(4)])]
    unnamed x18 -> x16, local copies, waits for them, and re-layouts: 4.73 us -> 5.31 us
    ppermute x4 -> x3, starting transfers between devices: 16 us -> 15.9 us  [the longest x2 7.97 us: sum_groups(): share = share + lax.ppermute(share, 'x', [(i, i ^ bit) for i in range(4)])]
  transfers between devices with their start and end apart: 17 -> 16, of which waited for: 9 -> 9; matrix products, arithmetic and copies ran while one was open for 3% -> 4% of each run, Pallas kernels for 9% -> 7%
where the time goes in v3:
time: 186 us; the launch traced here: 182 us
  starting transfers between devices  78.7 us (42%)
  waiting for transfers between devices  68.5 us (37%)
  Pallas kernels  18.8 us (10%)
  local copies, waits for them, and re-layouts  10.3 us (6%)
  other arithmetic  5.05 us (3%)
    all_to_all x1, waiting for transfers between devices, gather_plane(): lax.all_to_all(jnp.broadcast_to(mine[None], (32, 16, D)), PLANE_AXES, 0,...  25.1 us
    ppermute x1, waiting for transfers between devices, spread_x(): before = lax.ppermute(plane, 'x', ring(4, 1))  21.2 us
    ppermute x5, starting transfers between devices, swap_cores(): return lax.ppermute(block, 'c', ring(2, 1))  14.2 us
    all_to_all x1, starting transfers between devices, gather_plane(): lax.all_to_all(jnp.broadcast_to(mine[None], (32, 16, D)), PLANE_AXES, 0,...  13.5 us
    all_to_all x1, waiting for transfers between devices, on_device(): lax.all_to_all(share.reshape(32, 16, D), PLANE_AXES, 0, 0, tiled=True)  9.97 us
    ppermute x2, starting transfers between devices, sum_groups(): share = share + lax.ppermute(share, 'x', [(i, i ^ bit) for i in range(4)])  7.97 us
    ppermute x1, starting transfers between devices, sum_groups(): return share + lax.ppermute(share, 'zh', ring(2, 1))  7.94 us
    all_to_all x1, starting transfers between devices, on_device(): lax.all_to_all(share.reshape(32, 16, D), PLANE_AXES, 0, 0, tiled=True)  7.64 us
  transfers between devices with their start and end apart: 16, of which 9 were waited for; matrix products, arithmetic and copies ran while one was open for 4% of the time, Pallas kernels for 7%

profile of v3, /device:TPU:1, one launch (start us, length us, event | category | flops | bytes accessed | tf_op | source)
XLA Modules:
  0.0 182.3 jit_solution(12137705497250210360)
XLA Ops:
  0.6 0.0 copy-start
  0.6 0.0 copy-start.3
  0.7 0.0 copy-start.4
  0.7 0.0 copy-start.5
  0.7 0.0 copy-start.6
  0.7 0.9 constant_dynamic-slice_fusion
  1.5 0.0 copy-done
  1.6 1.1 broadcast_in_dim.2
  2.7 13.5 %all-to-all-start = ((bf16[32,16,1024]{2,1,0:T(8,128)(2,1)}), bf16[32,16,1024]{2,1,0:T(8,128)(2,1)S(1)}, u32[]{:S(2)}, u32[]{:S(2)}) async-start(bf16[32,16,1024]{2,1,0:T(8,128)(2,1)} %broadcast_in_dim.2), calls=%async_computation | async-start | bytes 2097152 | tf_op jit(solution)/shard_map/all_to_all | solution.py:205
  16.1 0.0 copy-done.3
  16.2 0.0 copy-done.4
  16.2 0.0 copy-done.5
  16.2 0.0 copy-done.6
  16.2 1.5 pad_maximum_fusion
  17.7 25.1 %all-to-all-done.refs_0_ = bf16[32,16,1024]{2,1,0:T(8,128)(2,1)S(1)} async-done(((bf16[32,16,1024]{2,1,0:T(8,128)(2,1)}), bf16[32,16,1024]{2,1,0:T(8,128)(2,1)S(1)}, u32[]{:S(2)}, u32[]{:S(2)}) %all-to-all-start) | async-done | bytes 1048608 | tf_op jit(solution)/shard_map/all_to_all | solution.py:205
  42.8 7.4 %all-to-all-start.1 = ((bf16[32,8,4096]{2,1,0:T(8,128)(2,1)}), bf16[32,8,4096]{2,1,0:T(8,128)(2,1)S(1)}, u32[]{:S(2)}, u32[]{:S(2)}) async-start(bf16[32,8,4096]{2,1,0:T(8,128)(2,1)} %pad_maximum_fusion), calls=%async_computation.1 | async-start | bytes 4194304 | tf_op jit(solution)/shard_map/all_to_all | solution.py:241
  50.2 3.1 %collective-permute-start.1 = (bf16[32,16,1024]{2,1,0:T(8,128)(2,1)S(1)}, bf16[32,16,1024]{2,1,0:T(8,128)(2,1)}, u32[]{:S(2)}, u32[]{:S(2)}) collective-permute-start(bf16[32,16,1024]{2,1,0:T(8,128)(2,1)S(1)} %all-to-all-done.refs_0_), channel_id=1, source_target_pairs={{0,1},{1,2},{2,3},{3,0},{4,5},{5,6},{6,7},{7,4},{8,9},{9,10},{10,1... | collective-permute-start | bytes 3145736 | tf_op jit(solution)/shard_map/ppermute | solution.py:215
  53.4 3.4 %collective-permute-start = (bf16[32,16,1024]{2,1,0:T(8,128)(2,1)S(1)}, bf16[32,16,1024]{2,1,0:T(8,128)(2,1)}, u32[]{:S(2)}, u32[]{:S(2)}) collective-permute-start(bf16[32,16,1024]{2,1,0:T(8,128)(2,1)S(1)} %all-to-all-done.refs_0_), channel_id=1, source_target_pairs={{0,3},{1,0},{2,1},{3,2},{4,7},{5,4},{6,5},{7,6},{8,11},{9,8},{10,9... | collective-permute-start | bytes 3145736 | tf_op jit(solution)/shard_map/ppermute | solution.py:214
  56.7 21.2 %collective-permute-done.1.refs_3_ = bf16[32,16,1024]{2,1,0:T(8,128)(2,1)} collective-permute-done((bf16[32,16,1024]{2,1,0:T(8,128)(2,1)S(1)}, bf16[32,16,1024]{2,1,0:T(8,128)(2,1)}, u32[]{:S(2)}, u32[]{:S(2)}) %collective-permute-start.1) | collective-permute-done | bytes 1048608 | tf_op jit(solution)/shard_map/ppermute | solution.py:215
  78.0 1.1 slice.8
  79.0 1.9 %collective-permute-start.2 = (bf16[16,16,1024]{2,1,0:T(8,128)(2,1)S(1)}, bf16[16,16,1024]{2,1,0:T(8,128)(2,1)S(1)}, u32[]{:S(2)}, u32[]{:S(2)}) collective-permute-start(bf16[16,16,1024]{2,1,0:T(8,128)(2,1)S(1)} %slice.8), channel_id=1, source_target_pairs={{0,1},{1,2},{2,3},{3,0},{4,5},{5,6},{6,7},{7,4},{8,9},{9,10},{10,1... | collective-permute-start | bytes 1572872 | tf_op jit(solution)/shard_map/ppermute | solution.py:216
  81.0 0.0 collective-permute-done.refs_1_
  81.0 1.1 slice.9
  82.1 4.6 %collective-permute-start.3 = (bf16[16,16,1024]{2,1,0:T(8,128)(2,1)S(1)}, bf16[16,16,1024]{2,1,0:T(8,128)(2,1)S(1)}, u32[]{:S(2)}, u32[]{:S(2)}) collective-permute-start(bf16[16,16,1024]{2,1,0:T(8,128)(2,1)S(1)} %slice.9), channel_id=1, source_target_pairs={{0,3},{1,0},{2,1},{3,2},{4,7},{5,4},{6,5},{7,6},{8,11},{9,8},{10,9... | collective-permute-start | bytes 1572872 | tf_op jit(solution)/shard_map/ppermute | solution.py:217
  86.6 3.5 %collective-permute-start.4 = (bf16[32,16,1024]{2,1,0:T(8,128)(2,1)S(1)}, bf16[32,16,1024]{2,1,0:T(8,128)(2,1)}, u32[]{:S(2)}, u32[]{:S(2)}) collective-permute-start(bf16[32,16,1024]{2,1,0:T(8,128)(2,1)S(1)} %all-to-all-done.refs_0_), channel_id=1, source_target_pairs={{0,8},{8,0},{1,9},{9,1},{2,10},{10,2},{3,11},{11,3},{4,12},{12,4},... | collective-permute-start | bytes 3145736 | tf_op jit(solution)/shard_map/ppermute | solution.py:209
  90.2 1.9 %collective-permute-start.7 = (bf16[32,16,1024]{2,1,0:T(8,128)(2,1)}, bf16[32,16,1024]{2,1,0:T(8,128)(2,1)}, u32[]{:S(2)}, u32[]{:S(2)}) collective-permute-start(bf16[32,16,1024]{2,1,0:T(8,128)(2,1)} %collective-permute-done.1.refs_3_), channel_id=1, source_target_pairs={{0,8},{8,0},{1,9},{9,1},{2,10},{10,2},{3,11},{11,3},{4,12},{12,4},... | collective-permute-start | bytes 3145736 | tf_op jit(solution)/shard_map/ppermute | solution.py:209
  92.1 2.4 %collective-permute-start.5 = (bf16[32,16,1024]{2,1,0:T(8,128)(2,1)}, bf16[32,16,1024]{2,1,0:T(8,128)(2,1)}, u32[]{:S(2)}, u32[]{:S(2)}) collective-permute-start(bf16[32,16,1024]{2,1,0:T(8,128)(2,1)} %collective-permute-done.refs_1_), channel_id=1, source_target_pairs={{0,8},{8,0},{1,9},{9,1},{2,10},{10,2},{3,11},{11,3},{4,12},{12,4},... | collective-permute-start | bytes 3145736 | tf_op jit(solution)/shard_map/ppermute | solution.py:209
  94.5 0.0 collective-permute-done.2
  94.5 0.9 constant_dynamic-update-slice_fusion.1
  95.4 1.1 collective-permute-done.3
  96.5 0.8 constant_dynamic-update-slice_fusion.refs_2_
  97.4 4.1 %collective-permute-start.6 = (bf16[32,16,1024]{2,1,0:T(8,128)(2,1)}, bf16[32,16,1024]{2,1,0:T(8,128)(2,1)}, u32[]{:S(2)}, u32[]{:S(2)}) collective-permute-start(bf16[32,16,1024]{2,1,0:T(8,128)(2,1)} %constant_dynamic-update-slice_fusion.refs_2_), channel_id=1, source_target_pairs={{0,8},{8,0},{1,9},{9,1},{2,10},{10,2},{3,11},{11,3},{4,12},{12,4},... | collective-permute-start | bytes 3145736 | tf_op jit(solution)/shard_map/ppermute | solution.py:209
  101.5 0.1 pad_add_fusion.place
  101.6 0.0 collective-permute-done.4.refs_4_
  101.6 0.0 collective-permute-done.7.refs_7_
  101.6 0.0 collective-permute-done.5.refs_5_
  101.6 2.5 %collective-permute-done.6.refs_6_ = bf16[32,16,1024]{2,1,0:T(8,128)(2,1)} collective-permute-done((bf16[32,16,1024]{2,1,0:T(8,128)(2,1)}, bf16[32,16,1024]{2,1,0:T(8,128)(2,1)}, u32[]{:S(2)}, u32[]{:S(2)}) %collective-permute-start.6) | collective-permute-done | bytes 1048608 | tf_op jit(solution)/shard_map/ppermute | solution.py:209
  104.1 0.0 all-to-all-done.1
  104.1 5.4 %attention_and_weight_grad.1 = (f32[16,256,256]{2,1,0:T(8,128)}, bf16[512,1024]{1,0:T(8,128)(2,1)S(1)}, bf16[512,1024]{1,0:T(8,128)(2,1)S(1)}) custom-call(s32[2]{0:T(128)S(1)} %pad_add_fusion.place, bf16[256,4096]{1,0:T(8,128)(2,1)S(1)} %bitcast.11, bf16[256,4096]{1,0:T(8,128)(2,1)S(1)} %bitcast.12, bf16[256,4096]{1,0:T(8,128)(2,1)S(1)} %bitcast.13, ...), custom_call_target="tpu_custom_call" | custom-call | flops 2000000000 | bytes 8388608 | tf_op jit(solution)/shard_map/attention_and_weight_grad/pallas_call | solution.py:84
  109.5 2.3 %collective-permute-start.8 = (bf16[512,1024]{1,0:T(8,128)(2,1)S(1)}, bf16[512,1024]{1,0:T(8,128)(2,1)S(1)}, u32[]{:S(2)}, u32[]{:S(2)}) collective-permute-start(bf16[512,1024]{1,0:T(8,128)(2,1)S(1)} %get-tuple-element.25), channel_id=1, source_target_pairs={{0,8},{8,0},{1,9},{9,1},{2,10},{10,2},{3,11},{11,3},{4,12},{12,4},... | collective-permute-start | bytes 3145736 | tf_op jit(solution)/shard_map/ppermute | solution.py:209
  111.8 2.3 %collective-permute-done.8 = bf16[512,1024]{1,0:T(8,128)(2,1)S(1)} collective-permute-done((bf16[512,1024]{1,0:T(8,128)(2,1)S(1)}, bf16[512,1024]{1,0:T(8,128)(2,1)S(1)}, u32[]{:S(2)}, u32[]{:S(2)}) %collective-permute-start.8) | collective-permute-done | bytes 1048608 | tf_op jit(solution)/shard_map/ppermute | solution.py:209
  114.1 1.4 add_convert_fusion
  115.5 7.6 %all-to-all-start.2 = ((bf16[32,16,1024]{2,1,0:T(8,128)(2,1)}), bf16[32,16,1024]{2,1,0:T(8,128)(2,1)}, u32[]{:S(2)}, u32[]{:S(2)}) async-start(bf16[32,16,1024]{2,1,0:T(8,128)(2,1)} %bitcast.20), calls=%async_computation.2 | async-start | bytes 2097152 | tf_op jit(solution)/shard_map/all_to_all | solution.py:245
  123.1 0.0 copy-start.2
  123.1 2.2 %copy-done.2 = f32[16,256,256]{2,1,0:T(8,128)S(1)} copy-done((f32[16,256,256]{2,1,0:T(8,128)S(1)}, f32[16,256,256]{2,1,0:T(8,128)}, u32[]{:S(2)}) %copy-start.2) | copy-done | bytes 4194328
  125.3 7.2 %attention_grads.1 = bf16[3,1024,256]{2,1,0:T(8,128)(2,1)} custom-call(s32[2]{0:T(128)S(1)} %pad_add_fusion.place, f32[16,256,256]{2,1,0:T(8,128)S(1)} %copy-done.2, bf16[256,4096]{1,0:T(8,128)(2,1)S(1)} %bitcast.15, bf16[256,4096]{1,0:T(8,128)(2,1)S(1)} %bitcast.16, bf16[256,4096]{1,0:T(8,128)(2,1)S(1)} %bitcast.17, bf16[256,4096]{1,0:T(8,128)(2,1)S(1)} %bitcast.18, ...), custom_call_target="tpu_custom_call" | custom-call | flops 3000000000 | bytes 10485760 | tf_op jit(solution)/shard_map/attention_grads/pallas_call | solution.py:141
  132.5 0.0 copy-start.1
  132.5 1.4 copy-done.1
  133.9 6.2 %input_projection.1 = bf16[256,1024]{1,0:T(8,128)(2,1)} custom-call(s32[2]{0:T(128)S(1)} %pad_add_fusion.place, bf16[3072,256]{1,0:T(8,128)(2,1)S(1)} %bitcast.19, bf16[32,16,1024]{2,1,0:T(8,128)(2,1)S(1)} %all-to-all-done.refs_0_, bf16[32,16,1024]{2,1,0:T(8,128)(2,1)} %collective-permute-done.refs_1_, ...), custom_call_target="tpu_custom_call" | custom-call | flops 2000000000 | bytes 8388608 | tf_op jit(solution)/shard_map/input_projection/pallas_call | solution.py:178
  140.1 10.0 %all-to-all-done.2 = bf16[32,16,1024]{2,1,0:T(8,128)(2,1)} async-done(((bf16[32,16,1024]{2,1,0:T(8,128)(2,1)}), bf16[32,16,1024]{2,1,0:T(8,128)(2,1)}, u32[]{:S(2)}, u32[]{:S(2)}) %all-to-all-start.2) | async-done | bytes 1048608 | tf_op jit(solution)/shard_map/all_to_all | solution.py:245
  150.1 7.0 %all-to-all-start.3 = ((bf16[32,8,1024]{2,1,0:T(8,128)(2,1)}), bf16[32,8,1024]{2,1,0:T(8,128)(2,1)S(1)}, u32[]{:S(2)}, u32[]{:S(2)}) async-start(bf16[32,8,1024]{2,1,0:T(8,128)(2,1)} %bitcast.8), calls=%async_computation.3 | async-start | bytes 1048576 | tf_op jit(solution)/shard_map/all_to_all | solution.py:249
  157.2 1.4 convert_reduce_fusion
  158.6 2.6 %collective-permute-start.9 = (f32[16,1024]{1,0:T(8,128)S(1)}, f32[16,1024]{1,0:T(8,128)S(1)}, u32[]{:S(2)}, u32[]{:S(2)}) collective-permute-start(f32[16,1024]{1,0:T(8,128)S(1)} %broadcast_multiply_fusion), channel_id=1, source_target_pairs={{0,1},{1,0},{2,3},{3,2},{4,5},{5,4},{6,7},{7,6},{8,9},{9,8},{10,11... | collective-permute-start | bytes 196616 | tf_op jit(solution)/shard_map/ppermute | solution.py:228
  161.2 2.7 %collective-permute-done.9 = f32[16,1024]{1,0:T(8,128)S(1)} collective-permute-done((f32[16,1024]{1,0:T(8,128)S(1)}, f32[16,1024]{1,0:T(8,128)S(1)}, u32[]{:S(2)}, u32[]{:S(2)}) %collective-permute-start.9) | collective-permute-done | bytes 65568 | tf_op jit(solution)/shard_map/ppermute | solution.py:228
  163.9 5.4 %collective-permute-start.10 = (f32[16,1024]{1,0:T(8,128)S(1)}, f32[16,1024]{1,0:T(8,128)S(1)}, u32[]{:S(2)}, u32[]{:S(2)}) collective-permute-start(f32[16,1024]{1,0:T(8,128)S(1)} %fusion), channel_id=1, source_target_pairs={{0,2},{1,3},{2,0},{3,1},{4,6},{5,7},{6,4},{7,5},{8,10},{9,11},{10,... | collective-permute-start | bytes 196616 | tf_op jit(solution)/shard_map/ppermute | solution.py:228
  169.3 1.9 %collective-permute-done.10 = f32[16,1024]{1,0:T(8,128)S(1)} collective-permute-done((f32[16,1024]{1,0:T(8,128)S(1)}, f32[16,1024]{1,0:T(8,128)S(1)}, u32[]{:S(2)}, u32[]{:S(2)}) %collective-permute-start.10) | collective-permute-done | bytes 65568 | tf_op jit(solution)/shard_map/ppermute | solution.py:228
  171.2 7.9 %collective-permute-start.11 = (f32[16,1024]{1,0:T(8,128)S(1)}, f32[16,1024]{1,0:T(8,128)S(1)}, u32[]{:S(2)}, u32[]{:S(2)}) collective-permute-start(f32[16,1024]{1,0:T(8,128)S(1)} %add.22), channel_id=1, source_target_pairs={{0,4},{4,0},{1,5},{5,1},{2,6},{6,2},{3,7},{7,3},{8,12},{12,8},{9,1... | collective-permute-start | bytes 196616 | tf_op jit(solution)/shard_map/ppermute | solution.py:229
  179.1 1.7 collective-permute-done.11
  180.9 0.6 add.23
  181.5 0.0 all-to-all-done.3
  181.5 0.8 copy.10
  (5 shorter events, 0.0 us)
Async XLA Ops:
  0.6 0.9 copy-start
  0.6 15.5 %copy-start.3 = (bf16[1,1,256,1024]{3,2,1,0:T(8,128)(2,1)S(1)}, bf16[1,1,256,1024]{3,2,1,0:T(8,128)(2,1)}, u32[]{:S(2)}) copy-start(bf16[1,1,256,1024]{3,2,1,0:T(8,128)(2,1)} %param.9) | copy-start | bytes 1572868
  0.7 15.5 %copy-start.4 = (bf16[1,1,256,1024]{3,2,1,0:T(8,128)(2,1)S(1)}, bf16[1,1,256,1024]{3,2,1,0:T(8,128)(2,1)}, u32[]{:S(2)}) copy-start(bf16[1,1,256,1024]{3,2,1,0:T(8,128)(2,1)} %param.8) | copy-start | bytes 1572868
  0.7 15.5 %copy-start.5 = (bf16[1,1,256,1024]{3,2,1,0:T(8,128)(2,1)S(1)}, bf16[1,1,256,1024]{3,2,1,0:T(8,128)(2,1)}, u32[]{:S(2)}) copy-start(bf16[1,1,256,1024]{3,2,1,0:T(8,128)(2,1)} %param.7) | copy-start | bytes 1572868
  0.7 15.5 %copy-start.6 = (bf16[1,1,256,1024]{3,2,1,0:T(8,128)(2,1)S(1)}, bf16[1,1,256,1024]{3,2,1,0:T(8,128)(2,1)}, u32[]{:S(2)}) copy-start(bf16[1,1,256,1024]{3,2,1,0:T(8,128)(2,1)} %param.6) | copy-start | bytes 1572868
  2.7 40.1 %all-to-all-start = ((bf16[32,16,1024]{2,1,0:T(8,128)(2,1)}), bf16[32,16,1024]{2,1,0:T(8,128)(2,1)S(1)}, u32[]{:S(2)}, u32[]{:S(2)}) async-start(bf16[32,16,1024]{2,1,0:T(8,128)(2,1)} %broadcast_in_dim.2), calls=%async_computation | async-start | bytes 2097152 | tf_op jit(solution)/shard_map/all_to_all | solution.py:205
  42.8 61.3 %all-to-all-start.1 = ((bf16[32,8,4096]{2,1,0:T(8,128)(2,1)}), bf16[32,8,4096]{2,1,0:T(8,128)(2,1)S(1)}, u32[]{:S(2)}, u32[]{:S(2)}) async-start(bf16[32,8,4096]{2,1,0:T(8,128)(2,1)} %pad_maximum_fusion), calls=%async_computation.1 | async-start | bytes 4194304 | tf_op jit(solution)/shard_map/all_to_all | solution.py:241
  50.2 27.7 %collective-permute-start.1 = (bf16[32,16,1024]{2,1,0:T(8,128)(2,1)S(1)}, bf16[32,16,1024]{2,1,0:T(8,128)(2,1)}, u32[]{:S(2)}, u32[]{:S(2)}) collective-permute-start(bf16[32,16,1024]{2,1,0:T(8,128)(2,1)S(1)} %all-to-all-done.refs_0_), channel_id=1, source_target_pairs={{0,1},{1,2},{2,3},{3,0},{4,5},{5,6},{6,7},{7,4},{8,9},{9,10},{10,1... | collective-permute-start | bytes 3145736 | tf_op jit(solution)/shard_map/ppermute | solution.py:215
  53.4 27.6 %collective-permute-start = (bf16[32,16,1024]{2,1,0:T(8,128)(2,1)S(1)}, bf16[32,16,1024]{2,1,0:T(8,128)(2,1)}, u32[]{:S(2)}, u32[]{:S(2)}) collective-permute-start(bf16[32,16,1024]{2,1,0:T(8,128)(2,1)S(1)} %all-to-all-done.refs_0_), channel_id=1, source_target_pairs={{0,3},{1,0},{2,1},{3,2},{4,7},{5,4},{6,5},{7,6},{8,11},{9,8},{10,9... | collective-permute-start | bytes 3145736 | tf_op jit(solution)/shard_map/ppermute | solution.py:214
  79.0 15.5 %collective-permute-start.2 = (bf16[16,16,1024]{2,1,0:T(8,128)(2,1)S(1)}, bf16[16,16,1024]{2,1,0:T(8,128)(2,1)S(1)}, u32[]{:S(2)}, u32[]{:S(2)}) collective-permute-start(bf16[16,16,1024]{2,1,0:T(8,128)(2,1)S(1)} %slice.8), channel_id=1, source_target_pairs={{0,1},{1,2},{2,3},{3,0},{4,5},{5,6},{6,7},{7,4},{8,9},{9,10},{10,1... | collective-permute-start | bytes 1572872 | tf_op jit(solution)/shard_map/ppermute | solution.py:216
  82.1 14.4 %collective-permute-start.3 = (bf16[16,16,1024]{2,1,0:T(8,128)(2,1)S(1)}, bf16[16,16,1024]{2,1,0:T(8,128)(2,1)S(1)}, u32[]{:S(2)}, u32[]{:S(2)}) collective-permute-start(bf16[16,16,1024]{2,1,0:T(8,128)(2,1)S(1)} %slice.9), channel_id=1, source_target_pairs={{0,3},{1,0},{2,1},{3,2},{4,7},{5,4},{6,5},{7,6},{8,11},{9,8},{10,9... | collective-permute-start | bytes 1572872 | tf_op jit(solution)/shard_map/ppermute | solution.py:217
  86.6 14.9 %collective-permute-start.4 = (bf16[32,16,1024]{2,1,0:T(8,128)(2,1)S(1)}, bf16[32,16,1024]{2,1,0:T(8,128)(2,1)}, u32[]{:S(2)}, u32[]{:S(2)}) collective-permute-start(bf16[32,16,1024]{2,1,0:T(8,128)(2,1)S(1)} %all-to-all-done.refs_0_), channel_id=1, source_target_pairs={{0,8},{8,0},{1,9},{9,1},{2,10},{10,2},{3,11},{11,3},{4,12},{12,4},... | collective-permute-start | bytes 3145736 | tf_op jit(solution)/shard_map/ppermute | solution.py:209
  90.2 11.4 %collective-permute-start.7 = (bf16[32,16,1024]{2,1,0:T(8,128)(2,1)}, bf16[32,16,1024]{2,1,0:T(8,128)(2,1)}, u32[]{:S(2)}, u32[]{:S(2)}) collective-permute-start(bf16[32,16,1024]{2,1,0:T(8,128)(2,1)} %collective-permute-done.1.refs_3_), channel_id=1, source_target_pairs={{0,8},{8,0},{1,9},{9,1},{2,10},{10,2},{3,11},{11,3},{4,12},{12,4},... | collective-permute-start | bytes 3145736 | tf_op jit(solution)/shard_map/ppermute | solution.py:209
  92.1 9.5 %collective-permute-start.5 = (bf16[32,16,1024]{2,1,0:T(8,128)(2,1)}, bf16[32,16,1024]{2,1,0:T(8,128)(2,1)}, u32[]{:S(2)}, u32[]{:S(2)}) collective-permute-start(bf16[32,16,1024]{2,1,0:T(8,128)(2,1)} %collective-permute-done.refs_1_), channel_id=1, source_target_pairs={{0,8},{8,0},{1,9},{9,1},{2,10},{10,2},{3,11},{11,3},{4,12},{12,4},... | collective-permute-start | bytes 3145736 | tf_op jit(solution)/shard_map/ppermute | solution.py:209
  97.4 6.8 %collective-permute-start.6 = (bf16[32,16,1024]{2,1,0:T(8,128)(2,1)}, bf16[32,16,1024]{2,1,0:T(8,128)(2,1)}, u32[]{:S(2)}, u32[]{:S(2)}) collective-permute-start(bf16[32,16,1024]{2,1,0:T(8,128)(2,1)} %constant_dynamic-update-slice_fusion.refs_2_), channel_id=1, source_target_pairs={{0,8},{8,0},{1,9},{9,1},{2,10},{10,2},{3,11},{11,3},{4,12},{12,4},... | collective-permute-start | bytes 3145736 | tf_op jit(solution)/shard_map/ppermute | solution.py:209
  109.5 4.5 %collective-permute-start.8 = (bf16[512,1024]{1,0:T(8,128)(2,1)S(1)}, bf16[512,1024]{1,0:T(8,128)(2,1)S(1)}, u32[]{:S(2)}, u32[]{:S(2)}) collective-permute-start(bf16[512,1024]{1,0:T(8,128)(2,1)S(1)} %get-tuple-element.25), channel_id=1, source_target_pairs={{0,8},{8,0},{1,9},{9,1},{2,10},{10,2},{3,11},{11,3},{4,12},{12,4},... | collective-permute-start | bytes 3145736 | tf_op jit(solution)/shard_map/ppermute | solution.py:209
  115.5 34.6 %all-to-all-start.2 = ((bf16[32,16,1024]{2,1,0:T(8,128)(2,1)}), bf16[32,16,1024]{2,1,0:T(8,128)(2,1)}, u32[]{:S(2)}, u32[]{:S(2)}) async-start(bf16[32,16,1024]{2,1,0:T(8,128)(2,1)} %bitcast.20), calls=%async_computation.2 | async-start | bytes 2097152 | tf_op jit(solution)/shard_map/all_to_all | solution.py:245
  123.1 2.2 %copy-start.2 = (f32[16,256,256]{2,1,0:T(8,128)S(1)}, f32[16,256,256]{2,1,0:T(8,128)}, u32[]{:S(2)}) copy-start(f32[16,256,256]{2,1,0:T(8,128)} %get-tuple-element.26.attention_ref) | copy-start | bytes 12582916
  132.5 1.4 copy-start.1
  150.1 31.4 %all-to-all-start.3 = ((bf16[32,8,1024]{2,1,0:T(8,128)(2,1)}), bf16[32,8,1024]{2,1,0:T(8,128)(2,1)S(1)}, u32[]{:S(2)}, u32[]{:S(2)}) async-start(bf16[32,8,1024]{2,1,0:T(8,128)(2,1)} %bitcast.8), calls=%async_computation.3 | async-start | bytes 1048576 | tf_op jit(solution)/shard_map/all_to_all | solution.py:249
  158.6 5.4 %collective-permute-start.9 = (f32[16,1024]{1,0:T(8,128)S(1)}, f32[16,1024]{1,0:T(8,128)S(1)}, u32[]{:S(2)}, u32[]{:S(2)}) collective-permute-start(f32[16,1024]{1,0:T(8,128)S(1)} %broadcast_multiply_fusion), channel_id=1, source_target_pairs={{0,1},{1,0},{2,3},{3,2},{4,5},{5,4},{6,7},{7,6},{8,9},{9,8},{10,11... | collective-permute-start | bytes 196616 | tf_op jit(solution)/shard_map/ppermute | solution.py:228
  163.9 7.2 %collective-permute-start.10 = (f32[16,1024]{1,0:T(8,128)S(1)}, f32[16,1024]{1,0:T(8,128)S(1)}, u32[]{:S(2)}, u32[]{:S(2)}) collective-permute-start(f32[16,1024]{1,0:T(8,128)S(1)} %fusion), channel_id=1, source_target_pairs={{0,2},{1,3},{2,0},{3,1},{4,6},{5,7},{6,4},{7,5},{8,10},{9,11},{10,... | collective-permute-start | bytes 196616 | tf_op jit(solution)/shard_map/ppermute | solution.py:228
  171.2 9.7 %collective-permute-start.11 = (f32[16,1024]{1,0:T(8,128)S(1)}, f32[16,1024]{1,0:T(8,128)S(1)}, u32[]{:S(2)}, u32[]{:S(2)}) collective-permute-start(f32[16,1024]{1,0:T(8,128)S(1)} %add.22), channel_id=1, source_target_pairs={{0,4},{4,0},{1,5},{5,1},{2,6},{6,2},{3,7},{7,3},{8,12},{12,8},{9,1... | collective-permute-start | bytes 196616 | tf_op jit(solution)/shard_map/ppermute | solution.py:229

commit v4 on v3

--- a/solution.py
+++ b/solution.py
@@ -193,7 +193,7 @@
     )(place, grads.reshape(3 * D, ROWS), *pieces)
 
 
-def gather_plane(input_weights, output_weight):
+def own_columns(input_weights, output_weight):
     x_at = lax.axis_index("x")
     mine = jnp.concatenate(
         [
@@ -202,7 +202,7 @@
         ],
         axis=1,
     )
-    return lax.all_to_all(jnp.broadcast_to(mine[None], (32, 16, D)), PLANE_AXES, 0, 0, tiled=True)
+    return jnp.broadcast_to(mine[None], (32, 16, D))
 
 
 def swap_cores(block):
@@ -215,8 +215,7 @@
     before = lax.ppermute(plane, "x", ring(4, 1))
     far_a = lax.ppermute(before[:half], "x", ring(4, 1))
     far_b = lax.ppermute(after[half:], "x", ring(4, -1))
-    own = [plane, after, jnp.concatenate([far_a, far_b], axis=0), before]
-    return own + [swap_cores(piece) for piece in own]
+    return [plane, after, far_a, far_b, before]
 
 
 def sum_cores(keep, send):
@@ -232,17 +231,32 @@
 def on_device(query_rows, key_rows, value_rows, upstream, input_weights, output_weight):
     factor = 1.0 / (8 * math.sqrt(16384))
     place = jnp.stack([lax.axis_index(a) for a in ("x", "c")]).astype(jnp.int32)
-    plane = gather_plane(input_weights, output_weight)
+    columns = own_columns(input_weights, output_weight)
+    columns, query_rows, key_rows, value_rows, upstream = lax.optimization_barrier(
+        (columns, query_rows, key_rows, value_rows, upstream)
+    )
+    plane = lax.all_to_all(columns, PLANE_AXES, 0, 0, tiled=True)
+    core = lax.axis_index("c")
+
+    def both_frames(rows):
+        rows = rows.reshape(CLIP_LEN // 2, 2, PATCH_BLOCK, D)
+        mine = lax.dynamic_index_in_dim(rows, core, 1, keepdims=False)
+        other = swap_cores(lax.dynamic_index_in_dim(rows, 1 - core, 1, keepdims=False))
+        return jnp.stack(
+            [jnp.where(core == 0, mine, other), jnp.where(core == 0, other, mine)], axis=1
+        )
+
     sent = jnp.concatenate(
-        [a.reshape(CLIP_LEN, PATCH_BLOCK, D) for a in (query_rows, key_rows, value_rows, upstream)],
-        axis=2,
+        [both_frames(a) for a in (query_rows, key_rows, value_rows, upstream)], axis=3
     )
     sent, plane = lax.optimization_barrier((sent, plane))
-    moved = lax.all_to_all(sent, CLIP_AXES, 0, 0, tiled=True).reshape(ROWS, 4 * D)
-    moved, pieces = lax.optimization_barrier((moved, spread_x(plane)))
+    moved = lax.all_to_all(sent, ("yl", "zl"), 0, 0, tiled=True).reshape(ROWS, 4 * D)
+    moved, own = lax.optimization_barrier((moved, spread_x(plane)))
     attention, keep, send = forward_call(place, moved)
-    attention, share = lax.optimization_barrier((attention, sum_cores(keep, send)))
+    attention, share, own = lax.optimization_barrier((attention, sum_cores(keep, send), own))
     share = lax.all_to_all(share.reshape(32, 16, D), PLANE_AXES, 0, 0, tiled=True)
+    own = [own[0], own[1], jnp.concatenate(own[2:4], axis=0), own[4]]
+    pieces = own + [swap_cores(piece) for piece in own]
     grads = backward_call(place, attention, moved, pieces)
     result = projection_call(place, grads, pieces).reshape(CLIP_LEN, PATCH_BLOCK, D)
     result, share = lax.optimization_barrier((result, share))

time: 186 us -> 183 us (0.984)
  waiting for transfers between devices: 68.5 us -> 53.4 us
  starting transfers between devices: 78.7 us -> 89.5 us
  other arithmetic: 5.05 us -> 8.2 us
  Pallas kernels: 18.8 us -> 15.8 us
  local copies, waits for them, and re-layouts: 10.3 us -> 12.5 us
    all_to_all x1, waiting for transfers between devices: 9.97 us -> 0.01 us  [on_device(): lax.all_to_all(share.reshape(32, 16, D), PLANE_AXES, 0, 0, tiled=True)]
    all_to_all x2, waiting for transfers between devices: 25.1 us -> 15.9 us  [the longest x1 9.89 us: on_device(): plane = lax.all_to_all(columns, PLANE_AXES, 0, 0, tiled=True)]
    ppermute x5 -> x9, starting transfers between devices: 14.2 us -> 21.9 us  [swap_cores(): return lax.ppermute(block, 'c', ring(2, 1))]
    ppermute x1, waiting for transfers between devices: 0.01 us -> 6.98 us  [spread_x(): far_a = lax.ppermute(before[:half], 'x', ring(4, 1))]
    all_to_all x1, starting transfers between devices: 7.64 us -> 12.1 us  [on_device(): lax.all_to_all(share.reshape(32, 16, D), PLANE_AXES, 0, 0, tiled=True)]
    another operation x0 -> x6, other arithmetic: none -> 3.13 us  [both_frames(): jnp.stack([jnp.where(core == 0, mine, other), jnp.where(core == 0, other,...]
    squeeze x0 -> x4, local copies, waits for them, and re-layouts: none -> 2.92 us  [both_frames(): lax.dynamic_index_in_dim(rows, 1 - core, 1, keepdims=False)]
    pallas_call x1, Pallas kernels: 6.21 us -> 3.83 us  [projection_call(): pl.pallas_call(projection_kernel, grid_spec=pltpu.PrefetchScalarGridSpec(...]
  transfers between devices with their start and end apart: 16 -> 20, of which waited for: 9 -> 11; matrix products, arithmetic and copies ran while one was open for 4% -> 7% of each run, Pallas kernels for 7% -> 6%
where the time goes in v4:
time: 183 us; the launch traced here: 180 us
  starting transfers between devices  89.5 us (49%)
  waiting for transfers between devices  53.4 us (29%)
  Pallas kernels  15.8 us (9%)
  local copies, waits for them, and re-layouts  12.5 us (7%)
  other arithmetic  8.2 us (4%)
    ppermute x9, starting transfers between devices, swap_cores(): return lax.ppermute(block, 'c', ring(2, 1))  21.9 us
    ppermute x1, waiting for transfers between devices, spread_x(): before = lax.ppermute(plane, 'x', ring(4, 1))  19.3 us
    all_to_all x1, starting transfers between devices, on_device(): plane = lax.all_to_all(columns, PLANE_AXES, 0, 0, tiled=True)  13.6 us
    all_to_all x1, starting transfers between devices, on_device(): lax.all_to_all(share.reshape(32, 16, D), PLANE_AXES, 0, 0, tiled=True)  12.1 us
    all_to_all x1, waiting for transfers between devices, on_device(): plane = lax.all_to_all(columns, PLANE_AXES, 0, 0, tiled=True)  9.89 us
    ppermute x1, starting transfers between devices, sum_groups(): return share + lax.ppermute(share, 'zh', ring(2, 1))  7.94 us
    all_to_all x1, starting transfers between devices, on_device(): input_gradient = lax.all_to_all(result, CLIP_AXES, 0, 0, tiled=True)  7.8 us
    ppermute x2, starting transfers between devices, sum_groups(): share = share + lax.ppermute(share, 'x', [(i, i ^ bit) for i in range(4)])  7.75 us
  transfers between devices with their start and end apart: 20, of which 11 were waited for; matrix products, arithmetic and copies ran while one was open for 7% of the time, Pallas kernels for 6%

profile of v4, /device:TPU:1, one launch (start us, length us, event | category | flops | bytes accessed | tf_op | source)
XLA Modules:
  0.0 180.5 jit_solution(14314325087251065785)
XLA Ops:
  0.6 0.0 copy-start
  0.7 0.8 constant_dynamic-slice_fusion
  1.5 0.1 copy-done
  1.5 1.1 broadcast_in_dim.2
  2.7 13.6 %all-to-all-start = ((bf16[32,16,1024]{2,1,0:T(8,128)(2,1)}), bf16[32,16,1024]{2,1,0:T(8,128)(2,1)S(1)}, u32[]{:S(2)}, u32[]{:S(2)}) async-start(bf16[32,16,1024]{2,1,0:T(8,128)(2,1)} %broadcast_in_dim.2), calls=%async_computation | async-start | bytes 2097152 | tf_op jit(solution)/shard_map/all_to_all | solution.py:238
  16.3 0.7 dynamic-slice_bitcast_fusion.1
  17.0 2.9 %collective-permute-start.2 = (bf16[16,8,1024]{2,1,0:T(8,128)(2,1)}, bf16[16,8,1024]{2,1,0:T(8,128)(2,1)}, u32[]{:S(2)}, u32[]{:S(2)}) collective-permute-start(bf16[16,8,1024]{2,1,0:T(8,128)(2,1)} %dynamic-slice_bitcast_fusion.1), channel_id=1, source_target_pairs={{0,8},{8,0},{1,9},{9,1},{2,10},{10,2},{3,11},{11,3},{4,12},{12,4},... | collective-permute-start | bytes 786440 | tf_op jit(solution)/shard_map/ppermute | solution.py:209
  19.9 0.7 dynamic-slice_bitcast_fusion
  20.6 1.9 %collective-permute-start.3 = (bf16[16,8,1024]{2,1,0:T(8,128)(2,1)}, bf16[16,8,1024]{2,1,0:T(8,128)(2,1)S(1)}, u32[]{:S(2)}, u32[]{:S(2)}) collective-permute-start(bf16[16,8,1024]{2,1,0:T(8,128)(2,1)} %dynamic-slice_bitcast_fusion), channel_id=1, source_target_pairs={{0,8},{8,0},{1,9},{9,1},{2,10},{10,2},{3,11},{11,3},{4,12},{12,4},... | collective-permute-start | bytes 786440 | tf_op jit(solution)/shard_map/ppermute | solution.py:209
  22.5 0.7 dynamic-slice_bitcast_fusion.2
  23.3 2.4 %collective-permute-start.1 = (bf16[16,8,1024]{2,1,0:T(8,128)(2,1)}, bf16[16,8,1024]{2,1,0:T(8,128)(2,1)}, u32[]{:S(2)}, u32[]{:S(2)}) collective-permute-start(bf16[16,8,1024]{2,1,0:T(8,128)(2,1)} %dynamic-slice_bitcast_fusion.2), channel_id=1, source_target_pairs={{0,8},{8,0},{1,9},{9,1},{2,10},{10,2},{3,11},{11,3},{4,12},{12,4},... | collective-permute-start | bytes 786440 | tf_op jit(solution)/shard_map/ppermute | solution.py:209
  25.7 0.7 dynamic-slice_bitcast_fusion.3
  26.4 1.9 %collective-permute-start = (bf16[16,8,1024]{2,1,0:T(8,128)(2,1)}, bf16[16,8,1024]{2,1,0:T(8,128)(2,1)}, u32[]{:S(2)}, u32[]{:S(2)}) collective-permute-start(bf16[16,8,1024]{2,1,0:T(8,128)(2,1)} %dynamic-slice_bitcast_fusion.3), channel_id=1, source_target_pairs={{0,8},{8,0},{1,9},{9,1},{2,10},{10,2},{3,11},{11,3},{4,12},{12,4},... | collective-permute-start | bytes 786440 | tf_op jit(solution)/shard_map/ppermute | solution.py:209
  28.3 0.0 collective-permute-done.2
  28.3 1.0 fusion.2
  29.3 0.0 collective-permute-done.1
  29.4 1.0 fusion.4
  30.3 0.1 pad_maximum_fusion.2
  30.4 0.1 pad_maximum_fusion.1
  30.5 0.0 collective-permute-done.3
  30.5 1.0 fusion.6
  31.5 1.5 maximum_maximum_fusion
  33.0 9.9 %all-to-all-done.refs_0_ = bf16[32,16,1024]{2,1,0:T(8,128)(2,1)S(1)} async-done(((bf16[32,16,1024]{2,1,0:T(8,128)(2,1)}), bf16[32,16,1024]{2,1,0:T(8,128)(2,1)S(1)}, u32[]{:S(2)}, u32[]{:S(2)}) %all-to-all-start) | async-done | bytes 1048608 | tf_op jit(solution)/shard_map/all_to_all | solution.py:238
  42.9 5.4 %all-to-all-start.1 = ((bf16[16,2,8,4096]{3,2,1,0:T(8,128)(2,1)}), bf16[16,2,8,4096]{3,2,1,0:T(8,128)(2,1)S(1)}, u32[]{:S(2)}, u32[]{:S(2)}) async-start(bf16[16,2,8,4096]{3,2,1,0:T(8,128)(2,1)} %maximum_maximum_fusion), calls=%async_computation.1 | async-start | bytes 4194304 | tf_op jit(solution)/shard_map/all_to_all | solution.py:253
  48.3 3.1 %collective-permute-start.5 = (bf16[32,16,1024]{2,1,0:T(8,128)(2,1)S(1)}, bf16[32,16,1024]{2,1,0:T(8,128)(2,1)S(1)}, u32[]{:S(2)}, u32[]{:S(2)}) collective-permute-start(bf16[32,16,1024]{2,1,0:T(8,128)(2,1)S(1)} %all-to-all-done.refs_0_), channel_id=1, source_target_pairs={{0,1},{1,2},{2,3},{3,0},{4,5},{5,6},{6,7},{7,4},{8,9},{9,10},{10,1... | collective-permute-start | bytes 3145736 | tf_op jit(solution)/shard_map/ppermute | solution.py:215
  51.5 3.4 %collective-permute-start.4 = (bf16[32,16,1024]{2,1,0:T(8,128)(2,1)S(1)}, bf16[32,16,1024]{2,1,0:T(8,128)(2,1)S(1)}, u32[]{:S(2)}, u32[]{:S(2)}) collective-permute-start(bf16[32,16,1024]{2,1,0:T(8,128)(2,1)S(1)} %all-to-all-done.refs_0_), channel_id=1, source_target_pairs={{0,3},{1,0},{2,1},{3,2},{4,7},{5,4},{6,5},{7,6},{8,11},{9,8},{10,9... | collective-permute-start | bytes 3145736 | tf_op jit(solution)/shard_map/ppermute | solution.py:214
  54.8 19.3 %collective-permute-done.5.refs_3_ = bf16[32,16,1024]{2,1,0:T(8,128)(2,1)S(1)} collective-permute-done((bf16[32,16,1024]{2,1,0:T(8,128)(2,1)S(1)}, bf16[32,16,1024]{2,1,0:T(8,128)(2,1)S(1)}, u32[]{:S(2)}, u32[]{:S(2)}) %collective-permute-start.5) | collective-permute-done | bytes 1048608 | tf_op jit(solution)/shard_map/ppermute | solution.py:215
  74.2 1.9 %collective-permute-start.6 = (bf16[16,16,1024]{2,1,0:T(8,128)(2,1)S(1)}, bf16[16,16,1024]{2,1,0:T(8,128)(2,1)S(1)}, u32[]{:S(2)}, u32[]{:S(2)}) collective-permute-start(bf16[16,16,1024]{2,1,0:T(8,128)(2,1)S(1)} %slice.8), channel_id=1, source_target_pairs={{0,1},{1,2},{2,3},{3,0},{4,5},{5,6},{6,7},{7,4},{8,9},{9,10},{10,1... | collective-permute-start | bytes 1572872 | tf_op jit(solution)/shard_map/ppermute | solution.py:216
  76.1 0.0 collective-permute-done.4.refs_1_
  76.2 4.6 %collective-permute-start.7 = (bf16[16,16,1024]{2,1,0:T(8,128)(2,1)S(1)}, bf16[16,16,1024]{2,1,0:T(8,128)(2,1)}, u32[]{:S(2)}, u32[]{:S(2)}) collective-permute-start(bf16[16,16,1024]{2,1,0:T(8,128)(2,1)S(1)} %slice.9), channel_id=1, source_target_pairs={{0,3},{1,0},{2,1},{3,2},{4,7},{5,4},{6,5},{7,6},{8,11},{9,8},{10,9... | collective-permute-start | bytes 1572872 | tf_op jit(solution)/shard_map/ppermute | solution.py:217
  80.8 0.1 pad_add_fusion.place
  80.8 7.0 %collective-permute-done.6 = bf16[16,16,1024]{2,1,0:T(8,128)(2,1)S(1)} collective-permute-done((bf16[16,16,1024]{2,1,0:T(8,128)(2,1)S(1)}, bf16[16,16,1024]{2,1,0:T(8,128)(2,1)S(1)}, u32[]{:S(2)}, u32[]{:S(2)}) %collective-permute-start.6) | collective-permute-done | bytes 524320 | tf_op jit(solution)/shard_map/ppermute | solution.py:216
  87.8 0.8 copy-done.11
  88.6 0.2 collective-permute-done.7
  88.8 6.1 %all-to-all-done.1 = bf16[16,2,8,4096]{3,2,1,0:T(8,128)(2,1)S(1)} async-done(((bf16[16,2,8,4096]{3,2,1,0:T(8,128)(2,1)}), bf16[16,2,8,4096]{3,2,1,0:T(8,128)(2,1)S(1)}, u32[]{:S(2)}, u32[]{:S(2)}) %all-to-all-start.1) | async-done | bytes 2097184 | tf_op jit(solution)/shard_map/all_to_all | solution.py:253
  94.9 5.4 %attention_and_weight_grad.1 = (f32[16,256,256]{2,1,0:T(8,128)}, bf16[512,1024]{1,0:T(8,128)(2,1)S(1)}, bf16[512,1024]{1,0:T(8,128)(2,1)S(1)}) custom-call(s32[2]{0:T(128)S(1)} %pad_add_fusion.place, bf16[256,4096]{1,0:T(8,128)(2,1)S(1)} %bitcast.65, bf16[256,4096]{1,0:T(8,128)(2,1)S(1)} %bitcast.66, bf16[256,4096]{1,0:T(8,128)(2,1)S(1)} %bitcast.67, ...), custom_call_target="tpu_custom_call" | custom-call | flops 2000000000 | bytes 8388608 | tf_op jit(solution)/shard_map/attention_and_weight_grad/pallas_call | solution.py:84
  100.3 4.0 %collective-permute-start.8 = (bf16[512,1024]{1,0:T(8,128)(2,1)S(1)}, bf16[512,1024]{1,0:T(8,128)(2,1)S(1)}, u32[]{:S(2)}, u32[]{:S(2)}) collective-permute-start(bf16[512,1024]{1,0:T(8,128)(2,1)S(1)} %get-tuple-element.37), channel_id=1, source_target_pairs={{0,8},{8,0},{1,9},{9,1},{2,10},{10,2},{3,11},{11,3},{4,12},{12,4},... | collective-permute-start | bytes 3145736 | tf_op jit(solution)/shard_map/ppermute | solution.py:209
  104.3 2.3 %collective-permute-done.8 = bf16[512,1024]{1,0:T(8,128)(2,1)S(1)} collective-permute-done((bf16[512,1024]{1,0:T(8,128)(2,1)S(1)}, bf16[512,1024]{1,0:T(8,128)(2,1)S(1)}, u32[]{:S(2)}, u32[]{:S(2)}) %collective-permute-start.8) | collective-permute-done | bytes 1048608 | tf_op jit(solution)/shard_map/ppermute | solution.py:209
  106.6 1.5 add_convert_fusion
  108.1 12.1 %all-to-all-start.2 = ((bf16[32,16,1024]{2,1,0:T(8,128)(2,1)}), bf16[32,16,1024]{2,1,0:T(8,128)(2,1)}, u32[]{:S(2)}, u32[]{:S(2)}) async-start(bf16[32,16,1024]{2,1,0:T(8,128)(2,1)} %bitcast.74), calls=%async_computation.2 | async-start | bytes 2097152 | tf_op jit(solution)/shard_map/all_to_all | solution.py:257
  120.2 1.2 constant_dynamic-update-slice_fusion.1
  121.4 1.1 constant_dynamic-update-slice_fusion.refs_2_
  122.5 2.6 %collective-permute-start.11 = (bf16[32,16,1024]{2,1,0:T(8,128)(2,1)S(1)}, bf16[32,16,1024]{2,1,0:T(8,128)(2,1)S(1)}, u32[]{:S(2)}, u32[]{:S(2)}) collective-permute-start(bf16[32,16,1024]{2,1,0:T(8,128)(2,1)S(1)} %constant_dynamic-update-slice_fusion.refs_2_), channel_id=1, source_target_pairs={{0,8},{8,0},{1,9},{9,1},{2,10},{10,2},{3,11},{11,3},{4,12},{12,4},... | collective-permute-start | bytes 3145736 | tf_op jit(solution)/shard_map/ppermute | solution.py:209
  125.1 1.9 %collective-permute-start.9 = (bf16[32,16,1024]{2,1,0:T(8,128)(2,1)S(1)}, bf16[32,16,1024]{2,1,0:T(8,128)(2,1)S(1)}, u32[]{:S(2)}, u32[]{:S(2)}) collective-permute-start(bf16[32,16,1024]{2,1,0:T(8,128)(2,1)S(1)} %all-to-all-done.refs_0_), channel_id=1, source_target_pairs={{0,8},{8,0},{1,9},{9,1},{2,10},{10,2},{3,11},{11,3},{4,12},{12,4},... | collective-permute-start | bytes 3145736 | tf_op jit(solution)/shard_map/ppermute | solution.py:209
  127.0 2.4 %collective-permute-start.10 = (bf16[32,16,1024]{2,1,0:T(8,128)(2,1)S(1)}, bf16[32,16,1024]{2,1,0:T(8,128)(2,1)S(1)}, u32[]{:S(2)}, u32[]{:S(2)}) collective-permute-start(bf16[32,16,1024]{2,1,0:T(8,128)(2,1)S(1)} %copy-done.4), channel_id=1, source_target_pairs={{0,8},{8,0},{1,9},{9,1},{2,10},{10,2},{3,11},{11,3},{4,12},{12,4},... | collective-permute-start | bytes 3145736 | tf_op jit(solution)/shard_map/ppermute | solution.py:209
  129.4 1.9 %collective-permute-start.12 = (bf16[32,16,1024]{2,1,0:T(8,128)(2,1)S(1)}, bf16[32,16,1024]{2,1,0:T(8,128)(2,1)S(1)}, u32[]{:S(2)}, u32[]{:S(2)}) collective-permute-start(bf16[32,16,1024]{2,1,0:T(8,128)(2,1)S(1)} %copy-done.2), channel_id=1, source_target_pairs={{0,8},{8,0},{1,9},{9,1},{2,10},{10,2},{3,11},{11,3},{4,12},{12,4},... | collective-permute-start | bytes 3145736 | tf_op jit(solution)/shard_map/ppermute | solution.py:209
  131.4 0.0 collective-permute-done.9.refs_4_
  131.4 0.3 collective-permute-done.10.refs_5_
  131.7 2.3 %collective-permute-done.12.refs_7_ = bf16[32,16,1024]{2,1,0:T(8,128)(2,1)S(1)} collective-permute-done((bf16[32,16,1024]{2,1,0:T(8,128)(2,1)S(1)}, bf16[32,16,1024]{2,1,0:T(8,128)(2,1)S(1)}, u32[]{:S(2)}, u32[]{:S(2)}) %collective-permute-start.12) | collective-permute-done | bytes 1048608 | tf_op jit(solution)/shard_map/ppermute | solution.py:209
  134.0 2.2 %copy-done.6 = f32[16,256,256]{2,1,0:T(8,128)S(1)} copy-done((f32[16,256,256]{2,1,0:T(8,128)S(1)}, f32[16,256,256]{2,1,0:T(8,128)}, u32[]{:S(2)}) %copy-start.6) | copy-done | bytes 4194328
  136.2 6.5 %attention_grads.1 = bf16[3,1024,256]{2,1,0:T(8,128)(2,1)} custom-call(s32[2]{0:T(128)S(1)} %pad_add_fusion.place, f32[16,256,256]{2,1,0:T(8,128)S(1)} %copy-done.6, bf16[256,4096]{1,0:T(8,128)(2,1)S(1)} %bitcast.69, bf16[256,4096]{1,0:T(8,128)(2,1)S(1)} %bitcast.70, bf16[256,4096]{1,0:T(8,128)(2,1)S(1)} %bitcast.71, bf16[256,4096]{1,0:T(8,128)(2,1)S(1)} %bitcast.72, ...), custom_call_target="tpu_custom_call" | custom-call | flops 3000000000 | bytes 10485760 | tf_op jit(solution)/shard_map/attention_grads/pallas_call | solution.py:141
  142.7 1.4 copy-done.5
  144.1 3.8 %input_projection.1 = bf16[256,1024]{1,0:T(8,128)(2,1)} custom-call(s32[2]{0:T(128)S(1)} %pad_add_fusion.place, bf16[3072,256]{1,0:T(8,128)(2,1)S(1)} %bitcast.73, bf16[32,16,1024]{2,1,0:T(8,128)(2,1)S(1)} %all-to-all-done.refs_0_, bf16[32,16,1024]{2,1,0:T(8,128)(2,1)S(1)} %copy-done.4, bf16[32,16,1024]{2,1,0:T(8,128)(2,1)S(1)} %constant_dynamic-update-slice_fusion.refs_2_, ...), custom_call_target="tpu_custom_call" | custom-call | flops 2000000000 | bytes 8388608 | tf_op jit(solution)/shard_map/input_projection/pallas_call | solution.py:178
  147.9 0.0 all-to-all-done.2
  148.0 7.8 %all-to-all-start.3 = ((bf16[32,8,1024]{2,1,0:T(8,128)(2,1)}), bf16[32,8,1024]{2,1,0:T(8,128)(2,1)S(1)}, u32[]{:S(2)}, u32[]{:S(2)}) async-start(bf16[32,8,1024]{2,1,0:T(8,128)(2,1)} %bitcast.25), calls=%async_computation.3 | async-start | bytes 1048576 | tf_op jit(solution)/shard_map/all_to_all | solution.py:263
  155.8 1.4 convert_reduce_fusion
  157.2 3.1 %collective-permute-start.13 = (f32[16,1024]{1,0:T(8,128)S(1)}, f32[16,1024]{1,0:T(8,128)S(1)}, u32[]{:S(2)}, u32[]{:S(2)}) collective-permute-start(f32[16,1024]{1,0:T(8,128)S(1)} %broadcast_multiply_fusion), channel_id=1, source_target_pairs={{0,1},{1,0},{2,3},{3,2},{4,5},{5,4},{6,7},{7,6},{8,9},{9,8},{10,11... | collective-permute-start | bytes 196616 | tf_op jit(solution)/shard_map/ppermute | solution.py:227
  160.3 2.2 %collective-permute-done.13 = f32[16,1024]{1,0:T(8,128)S(1)} collective-permute-done((f32[16,1024]{1,0:T(8,128)S(1)}, f32[16,1024]{1,0:T(8,128)S(1)}, u32[]{:S(2)}, u32[]{:S(2)}) %collective-permute-start.13) | collective-permute-done | bytes 65568 | tf_op jit(solution)/shard_map/ppermute | solution.py:227
  162.5 4.7 %collective-permute-start.14 = (f32[16,1024]{1,0:T(8,128)S(1)}, f32[16,1024]{1,0:T(8,128)S(1)}, u32[]{:S(2)}, u32[]{:S(2)}) collective-permute-start(f32[16,1024]{1,0:T(8,128)S(1)} %fusion.8), channel_id=1, source_target_pairs={{0,2},{1,3},{2,0},{3,1},{4,6},{5,7},{6,4},{7,5},{8,10},{9,11},{10,... | collective-permute-start | bytes 196616 | tf_op jit(solution)/shard_map/ppermute | solution.py:227
  167.2 2.1 %collective-permute-done.14 = f32[16,1024]{1,0:T(8,128)S(1)} collective-permute-done((f32[16,1024]{1,0:T(8,128)S(1)}, f32[16,1024]{1,0:T(8,128)S(1)}, u32[]{:S(2)}, u32[]{:S(2)}) %collective-permute-start.14) | collective-permute-done | bytes 65568 | tf_op jit(solution)/shard_map/ppermute | solution.py:227
  169.3 7.9 %collective-permute-start.15 = (f32[16,1024]{1,0:T(8,128)S(1)}, f32[16,1024]{1,0:T(8,128)S(1)}, u32[]{:S(2)}, u32[]{:S(2)}) collective-permute-start(f32[16,1024]{1,0:T(8,128)S(1)} %add.38), channel_id=1, source_target_pairs={{0,4},{4,0},{1,5},{5,1},{2,6},{6,2},{3,7},{7,3},{8,12},{12,8},{9,1... | collective-permute-start | bytes 196616 | tf_op jit(solution)/shard_map/ppermute | solution.py:228
  177.3 1.7 collective-permute-done.15
  179.0 0.6 add.39
  179.7 0.8 copy.20
  (30 shorter events, 0.2 us)
Async XLA Ops:
  0.6 0.9 copy-start
  0.6 19.2 %copy-start.9 = (bf16[1,1,256,1024]{3,2,1,0:T(8,128)(2,1)S(1)}, bf16[1,1,256,1024]{3,2,1,0:T(8,128)(2,1)}, u32[]{:S(2)}) copy-start(bf16[1,1,256,1024]{3,2,1,0:T(8,128)(2,1)} %param.9) | copy-start | bytes 1572868
  0.7 15.6 %copy-start.7 = (bf16[1,1,256,1024]{3,2,1,0:T(8,128)(2,1)S(1)}, bf16[1,1,256,1024]{3,2,1,0:T(8,128)(2,1)}, u32[]{:S(2)}) copy-start(bf16[1,1,256,1024]{3,2,1,0:T(8,128)(2,1)} %param.8) | copy-start | bytes 1572868
  1.5 21.0 %copy-start.8 = (bf16[1,1,256,1024]{3,2,1,0:T(8,128)(2,1)S(1)}, bf16[1,1,256,1024]{3,2,1,0:T(8,128)(2,1)}, u32[]{:S(2)}) copy-start(bf16[1,1,256,1024]{3,2,1,0:T(8,128)(2,1)} %param.7) | copy-start | bytes 1572868
  2.7 23.0 %copy-start.10 = (bf16[1,1,256,1024]{3,2,1,0:T(8,128)(2,1)S(1)}, bf16[1,1,256,1024]{3,2,1,0:T(8,128)(2,1)}, u32[]{:S(2)}) copy-start(bf16[1,1,256,1024]{3,2,1,0:T(8,128)(2,1)} %param.6) | copy-start | bytes 1572868
  2.7 40.2 %all-to-all-start = ((bf16[32,16,1024]{2,1,0:T(8,128)(2,1)}), bf16[32,16,1024]{2,1,0:T(8,128)(2,1)S(1)}, u32[]{:S(2)}, u32[]{:S(2)}) async-start(bf16[32,16,1024]{2,1,0:T(8,128)(2,1)} %broadcast_in_dim.2), calls=%async_computation | async-start | bytes 2097152 | tf_op jit(solution)/shard_map/all_to_all | solution.py:238
  17.0 11.3 %collective-permute-start.2 = (bf16[16,8,1024]{2,1,0:T(8,128)(2,1)}, bf16[16,8,1024]{2,1,0:T(8,128)(2,1)}, u32[]{:S(2)}, u32[]{:S(2)}) collective-permute-start(bf16[16,8,1024]{2,1,0:T(8,128)(2,1)} %dynamic-slice_bitcast_fusion.1), channel_id=1, source_target_pairs={{0,8},{8,0},{1,9},{9,1},{2,10},{10,2},{3,11},{11,3},{4,12},{12,4},... | collective-permute-start | bytes 786440 | tf_op jit(solution)/shard_map/ppermute | solution.py:209
  20.6 9.9 %collective-permute-start.3 = (bf16[16,8,1024]{2,1,0:T(8,128)(2,1)}, bf16[16,8,1024]{2,1,0:T(8,128)(2,1)S(1)}, u32[]{:S(2)}, u32[]{:S(2)}) collective-permute-start(bf16[16,8,1024]{2,1,0:T(8,128)(2,1)} %dynamic-slice_bitcast_fusion), channel_id=1, source_target_pairs={{0,8},{8,0},{1,9},{9,1},{2,10},{10,2},{3,11},{11,3},{4,12},{12,4},... | collective-permute-start | bytes 786440 | tf_op jit(solution)/shard_map/ppermute | solution.py:209
  23.3 6.1 %collective-permute-start.1 = (bf16[16,8,1024]{2,1,0:T(8,128)(2,1)}, bf16[16,8,1024]{2,1,0:T(8,128)(2,1)}, u32[]{:S(2)}, u32[]{:S(2)}) collective-permute-start(bf16[16,8,1024]{2,1,0:T(8,128)(2,1)} %dynamic-slice_bitcast_fusion.2), channel_id=1, source_target_pairs={{0,8},{8,0},{1,9},{9,1},{2,10},{10,2},{3,11},{11,3},{4,12},{12,4},... | collective-permute-start | bytes 786440 | tf_op jit(solution)/shard_map/ppermute | solution.py:209
  26.4 4.1 %collective-permute-start = (bf16[16,8,1024]{2,1,0:T(8,128)(2,1)}, bf16[16,8,1024]{2,1,0:T(8,128)(2,1)}, u32[]{:S(2)}, u32[]{:S(2)}) collective-permute-start(bf16[16,8,1024]{2,1,0:T(8,128)(2,1)} %dynamic-slice_bitcast_fusion.3), channel_id=1, source_target_pairs={{0,8},{8,0},{1,9},{9,1},{2,10},{10,2},{3,11},{11,3},{4,12},{12,4},... | collective-permute-start | bytes 786440 | tf_op jit(solution)/shard_map/ppermute | solution.py:209
  42.9 52.0 %all-to-all-start.1 = ((bf16[16,2,8,4096]{3,2,1,0:T(8,128)(2,1)}), bf16[16,2,8,4096]{3,2,1,0:T(8,128)(2,1)S(1)}, u32[]{:S(2)}, u32[]{:S(2)}) async-start(bf16[16,2,8,4096]{3,2,1,0:T(8,128)(2,1)} %maximum_maximum_fusion), calls=%async_computation.1 | async-start | bytes 4194304 | tf_op jit(solution)/shard_map/all_to_all | solution.py:253
  48.3 25.8 %collective-permute-start.5 = (bf16[32,16,1024]{2,1,0:T(8,128)(2,1)S(1)}, bf16[32,16,1024]{2,1,0:T(8,128)(2,1)S(1)}, u32[]{:S(2)}, u32[]{:S(2)}) collective-permute-start(bf16[32,16,1024]{2,1,0:T(8,128)(2,1)S(1)} %all-to-all-done.refs_0_), channel_id=1, source_target_pairs={{0,1},{1,2},{2,3},{3,0},{4,5},{5,6},{6,7},{7,4},{8,9},{9,10},{10,1... | collective-permute-start | bytes 3145736 | tf_op jit(solution)/shard_map/ppermute | solution.py:215
  51.5 24.7 %collective-permute-start.4 = (bf16[32,16,1024]{2,1,0:T(8,128)(2,1)S(1)}, bf16[32,16,1024]{2,1,0:T(8,128)(2,1)S(1)}, u32[]{:S(2)}, u32[]{:S(2)}) collective-permute-start(bf16[32,16,1024]{2,1,0:T(8,128)(2,1)S(1)} %all-to-all-done.refs_0_), channel_id=1, source_target_pairs={{0,3},{1,0},{2,1},{3,2},{4,7},{5,4},{6,5},{7,6},{8,11},{9,8},{10,9... | collective-permute-start | bytes 3145736 | tf_op jit(solution)/shard_map/ppermute | solution.py:214
  74.1 13.7 %copy-start.1 = (bf16[32,16,1024]{2,1,0:T(8,128)(2,1)}, bf16[32,16,1024]{2,1,0:T(8,128)(2,1)S(1)}, u32[]{:S(2)}) copy-start(bf16[32,16,1024]{2,1,0:T(8,128)(2,1)S(1)} %collective-permute-done.5.refs_3_) | copy-start | bytes 3145732
  74.2 13.6 %collective-permute-start.6 = (bf16[16,16,1024]{2,1,0:T(8,128)(2,1)S(1)}, bf16[16,16,1024]{2,1,0:T(8,128)(2,1)S(1)}, u32[]{:S(2)}, u32[]{:S(2)}) collective-permute-start(bf16[16,16,1024]{2,1,0:T(8,128)(2,1)S(1)} %slice.8), channel_id=1, source_target_pairs={{0,1},{1,2},{2,3},{3,0},{4,5},{5,6},{6,7},{7,4},{8,9},{9,10},{10,1... | collective-permute-start | bytes 1572872 | tf_op jit(solution)/shard_map/ppermute | solution.py:216
  76.1 11.7 %copy-start.3 = (bf16[32,16,1024]{2,1,0:T(8,128)(2,1)}, bf16[32,16,1024]{2,1,0:T(8,128)(2,1)S(1)}, u32[]{:S(2)}) copy-start(bf16[32,16,1024]{2,1,0:T(8,128)(2,1)S(1)} %collective-permute-done.4.refs_1_) | copy-start | bytes 3145732
  76.2 12.6 %collective-permute-start.7 = (bf16[16,16,1024]{2,1,0:T(8,128)(2,1)S(1)}, bf16[16,16,1024]{2,1,0:T(8,128)(2,1)}, u32[]{:S(2)}, u32[]{:S(2)}) collective-permute-start(bf16[16,16,1024]{2,1,0:T(8,128)(2,1)S(1)} %slice.9), channel_id=1, source_target_pairs={{0,3},{1,0},{2,1},{3,2},{4,7},{5,4},{6,5},{7,6},{8,11},{9,8},{10,9... | collective-permute-start | bytes 1572872 | tf_op jit(solution)/shard_map/ppermute | solution.py:217
  87.8 0.8 copy-start.11
  100.3 6.3 %collective-permute-start.8 = (bf16[512,1024]{1,0:T(8,128)(2,1)S(1)}, bf16[512,1024]{1,0:T(8,128)(2,1)S(1)}, u32[]{:S(2)}, u32[]{:S(2)}) collective-permute-start(bf16[512,1024]{1,0:T(8,128)(2,1)S(1)} %get-tuple-element.37), channel_id=1, source_target_pairs={{0,8},{8,0},{1,9},{9,1},{2,10},{10,2},{3,11},{11,3},{4,12},{12,4},... | collective-permute-start | bytes 3145736 | tf_op jit(solution)/shard_map/ppermute | solution.py:209
  108.1 39.9 %all-to-all-start.2 = ((bf16[32,16,1024]{2,1,0:T(8,128)(2,1)}), bf16[32,16,1024]{2,1,0:T(8,128)(2,1)}, u32[]{:S(2)}, u32[]{:S(2)}) async-start(bf16[32,16,1024]{2,1,0:T(8,128)(2,1)} %bitcast.74), calls=%async_computation.2 | async-start | bytes 2097152 | tf_op jit(solution)/shard_map/all_to_all | solution.py:257
  120.2 6.8 %copy-start.4 = (bf16[32,16,1024]{2,1,0:T(8,128)(2,1)S(1)}, bf16[32,16,1024]{2,1,0:T(8,128)(2,1)}, u32[]{:S(2)}) copy-start(bf16[32,16,1024]{2,1,0:T(8,128)(2,1)} %copy-done.3) | copy-start | bytes 3145732
  120.2 9.3 %copy-start.2 = (bf16[32,16,1024]{2,1,0:T(8,128)(2,1)S(1)}, bf16[32,16,1024]{2,1,0:T(8,128)(2,1)}, u32[]{:S(2)}) copy-start(bf16[32,16,1024]{2,1,0:T(8,128)(2,1)} %copy-done.1) | copy-start | bytes 3145732
  122.5 8.9 %collective-permute-start.11 = (bf16[32,16,1024]{2,1,0:T(8,128)(2,1)S(1)}, bf16[32,16,1024]{2,1,0:T(8,128)(2,1)S(1)}, u32[]{:S(2)}, u32[]{:S(2)}) collective-permute-start(bf16[32,16,1024]{2,1,0:T(8,128)(2,1)S(1)} %constant_dynamic-update-slice_fusion.refs_2_), channel_id=1, source_target_pairs={{0,8},{8,0},{1,9},{9,1},{2,10},{10,2},{3,11},{11,3},{4,12},{12,4},... | collective-permute-start | bytes 3145736 | tf_op jit(solution)/shard_map/ppermute | solution.py:209
  125.1 6.3 %collective-permute-start.9 = (bf16[32,16,1024]{2,1,0:T(8,128)(2,1)S(1)}, bf16[32,16,1024]{2,1,0:T(8,128)(2,1)S(1)}, u32[]{:S(2)}, u32[]{:S(2)}) collective-permute-start(bf16[32,16,1024]{2,1,0:T(8,128)(2,1)S(1)} %all-to-all-done.refs_0_), channel_id=1, source_target_pairs={{0,8},{8,0},{1,9},{9,1},{2,10},{10,2},{3,11},{11,3},{4,12},{12,4},... | collective-permute-start | bytes 3145736 | tf_op jit(solution)/shard_map/ppermute | solution.py:209
  127.0 4.7 %collective-permute-start.10 = (bf16[32,16,1024]{2,1,0:T(8,128)(2,1)S(1)}, bf16[32,16,1024]{2,1,0:T(8,128)(2,1)S(1)}, u32[]{:S(2)}, u32[]{:S(2)}) collective-permute-start(bf16[32,16,1024]{2,1,0:T(8,128)(2,1)S(1)} %copy-done.4), channel_id=1, source_target_pairs={{0,8},{8,0},{1,9},{9,1},{2,10},{10,2},{3,11},{11,3},{4,12},{12,4},... | collective-permute-start | bytes 3145736 | tf_op jit(solution)/shard_map/ppermute | solution.py:209
  129.4 4.6 %collective-permute-start.12 = (bf16[32,16,1024]{2,1,0:T(8,128)(2,1)S(1)}, bf16[32,16,1024]{2,1,0:T(8,128)(2,1)S(1)}, u32[]{:S(2)}, u32[]{:S(2)}) collective-permute-start(bf16[32,16,1024]{2,1,0:T(8,128)(2,1)S(1)} %copy-done.2), channel_id=1, source_target_pairs={{0,8},{8,0},{1,9},{9,1},{2,10},{10,2},{3,11},{11,3},{4,12},{12,4},... | collective-permute-start | bytes 3145736 | tf_op jit(solution)/shard_map/ppermute | solution.py:209
  134.0 2.2 %copy-start.6 = (f32[16,256,256]{2,1,0:T(8,128)S(1)}, f32[16,256,256]{2,1,0:T(8,128)}, u32[]{:S(2)}) copy-start(f32[16,256,256]{2,1,0:T(8,128)} %get-tuple-element.43.attention_ref) | copy-start | bytes 12582916
  142.7 1.4 copy-start.5
  148.0 31.7 %all-to-all-start.3 = ((bf16[32,8,1024]{2,1,0:T(8,128)(2,1)}), bf16[32,8,1024]{2,1,0:T(8,128)(2,1)S(1)}, u32[]{:S(2)}, u32[]{:S(2)}) async-start(bf16[32,8,1024]{2,1,0:T(8,128)(2,1)} %bitcast.25), calls=%async_computation.3 | async-start | bytes 1048576 | tf_op jit(solution)/shard_map/all_to_all | solution.py:263
  157.2 5.4 %collective-permute-start.13 = (f32[16,1024]{1,0:T(8,128)S(1)}, f32[16,1024]{1,0:T(8,128)S(1)}, u32[]{:S(2)}, u32[]{:S(2)}) collective-permute-start(f32[16,1024]{1,0:T(8,128)S(1)} %broadcast_multiply_fusion), channel_id=1, source_target_pairs={{0,1},{1,0},{2,3},{3,2},{4,5},{5,4},{6,7},{7,6},{8,9},{9,8},{10,11... | collective-permute-start | bytes 196616 | tf_op jit(solution)/shard_map/ppermute | solution.py:227
  162.5 6.8 %collective-permute-start.14 = (f32[16,1024]{1,0:T(8,128)S(1)}, f32[16,1024]{1,0:T(8,128)S(1)}, u32[]{:S(2)}, u32[]{:S(2)}) collective-permute-start(f32[16,1024]{1,0:T(8,128)S(1)} %fusion.8), channel_id=1, source_target_pairs={{0,2},{1,3},{2,0},{3,1},{4,6},{5,7},{6,4},{7,5},{8,10},{9,11},{10,... | collective-permute-start | bytes 196616 | tf_op jit(solution)/shard_map/ppermute | solution.py:227
  169.3 9.7 %collective-permute-start.15 = (f32[16,1024]{1,0:T(8,128)S(1)}, f32[16,1024]{1,0:T(8,128)S(1)}, u32[]{:S(2)}, u32[]{:S(2)}) collective-permute-start(f32[16,1024]{1,0:T(8,128)S(1)} %add.38), channel_id=1, source_target_pairs={{0,4},{4,0},{1,5},{5,1},{2,6},{6,2},{3,7},{7,3},{8,12},{12,8},{9,1... | collective-permute-start | bytes 196616 | tf_op jit(solution)/shard_map/ppermute | solution.py:228

commit v5 on v4

--- a/solution.py
+++ b/solution.py
@@ -31,7 +31,7 @@
 def weight_rows(own, sibling, core, columns):
     first = core == 0
     parts = []
-    for at in range(8):
+    for at in range(own.shape[0]):
         mine, other = own[at, :, columns], sibling[at, :, columns]
         parts.append(jnp.where(first, mine, other))
         parts.append(jnp.where(first, other, mine))
@@ -53,11 +53,13 @@
         col = lax.broadcasted_iota(jnp.int32, (ROWS, ROWS), 1)
         bias[...] = jnp.where(lax.rem(row - col + ROWS, PATCH_BLOCK) == 0, 0.0, NEG)
 
-    q, k = q_ref[...], k_ref[...]
     v_t = v_ref[...].T
-    scores = [dot(q, head_only(k, head), NT) for head in range(4)]
+    scores = []
+    for head in range(8):
+        lanes = slice(head // 4 * SLICE, head // 4 * SLICE + SLICE)
+        scores.append(dot(q_ref[:, lanes], head_only(k_ref[:, lanes], head % 4), NT))
     weights = []
-    for head in range(4):
+    for head in range(8):
         masked = scores[head] + bias[...]
         top = jnp.max(masked, axis=1, keepdims=True)
         e = jnp.exp2((masked - top) * (math.log2(math.e) / math.sqrt(HEAD_DIM)))
@@ -65,34 +67,34 @@
         attention_ref[head] = attention
         weights.append(attention.astype(jnp.bfloat16))
     context_t = []
-    for head in range(4):
+    for head in range(8):
         rows = v_t[head * HEAD_DIM : (head + 1) * HEAD_DIM]
         context_t.append(dot(rows, weights[head], NT).astype(jnp.bfloat16))
     context_t = jnp.concatenate(context_t, axis=0)
     dw = dot(context_t, u_ref[...], NN).astype(jnp.bfloat16)
-    dw = dw.reshape(8, 2, 16, D)
-    halves = dw[:, 0].reshape(128, D), dw[:, 1].reshape(128, D)
+    dw = dw.reshape(16, 2, 16, D)
+    halves = dw[:, 0].reshape(256, D), dw[:, 1].reshape(256, D)
     keep_ref[...] = jnp.where(core == 0, halves[0], halves[1])
     send_ref[...] = jnp.where(core == 0, halves[1], halves[0])
 
 
 def forward_call(place, moved):
     def column(base):
-        return pl.BlockSpec((ROWS, SLICE), lambda i, s: (0, base + i))
-
-    shares = pl.BlockSpec((128, D), lambda i, s: (i, 0))
+        return pl.BlockSpec((ROWS, 512), lambda i, s: (0, base + i))
+
+    shares = pl.BlockSpec((256, D), lambda i, s: (i, 0))
     return pl.pallas_call(
         forward_kernel,
         grid_spec=pltpu.PrefetchScalarGridSpec(
             num_scalar_prefetch=1,
-            grid=(4,),
+            grid=(2,),
             in_specs=[
                 column(0),
+                column(2),
                 column(4),
-                column(8),
                 pl.BlockSpec((ROWS, D), lambda i, s: (0, 3)),
             ],
-            out_specs=[pl.BlockSpec((4, ROWS, ROWS), lambda i, s: (i, 0, 0)), shares, shares],
+            out_specs=[pl.BlockSpec((8, ROWS, ROWS), lambda i, s: (i, 0, 0)), shares, shares],
             scratch_shapes=[pltpu.VMEM((ROWS, ROWS), jnp.float32)],
         ),
         out_shape=[
@@ -100,7 +102,7 @@
             jax.ShapeDtypeStruct((512, D), jnp.bfloat16),
             jax.ShapeDtypeStruct((512, D), jnp.bfloat16),
         ],
-        compiler_params=pltpu.CompilerParams(vmem_limit_bytes=20 * 2**20),
+        compiler_params=pltpu.CompilerParams(vmem_limit_bytes=16 * 2**20),
         cost_estimate=pl.CostEstimate(
             flops=2 * 10**9, bytes_accessed=8 * 2**20, transcendentals=2**20
         ),
@@ -111,7 +113,7 @@
 def backward_kernel(place, attention_ref, q_ref, k_ref, v_ref, u_ref, *refs):
     pieces, g_ref = refs[:8], refs[8]
     x_at, core = place[0], place[1]
-    cg = jnp.zeros((ROWS, SLICE), jnp.float32)
+    cg = jnp.zeros((ROWS, 2 * SLICE), jnp.float32)
     for d in range(4):
         w = weight_rows(pieces[d], pieces[4 + d], core, slice(None))
         at = pl.multiple_of(lax.rem(x_at + d, 4) * SLICE, SLICE)
@@ -119,14 +121,17 @@
     cg = cg.astype(jnp.bfloat16)
     v = v_ref[...]
     q_t, k_t, cg_t = q_ref[...].T, k_ref[...].T, cg.T
-    grad_scores = [dot(cg, head_only(v, head), NT) for head in range(4)]
+    grad_scores = []
+    for head in range(8):
+        lanes = slice(head // 4 * SLICE, head // 4 * SLICE + SLICE)
+        grad_scores.append(dot(cg[:, lanes], head_only(v[:, lanes], head % 4), NT))
     score_grads = []
-    for head in range(4):
+    for head in range(8):
         attention = attention_ref[head]
         total = jnp.sum(attention * grad_scores[head], axis=1, keepdims=True)
         score_grad = attention * (grad_scores[head] - total) * (1.0 / math.sqrt(HEAD_DIM))
         score_grads.append(score_grad.astype(jnp.bfloat16))
-    for head in range(4):
+    for head in range(8):
         rows = slice(head * HEAD_DIM, (head + 1) * HEAD_DIM)
         attention_b = attention_ref[head].astype(jnp.bfloat16)
         g_ref[0, rows] = dot(k_t[rows], score_grads[head], NT).astype(jnp.bfloat16)
@@ -136,25 +141,25 @@
 
 def backward_call(place, attention, moved, pieces):
     def column(base):
-        return pl.BlockSpec((ROWS, SLICE), lambda i, s: (0, base + i))
+        return pl.BlockSpec((ROWS, 2 * SLICE), lambda i, s: (0, base + i))
 
     return pl.pallas_call(
         backward_kernel,
         grid_spec=pltpu.PrefetchScalarGridSpec(
             num_scalar_prefetch=1,
-            grid=(4,),
+            grid=(2,),
             in_specs=[
-                pl.BlockSpec((4, ROWS, ROWS), lambda i, s: (i, 0, 0)),
+                pl.BlockSpec((8, ROWS, ROWS), lambda i, s: (i, 0, 0)),
                 column(0),
+                column(2),
                 column(4),
-                column(8),
                 pl.BlockSpec((ROWS, D), lambda i, s: (0, 3)),
             ]
-            + [pl.BlockSpec((8, 16, SLICE), lambda i, s: (i, 0, 3))] * 8,
-            out_specs=pl.BlockSpec((3, SLICE, ROWS), lambda i, s: (0, i, 0)),
+            + [pl.BlockSpec((16, 16, SLICE), lambda i, s: (i, 0, 3))] * 8,
+            out_specs=pl.BlockSpec((3, 2 * SLICE, ROWS), lambda i, s: (0, i, 0)),
         ),
         out_shape=pltpu.HBM((3, D, ROWS), jnp.bfloat16),
-        compiler_params=pltpu.CompilerParams(vmem_limit_bytes=20 * 2**20),
+        compiler_params=pltpu.CompilerParams(vmem_limit_bytes=16 * 2**20),
         cost_estimate=pl.CostEstimate(
             flops=3 * 10**9, bytes_accessed=10 * 2**20, transcendentals=0
         ),

time: 183 us -> 181 us (0.989)
  Pallas kernels: 15.8 us -> 13.6 us
  transfers between devices with their start and end apart: 20 -> 20, of which waited for: 11 -> 12; matrix products, arithmetic and copies ran while one was open for 7% -> 7% of each run, Pallas kernels for 6% -> 5%
where the time goes in v5:
time: 181 us; the launch traced here: 178 us
  starting transfers between devices  88.9 us (49%)
  waiting for transfers between devices  54.1 us (30%)
  Pallas kernels  13.6 us (8%)
  local copies, waits for them, and re-layouts  12.5 us (7%)
  other arithmetic  8.21 us (5%)
    ppermute x9, starting transfers between devices, swap_cores(): return lax.ppermute(block, 'c', ring(2, 1))  21.9 us
    ppermute x1, waiting for transfers between devices, spread_x(): before = lax.ppermute(plane, 'x', ring(4, 1))  19.3 us
    all_to_all x1, starting transfers between devices, on_device(): plane = lax.all_to_all(columns, PLANE_AXES, 0, 0, tiled=True)  13.6 us
    all_to_all x1, starting transfers between devices, on_device(): lax.all_to_all(share.reshape(32, 16, D), PLANE_AXES, 0, 0, tiled=True)  12.1 us
    all_to_all x1, waiting for transfers between devices, on_device(): plane = lax.all_to_all(columns, PLANE_AXES, 0, 0, tiled=True)  9.89 us
    ppermute x1, starting transfers between devices, sum_groups(): return share + lax.ppermute(share, 'zh', ring(2, 1))  7.96 us
    ppermute x2, starting transfers between devices, sum_groups(): share = share + lax.ppermute(share, 'x', [(i, i ^ bit) for i in range(4)])  7.79 us
    all_to_all x1, starting transfers between devices, on_device(): input_gradient = lax.all_to_all(result, CLIP_AXES, 0, 0, tiled=True)  7.11 us
  transfers between devices with their start and end apart: 20, of which 12 were waited for; matrix products, arithmetic and copies ran while one was open for 7% of the time, Pallas kernels for 5%

profile of v5, /device:TPU:1, one launch (start us, length us, event | category | flops | bytes accessed | tf_op | source)
XLA Modules:
  0.0 178.3 jit_solution(872452244611881025)
XLA Ops:
  0.6 0.0 copy-start
  0.7 0.8 constant_dynamic-slice_fusion
  1.5 0.1 copy-done
  1.5 1.1 broadcast_in_dim.2
  2.7 13.6 %all-to-all-start = ((bf16[32,16,1024]{2,1,0:T(8,128)(2,1)}), bf16[32,16,1024]{2,1,0:T(8,128)(2,1)S(1)}, u32[]{:S(2)}, u32[]{:S(2)}) async-start(bf16[32,16,1024]{2,1,0:T(8,128)(2,1)} %broadcast_in_dim.2), calls=%async_computation | async-start | bytes 2097152 | tf_op jit(solution)/shard_map/all_to_all | solution.py:243
  16.3 0.7 dynamic-slice_bitcast_fusion.1
  17.0 2.9 %collective-permute-start.2 = (bf16[16,8,1024]{2,1,0:T(8,128)(2,1)}, bf16[16,8,1024]{2,1,0:T(8,128)(2,1)}, u32[]{:S(2)}, u32[]{:S(2)}) collective-permute-start(bf16[16,8,1024]{2,1,0:T(8,128)(2,1)} %dynamic-slice_bitcast_fusion.1), channel_id=1, source_target_pairs={{0,8},{8,0},{1,9},{9,1},{2,10},{10,2},{3,11},{11,3},{4,12},{12,4},... | collective-permute-start | bytes 786440 | tf_op jit(solution)/shard_map/ppermute | solution.py:214
  19.9 0.7 dynamic-slice_bitcast_fusion
  20.6 1.9 %collective-permute-start.3 = (bf16[16,8,1024]{2,1,0:T(8,128)(2,1)}, bf16[16,8,1024]{2,1,0:T(8,128)(2,1)S(1)}, u32[]{:S(2)}, u32[]{:S(2)}) collective-permute-start(bf16[16,8,1024]{2,1,0:T(8,128)(2,1)} %dynamic-slice_bitcast_fusion), channel_id=1, source_target_pairs={{0,8},{8,0},{1,9},{9,1},{2,10},{10,2},{3,11},{11,3},{4,12},{12,4},... | collective-permute-start | bytes 786440 | tf_op jit(solution)/shard_map/ppermute | solution.py:214
  22.5 0.7 dynamic-slice_bitcast_fusion.2
  23.3 2.4 %collective-permute-start.1 = (bf16[16,8,1024]{2,1,0:T(8,128)(2,1)}, bf16[16,8,1024]{2,1,0:T(8,128)(2,1)}, u32[]{:S(2)}, u32[]{:S(2)}) collective-permute-start(bf16[16,8,1024]{2,1,0:T(8,128)(2,1)} %dynamic-slice_bitcast_fusion.2), channel_id=1, source_target_pairs={{0,8},{8,0},{1,9},{9,1},{2,10},{10,2},{3,11},{11,3},{4,12},{12,4},... | collective-permute-start | bytes 786440 | tf_op jit(solution)/shard_map/ppermute | solution.py:214
  25.7 0.7 dynamic-slice_bitcast_fusion.3
  26.4 1.9 %collective-permute-start = (bf16[16,8,1024]{2,1,0:T(8,128)(2,1)}, bf16[16,8,1024]{2,1,0:T(8,128)(2,1)}, u32[]{:S(2)}, u32[]{:S(2)}) collective-permute-start(bf16[16,8,1024]{2,1,0:T(8,128)(2,1)} %dynamic-slice_bitcast_fusion.3), channel_id=1, source_target_pairs={{0,8},{8,0},{1,9},{9,1},{2,10},{10,2},{3,11},{11,3},{4,12},{12,4},... | collective-permute-start | bytes 786440 | tf_op jit(solution)/shard_map/ppermute | solution.py:214
  28.3 0.0 collective-permute-done.2
  28.3 1.0 fusion.2
  29.4 1.0 fusion.4
  30.3 0.1 pad_maximum_fusion.2
  30.4 0.1 pad_maximum_fusion.1
  30.5 0.0 collective-permute-done.3
  30.5 1.0 fusion.6
  31.5 1.5 maximum_maximum_fusion
  33.0 9.9 %all-to-all-done.refs_0_ = bf16[32,16,1024]{2,1,0:T(8,128)(2,1)S(1)} async-done(((bf16[32,16,1024]{2,1,0:T(8,128)(2,1)}), bf16[32,16,1024]{2,1,0:T(8,128)(2,1)S(1)}, u32[]{:S(2)}, u32[]{:S(2)}) %all-to-all-start) | async-done | bytes 1048608 | tf_op jit(solution)/shard_map/all_to_all | solution.py:243
  42.9 5.4 %all-to-all-start.1 = ((bf16[16,2,8,4096]{3,2,1,0:T(8,128)(2,1)}), bf16[16,2,8,4096]{3,2,1,0:T(8,128)(2,1)S(1)}, u32[]{:S(2)}, u32[]{:S(2)}) async-start(bf16[16,2,8,4096]{3,2,1,0:T(8,128)(2,1)} %maximum_maximum_fusion), calls=%async_computation.1 | async-start | bytes 4194304 | tf_op jit(solution)/shard_map/all_to_all | solution.py:258
  48.3 3.1 %collective-permute-start.5 = (bf16[32,16,1024]{2,1,0:T(8,128)(2,1)S(1)}, bf16[32,16,1024]{2,1,0:T(8,128)(2,1)S(1)}, u32[]{:S(2)}, u32[]{:S(2)}) collective-permute-start(bf16[32,16,1024]{2,1,0:T(8,128)(2,1)S(1)} %all-to-all-done.refs_0_), channel_id=1, source_target_pairs={{0,1},{1,2},{2,3},{3,0},{4,5},{5,6},{6,7},{7,4},{8,9},{9,10},{10,1... | collective-permute-start | bytes 3145736 | tf_op jit(solution)/shard_map/ppermute | solution.py:220
  51.5 3.4 %collective-permute-start.4 = (bf16[32,16,1024]{2,1,0:T(8,128)(2,1)S(1)}, bf16[32,16,1024]{2,1,0:T(8,128)(2,1)S(1)}, u32[]{:S(2)}, u32[]{:S(2)}) collective-permute-start(bf16[32,16,1024]{2,1,0:T(8,128)(2,1)S(1)} %all-to-all-done.refs_0_), channel_id=1, source_target_pairs={{0,3},{1,0},{2,1},{3,2},{4,7},{5,4},{6,5},{7,6},{8,11},{9,8},{10,9... | collective-permute-start | bytes 3145736 | tf_op jit(solution)/shard_map/ppermute | solution.py:219
  54.8 19.3 %collective-permute-done.5.refs_3_ = bf16[32,16,1024]{2,1,0:T(8,128)(2,1)S(1)} collective-permute-done((bf16[32,16,1024]{2,1,0:T(8,128)(2,1)S(1)}, bf16[32,16,1024]{2,1,0:T(8,128)(2,1)S(1)}, u32[]{:S(2)}, u32[]{:S(2)}) %collective-permute-start.5) | collective-permute-done | bytes 1048608 | tf_op jit(solution)/shard_map/ppermute | solution.py:220
  74.2 1.9 %collective-permute-start.6 = (bf16[16,16,1024]{2,1,0:T(8,128)(2,1)S(1)}, bf16[16,16,1024]{2,1,0:T(8,128)(2,1)S(1)}, u32[]{:S(2)}, u32[]{:S(2)}) collective-permute-start(bf16[16,16,1024]{2,1,0:T(8,128)(2,1)S(1)} %slice.8), channel_id=1, source_target_pairs={{0,1},{1,2},{2,3},{3,0},{4,5},{5,6},{6,7},{7,4},{8,9},{9,10},{10,1... | collective-permute-start | bytes 1572872 | tf_op jit(solution)/shard_map/ppermute | solution.py:221
  76.1 0.0 collective-permute-done.4.refs_1_
  76.2 4.6 %collective-permute-start.7 = (bf16[16,16,1024]{2,1,0:T(8,128)(2,1)S(1)}, bf16[16,16,1024]{2,1,0:T(8,128)(2,1)}, u32[]{:S(2)}, u32[]{:S(2)}) collective-permute-start(bf16[16,16,1024]{2,1,0:T(8,128)(2,1)S(1)} %slice.9), channel_id=1, source_target_pairs={{0,3},{1,0},{2,1},{3,2},{4,7},{5,4},{6,5},{7,6},{8,11},{9,8},{10,9... | collective-permute-start | bytes 1572872 | tf_op jit(solution)/shard_map/ppermute | solution.py:222
  80.8 0.1 pad_add_fusion.place
  80.8 7.0 %collective-permute-done.6 = bf16[16,16,1024]{2,1,0:T(8,128)(2,1)S(1)} collective-permute-done((bf16[16,16,1024]{2,1,0:T(8,128)(2,1)S(1)}, bf16[16,16,1024]{2,1,0:T(8,128)(2,1)S(1)}, u32[]{:S(2)}, u32[]{:S(2)}) %collective-permute-start.6) | collective-permute-done | bytes 524320 | tf_op jit(solution)/shard_map/ppermute | solution.py:221
  87.8 0.8 copy-done.11
  88.6 0.2 collective-permute-done.7
  88.8 6.1 %all-to-all-done.1 = bf16[16,2,8,4096]{3,2,1,0:T(8,128)(2,1)S(1)} async-done(((bf16[16,2,8,4096]{3,2,1,0:T(8,128)(2,1)}), bf16[16,2,8,4096]{3,2,1,0:T(8,128)(2,1)S(1)}, u32[]{:S(2)}, u32[]{:S(2)}) %all-to-all-start.1) | async-done | bytes 2097184 | tf_op jit(solution)/shard_map/all_to_all | solution.py:258
  94.9 4.6 %attention_and_weight_grad.1 = (f32[16,256,256]{2,1,0:T(8,128)}, bf16[512,1024]{1,0:T(8,128)(2,1)S(1)}, bf16[512,1024]{1,0:T(8,128)(2,1)S(1)}) custom-call(s32[2]{0:T(128)S(1)} %pad_add_fusion.place, bf16[256,4096]{1,0:T(8,128)(2,1)S(1)} %bitcast.65, bf16[256,4096]{1,0:T(8,128)(2,1)S(1)} %bitcast.66, bf16[256,4096]{1,0:T(8,128)(2,1)S(1)} %bitcast.67, ...), custom_call_target="tpu_custom_call" | custom-call | flops 2000000000 | bytes 8388608 | tf_op jit(solution)/shard_map/attention_and_weight_grad/pallas_call | solution.py:86
  99.5 4.0 %collective-permute-start.8 = (bf16[512,1024]{1,0:T(8,128)(2,1)S(1)}, bf16[512,1024]{1,0:T(8,128)(2,1)S(1)}, u32[]{:S(2)}, u32[]{:S(2)}) collective-permute-start(bf16[512,1024]{1,0:T(8,128)(2,1)S(1)} %get-tuple-element.37), channel_id=1, source_target_pairs={{0,8},{8,0},{1,9},{9,1},{2,10},{10,2},{3,11},{11,3},{4,12},{12,4},... | collective-permute-start | bytes 3145736 | tf_op jit(solution)/shard_map/ppermute | solution.py:214
  103.6 2.3 %collective-permute-done.8 = bf16[512,1024]{1,0:T(8,128)(2,1)S(1)} collective-permute-done((bf16[512,1024]{1,0:T(8,128)(2,1)S(1)}, bf16[512,1024]{1,0:T(8,128)(2,1)S(1)}, u32[]{:S(2)}, u32[]{:S(2)}) %collective-permute-start.8) | collective-permute-done | bytes 1048608 | tf_op jit(solution)/shard_map/ppermute | solution.py:214
  105.8 1.5 add_convert_fusion
  107.3 12.1 %all-to-all-start.2 = ((bf16[32,16,1024]{2,1,0:T(8,128)(2,1)}), bf16[32,16,1024]{2,1,0:T(8,128)(2,1)}, u32[]{:S(2)}, u32[]{:S(2)}) async-start(bf16[32,16,1024]{2,1,0:T(8,128)(2,1)} %bitcast.74), calls=%async_computation.2 | async-start | bytes 2097152 | tf_op jit(solution)/shard_map/all_to_all | solution.py:262
  119.4 1.2 constant_dynamic-update-slice_fusion.1
  120.6 1.1 constant_dynamic-update-slice_fusion.refs_2_
  121.7 2.6 %collective-permute-start.11 = (bf16[32,16,1024]{2,1,0:T(8,128)(2,1)S(1)}, bf16[32,16,1024]{2,1,0:T(8,128)(2,1)S(1)}, u32[]{:S(2)}, u32[]{:S(2)}) collective-permute-start(bf16[32,16,1024]{2,1,0:T(8,128)(2,1)S(1)} %constant_dynamic-update-slice_fusion.refs_2_), channel_id=1, source_target_pairs={{0,8},{8,0},{1,9},{9,1},{2,10},{10,2},{3,11},{11,3},{4,12},{12,4},... | collective-permute-start | bytes 3145736 | tf_op jit(solution)/shard_map/ppermute | solution.py:214
  124.3 1.9 %collective-permute-start.9 = (bf16[32,16,1024]{2,1,0:T(8,128)(2,1)S(1)}, bf16[32,16,1024]{2,1,0:T(8,128)(2,1)S(1)}, u32[]{:S(2)}, u32[]{:S(2)}) collective-permute-start(bf16[32,16,1024]{2,1,0:T(8,128)(2,1)S(1)} %all-to-all-done.refs_0_), channel_id=1, source_target_pairs={{0,8},{8,0},{1,9},{9,1},{2,10},{10,2},{3,11},{11,3},{4,12},{12,4},... | collective-permute-start | bytes 3145736 | tf_op jit(solution)/shard_map/ppermute | solution.py:214
  126.2 2.4 %collective-permute-start.10 = (bf16[32,16,1024]{2,1,0:T(8,128)(2,1)S(1)}, bf16[32,16,1024]{2,1,0:T(8,128)(2,1)S(1)}, u32[]{:S(2)}, u32[]{:S(2)}) collective-permute-start(bf16[32,16,1024]{2,1,0:T(8,128)(2,1)S(1)} %copy-done.4), channel_id=1, source_target_pairs={{0,8},{8,0},{1,9},{9,1},{2,10},{10,2},{3,11},{11,3},{4,12},{12,4},... | collective-permute-start | bytes 3145736 | tf_op jit(solution)/shard_map/ppermute | solution.py:214
  128.7 1.9 %collective-permute-start.12 = (bf16[32,16,1024]{2,1,0:T(8,128)(2,1)S(1)}, bf16[32,16,1024]{2,1,0:T(8,128)(2,1)S(1)}, u32[]{:S(2)}, u32[]{:S(2)}) collective-permute-start(bf16[32,16,1024]{2,1,0:T(8,128)(2,1)S(1)} %copy-done.2), channel_id=1, source_target_pairs={{0,8},{8,0},{1,9},{9,1},{2,10},{10,2},{3,11},{11,3},{4,12},{12,4},... | collective-permute-start | bytes 3145736 | tf_op jit(solution)/shard_map/ppermute | solution.py:214
  130.6 0.0 collective-permute-done.11.refs_6_
  130.6 0.3 collective-permute-done.10.refs_5_
  130.9 2.3 %collective-permute-done.12.refs_7_ = bf16[32,16,1024]{2,1,0:T(8,128)(2,1)S(1)} collective-permute-done((bf16[32,16,1024]{2,1,0:T(8,128)(2,1)S(1)}, bf16[32,16,1024]{2,1,0:T(8,128)(2,1)S(1)}, u32[]{:S(2)}, u32[]{:S(2)}) %collective-permute-start.12) | collective-permute-done | bytes 1048608 | tf_op jit(solution)/shard_map/ppermute | solution.py:214
  133.2 2.2 %copy-done.6 = f32[16,256,256]{2,1,0:T(8,128)S(1)} copy-done((f32[16,256,256]{2,1,0:T(8,128)S(1)}, f32[16,256,256]{2,1,0:T(8,128)}, u32[]{:S(2)}) %copy-start.6) | copy-done | bytes 4194328
  135.4 5.1 %attention_grads.1 = bf16[3,1024,256]{2,1,0:T(8,128)(2,1)} custom-call(s32[2]{0:T(128)S(1)} %pad_add_fusion.place, f32[16,256,256]{2,1,0:T(8,128)S(1)} %copy-done.6, bf16[256,4096]{1,0:T(8,128)(2,1)S(1)} %bitcast.69, bf16[256,4096]{1,0:T(8,128)(2,1)S(1)} %bitcast.70, bf16[256,4096]{1,0:T(8,128)(2,1)S(1)} %bitcast.71, bf16[256,4096]{1,0:T(8,128)(2,1)S(1)} %bitcast.72, ...), custom_call_target="tpu_custom_call" | custom-call | flops 3000000000 | bytes 10485760 | tf_op jit(solution)/shard_map/attention_grads/pallas_call | solution.py:146
  140.5 1.4 copy-done.5
  141.9 3.8 %input_projection.1 = bf16[256,1024]{1,0:T(8,128)(2,1)} custom-call(s32[2]{0:T(128)S(1)} %pad_add_fusion.place, bf16[3072,256]{1,0:T(8,128)(2,1)S(1)} %bitcast.73, bf16[32,16,1024]{2,1,0:T(8,128)(2,1)S(1)} %all-to-all-done.refs_0_, bf16[32,16,1024]{2,1,0:T(8,128)(2,1)S(1)} %copy-done.4, bf16[32,16,1024]{2,1,0:T(8,128)(2,1)S(1)} %constant_dynamic-update-slice_fusion.refs_2_, ...), custom_call_target="tpu_custom_call" | custom-call | flops 2000000000 | bytes 8388608 | tf_op jit(solution)/shard_map/input_projection/pallas_call | solution.py:183
  145.7 0.7 all-to-all-done.2
  146.4 7.1 %all-to-all-start.3 = ((bf16[32,8,1024]{2,1,0:T(8,128)(2,1)}), bf16[32,8,1024]{2,1,0:T(8,128)(2,1)S(1)}, u32[]{:S(2)}, u32[]{:S(2)}) async-start(bf16[32,8,1024]{2,1,0:T(8,128)(2,1)} %bitcast.25), calls=%async_computation.3 | async-start | bytes 1048576 | tf_op jit(solution)/shard_map/all_to_all | solution.py:268
  153.5 1.4 convert_reduce_fusion
  154.9 3.1 %collective-permute-start.13 = (f32[16,1024]{1,0:T(8,128)S(1)}, f32[16,1024]{1,0:T(8,128)S(1)}, u32[]{:S(2)}, u32[]{:S(2)}) collective-permute-start(f32[16,1024]{1,0:T(8,128)S(1)} %broadcast_multiply_fusion), channel_id=1, source_target_pairs={{0,1},{1,0},{2,3},{3,2},{4,5},{5,4},{6,7},{7,6},{8,9},{9,8},{10,11... | collective-permute-start | bytes 196616 | tf_op jit(solution)/shard_map/ppermute | solution.py:232
  158.1 2.2 %collective-permute-done.13 = f32[16,1024]{1,0:T(8,128)S(1)} collective-permute-done((f32[16,1024]{1,0:T(8,128)S(1)}, f32[16,1024]{1,0:T(8,128)S(1)}, u32[]{:S(2)}, u32[]{:S(2)}) %collective-permute-start.13) | collective-permute-done | bytes 65568 | tf_op jit(solution)/shard_map/ppermute | solution.py:232
  160.3 4.7 %collective-permute-start.14 = (f32[16,1024]{1,0:T(8,128)S(1)}, f32[16,1024]{1,0:T(8,128)S(1)}, u32[]{:S(2)}, u32[]{:S(2)}) collective-permute-start(f32[16,1024]{1,0:T(8,128)S(1)} %fusion.8), channel_id=1, source_target_pairs={{0,2},{1,3},{2,0},{3,1},{4,6},{5,7},{6,4},{7,5},{8,10},{9,11},{10,... | collective-permute-start | bytes 196616 | tf_op jit(solution)/shard_map/ppermute | solution.py:232
  165.0 2.1 %collective-permute-done.14 = f32[16,1024]{1,0:T(8,128)S(1)} collective-permute-done((f32[16,1024]{1,0:T(8,128)S(1)}, f32[16,1024]{1,0:T(8,128)S(1)}, u32[]{:S(2)}, u32[]{:S(2)}) %collective-permute-start.14) | collective-permute-done | bytes 65568 | tf_op jit(solution)/shard_map/ppermute | solution.py:232
  167.1 8.0 %collective-permute-start.15 = (f32[16,1024]{1,0:T(8,128)S(1)}, f32[16,1024]{1,0:T(8,128)S(1)}, u32[]{:S(2)}, u32[]{:S(2)}) collective-permute-start(f32[16,1024]{1,0:T(8,128)S(1)} %add.38), channel_id=1, source_target_pairs={{0,4},{4,0},{1,5},{5,1},{2,6},{6,2},{3,7},{7,3},{8,12},{12,8},{9,1... | collective-permute-start | bytes 196616 | tf_op jit(solution)/shard_map/ppermute | solution.py:233
  175.1 1.7 collective-permute-done.15
  176.8 0.6 add.39
  177.5 0.0 all-to-all-done.3
  177.5 0.8 copy.20
  (30 shorter events, 0.2 us)
Async XLA Ops:
  0.6 0.9 copy-start
  0.6 19.2 %copy-start.9 = (bf16[1,1,256,1024]{3,2,1,0:T(8,128)(2,1)S(1)}, bf16[1,1,256,1024]{3,2,1,0:T(8,128)(2,1)}, u32[]{:S(2)}) copy-start(bf16[1,1,256,1024]{3,2,1,0:T(8,128)(2,1)} %param.9) | copy-start | bytes 1572868
  0.7 15.6 %copy-start.7 = (bf16[1,1,256,1024]{3,2,1,0:T(8,128)(2,1)S(1)}, bf16[1,1,256,1024]{3,2,1,0:T(8,128)(2,1)}, u32[]{:S(2)}) copy-start(bf16[1,1,256,1024]{3,2,1,0:T(8,128)(2,1)} %param.8) | copy-start | bytes 1572868
  1.5 21.0 %copy-start.8 = (bf16[1,1,256,1024]{3,2,1,0:T(8,128)(2,1)S(1)}, bf16[1,1,256,1024]{3,2,1,0:T(8,128)(2,1)}, u32[]{:S(2)}) copy-start(bf16[1,1,256,1024]{3,2,1,0:T(8,128)(2,1)} %param.7) | copy-start | bytes 1572868
  2.7 23.0 %copy-start.10 = (bf16[1,1,256,1024]{3,2,1,0:T(8,128)(2,1)S(1)}, bf16[1,1,256,1024]{3,2,1,0:T(8,128)(2,1)}, u32[]{:S(2)}) copy-start(bf16[1,1,256,1024]{3,2,1,0:T(8,128)(2,1)} %param.6) | copy-start | bytes 1572868
  2.7 40.2 %all-to-all-start = ((bf16[32,16,1024]{2,1,0:T(8,128)(2,1)}), bf16[32,16,1024]{2,1,0:T(8,128)(2,1)S(1)}, u32[]{:S(2)}, u32[]{:S(2)}) async-start(bf16[32,16,1024]{2,1,0:T(8,128)(2,1)} %broadcast_in_dim.2), calls=%async_computation | async-start | bytes 2097152 | tf_op jit(solution)/shard_map/all_to_all | solution.py:243
  17.0 11.3 %collective-permute-start.2 = (bf16[16,8,1024]{2,1,0:T(8,128)(2,1)}, bf16[16,8,1024]{2,1,0:T(8,128)(2,1)}, u32[]{:S(2)}, u32[]{:S(2)}) collective-permute-start(bf16[16,8,1024]{2,1,0:T(8,128)(2,1)} %dynamic-slice_bitcast_fusion.1), channel_id=1, source_target_pairs={{0,8},{8,0},{1,9},{9,1},{2,10},{10,2},{3,11},{11,3},{4,12},{12,4},... | collective-permute-start | bytes 786440 | tf_op jit(solution)/shard_map/ppermute | solution.py:214
  20.6 9.9 %collective-permute-start.3 = (bf16[16,8,1024]{2,1,0:T(8,128)(2,1)}, bf16[16,8,1024]{2,1,0:T(8,128)(2,1)S(1)}, u32[]{:S(2)}, u32[]{:S(2)}) collective-permute-start(bf16[16,8,1024]{2,1,0:T(8,128)(2,1)} %dynamic-slice_bitcast_fusion), channel_id=1, source_target_pairs={{0,8},{8,0},{1,9},{9,1},{2,10},{10,2},{3,11},{11,3},{4,12},{12,4},... | collective-permute-start | bytes 786440 | tf_op jit(solution)/shard_map/ppermute | solution.py:214
  23.3 6.1 %collective-permute-start.1 = (bf16[16,8,1024]{2,1,0:T(8,128)(2,1)}, bf16[16,8,1024]{2,1,0:T(8,128)(2,1)}, u32[]{:S(2)}, u32[]{:S(2)}) collective-permute-start(bf16[16,8,1024]{2,1,0:T(8,128)(2,1)} %dynamic-slice_bitcast_fusion.2), channel_id=1, source_target_pairs={{0,8},{8,0},{1,9},{9,1},{2,10},{10,2},{3,11},{11,3},{4,12},{12,4},... | collective-permute-start | bytes 786440 | tf_op jit(solution)/shard_map/ppermute | solution.py:214
  26.4 4.1 %collective-permute-start = (bf16[16,8,1024]{2,1,0:T(8,128)(2,1)}, bf16[16,8,1024]{2,1,0:T(8,128)(2,1)}, u32[]{:S(2)}, u32[]{:S(2)}) collective-permute-start(bf16[16,8,1024]{2,1,0:T(8,128)(2,1)} %dynamic-slice_bitcast_fusion.3), channel_id=1, source_target_pairs={{0,8},{8,0},{1,9},{9,1},{2,10},{10,2},{3,11},{11,3},{4,12},{12,4},... | collective-permute-start | bytes 786440 | tf_op jit(solution)/shard_map/ppermute | solution.py:214
  42.9 52.0 %all-to-all-start.1 = ((bf16[16,2,8,4096]{3,2,1,0:T(8,128)(2,1)}), bf16[16,2,8,4096]{3,2,1,0:T(8,128)(2,1)S(1)}, u32[]{:S(2)}, u32[]{:S(2)}) async-start(bf16[16,2,8,4096]{3,2,1,0:T(8,128)(2,1)} %maximum_maximum_fusion), calls=%async_computation.1 | async-start | bytes 4194304 | tf_op jit(solution)/shard_map/all_to_all | solution.py:258
  48.3 25.8 %collective-permute-start.5 = (bf16[32,16,1024]{2,1,0:T(8,128)(2,1)S(1)}, bf16[32,16,1024]{2,1,0:T(8,128)(2,1)S(1)}, u32[]{:S(2)}, u32[]{:S(2)}) collective-permute-start(bf16[32,16,1024]{2,1,0:T(8,128)(2,1)S(1)} %all-to-all-done.refs_0_), channel_id=1, source_target_pairs={{0,1},{1,2},{2,3},{3,0},{4,5},{5,6},{6,7},{7,4},{8,9},{9,10},{10,1... | collective-permute-start | bytes 3145736 | tf_op jit(solution)/shard_map/ppermute | solution.py:220
  51.5 24.7 %collective-permute-start.4 = (bf16[32,16,1024]{2,1,0:T(8,128)(2,1)S(1)}, bf16[32,16,1024]{2,1,0:T(8,128)(2,1)S(1)}, u32[]{:S(2)}, u32[]{:S(2)}) collective-permute-start(bf16[32,16,1024]{2,1,0:T(8,128)(2,1)S(1)} %all-to-all-done.refs_0_), channel_id=1, source_target_pairs={{0,3},{1,0},{2,1},{3,2},{4,7},{5,4},{6,5},{7,6},{8,11},{9,8},{10,9... | collective-permute-start | bytes 3145736 | tf_op jit(solution)/shard_map/ppermute | solution.py:219
  74.1 13.7 %copy-start.1 = (bf16[32,16,1024]{2,1,0:T(8,128)(2,1)}, bf16[32,16,1024]{2,1,0:T(8,128)(2,1)S(1)}, u32[]{:S(2)}) copy-start(bf16[32,16,1024]{2,1,0:T(8,128)(2,1)S(1)} %collective-permute-done.5.refs_3_) | copy-start | bytes 3145732
  74.2 13.6 %collective-permute-start.6 = (bf16[16,16,1024]{2,1,0:T(8,128)(2,1)S(1)}, bf16[16,16,1024]{2,1,0:T(8,128)(2,1)S(1)}, u32[]{:S(2)}, u32[]{:S(2)}) collective-permute-start(bf16[16,16,1024]{2,1,0:T(8,128)(2,1)S(1)} %slice.8), channel_id=1, source_target_pairs={{0,1},{1,2},{2,3},{3,0},{4,5},{5,6},{6,7},{7,4},{8,9},{9,10},{10,1... | collective-permute-start | bytes 1572872 | tf_op jit(solution)/shard_map/ppermute | solution.py:221
  76.1 11.7 %copy-start.3 = (bf16[32,16,1024]{2,1,0:T(8,128)(2,1)}, bf16[32,16,1024]{2,1,0:T(8,128)(2,1)S(1)}, u32[]{:S(2)}) copy-start(bf16[32,16,1024]{2,1,0:T(8,128)(2,1)S(1)} %collective-permute-done.4.refs_1_) | copy-start | bytes 3145732
  76.2 12.6 %collective-permute-start.7 = (bf16[16,16,1024]{2,1,0:T(8,128)(2,1)S(1)}, bf16[16,16,1024]{2,1,0:T(8,128)(2,1)}, u32[]{:S(2)}, u32[]{:S(2)}) collective-permute-start(bf16[16,16,1024]{2,1,0:T(8,128)(2,1)S(1)} %slice.9), channel_id=1, source_target_pairs={{0,3},{1,0},{2,1},{3,2},{4,7},{5,4},{6,5},{7,6},{8,11},{9,8},{10,9... | collective-permute-start | bytes 1572872 | tf_op jit(solution)/shard_map/ppermute | solution.py:222
  87.8 0.8 copy-start.11
  99.5 6.3 %collective-permute-start.8 = (bf16[512,1024]{1,0:T(8,128)(2,1)S(1)}, bf16[512,1024]{1,0:T(8,128)(2,1)S(1)}, u32[]{:S(2)}, u32[]{:S(2)}) collective-permute-start(bf16[512,1024]{1,0:T(8,128)(2,1)S(1)} %get-tuple-element.37), channel_id=1, source_target_pairs={{0,8},{8,0},{1,9},{9,1},{2,10},{10,2},{3,11},{11,3},{4,12},{12,4},... | collective-permute-start | bytes 3145736 | tf_op jit(solution)/shard_map/ppermute | solution.py:214
  107.3 39.1 %all-to-all-start.2 = ((bf16[32,16,1024]{2,1,0:T(8,128)(2,1)}), bf16[32,16,1024]{2,1,0:T(8,128)(2,1)}, u32[]{:S(2)}, u32[]{:S(2)}) async-start(bf16[32,16,1024]{2,1,0:T(8,128)(2,1)} %bitcast.74), calls=%async_computation.2 | async-start | bytes 2097152 | tf_op jit(solution)/shard_map/all_to_all | solution.py:262
  119.4 6.8 %copy-start.4 = (bf16[32,16,1024]{2,1,0:T(8,128)(2,1)S(1)}, bf16[32,16,1024]{2,1,0:T(8,128)(2,1)}, u32[]{:S(2)}) copy-start(bf16[32,16,1024]{2,1,0:T(8,128)(2,1)} %copy-done.3) | copy-start | bytes 3145732
  119.4 9.3 %copy-start.2 = (bf16[32,16,1024]{2,1,0:T(8,128)(2,1)S(1)}, bf16[32,16,1024]{2,1,0:T(8,128)(2,1)}, u32[]{:S(2)}) copy-start(bf16[32,16,1024]{2,1,0:T(8,128)(2,1)} %copy-done.1) | copy-start | bytes 3145732
  121.7 8.9 %collective-permute-start.11 = (bf16[32,16,1024]{2,1,0:T(8,128)(2,1)S(1)}, bf16[32,16,1024]{2,1,0:T(8,128)(2,1)S(1)}, u32[]{:S(2)}, u32[]{:S(2)}) collective-permute-start(bf16[32,16,1024]{2,1,0:T(8,128)(2,1)S(1)} %constant_dynamic-update-slice_fusion.refs_2_), channel_id=1, source_target_pairs={{0,8},{8,0},{1,9},{9,1},{2,10},{10,2},{3,11},{11,3},{4,12},{12,4},... | collective-permute-start | bytes 3145736 | tf_op jit(solution)/shard_map/ppermute | solution.py:214
  124.3 6.3 %collective-permute-start.9 = (bf16[32,16,1024]{2,1,0:T(8,128)(2,1)S(1)}, bf16[32,16,1024]{2,1,0:T(8,128)(2,1)S(1)}, u32[]{:S(2)}, u32[]{:S(2)}) collective-permute-start(bf16[32,16,1024]{2,1,0:T(8,128)(2,1)S(1)} %all-to-all-done.refs_0_), channel_id=1, source_target_pairs={{0,8},{8,0},{1,9},{9,1},{2,10},{10,2},{3,11},{11,3},{4,12},{12,4},... | collective-permute-start | bytes 3145736 | tf_op jit(solution)/shard_map/ppermute | solution.py:214
  126.2 4.7 %collective-permute-start.10 = (bf16[32,16,1024]{2,1,0:T(8,128)(2,1)S(1)}, bf16[32,16,1024]{2,1,0:T(8,128)(2,1)S(1)}, u32[]{:S(2)}, u32[]{:S(2)}) collective-permute-start(bf16[32,16,1024]{2,1,0:T(8,128)(2,1)S(1)} %copy-done.4), channel_id=1, source_target_pairs={{0,8},{8,0},{1,9},{9,1},{2,10},{10,2},{3,11},{11,3},{4,12},{12,4},... | collective-permute-start | bytes 3145736 | tf_op jit(solution)/shard_map/ppermute | solution.py:214
  128.7 4.6 %collective-permute-start.12 = (bf16[32,16,1024]{2,1,0:T(8,128)(2,1)S(1)}, bf16[32,16,1024]{2,1,0:T(8,128)(2,1)S(1)}, u32[]{:S(2)}, u32[]{:S(2)}) collective-permute-start(bf16[32,16,1024]{2,1,0:T(8,128)(2,1)S(1)} %copy-done.2), channel_id=1, source_target_pairs={{0,8},{8,0},{1,9},{9,1},{2,10},{10,2},{3,11},{11,3},{4,12},{12,4},... | collective-permute-start | bytes 3145736 | tf_op jit(solution)/shard_map/ppermute | solution.py:214
  133.2 2.2 %copy-start.6 = (f32[16,256,256]{2,1,0:T(8,128)S(1)}, f32[16,256,256]{2,1,0:T(8,128)}, u32[]{:S(2)}) copy-start(f32[16,256,256]{2,1,0:T(8,128)} %get-tuple-element.43.attention_ref) | copy-start | bytes 12582916
  140.5 1.4 copy-start.5
  146.4 31.1 %all-to-all-start.3 = ((bf16[32,8,1024]{2,1,0:T(8,128)(2,1)}), bf16[32,8,1024]{2,1,0:T(8,128)(2,1)S(1)}, u32[]{:S(2)}, u32[]{:S(2)}) async-start(bf16[32,8,1024]{2,1,0:T(8,128)(2,1)} %bitcast.25), calls=%async_computation.3 | async-start | bytes 1048576 | tf_op jit(solution)/shard_map/all_to_all | solution.py:268
  154.9 5.4 %collective-permute-start.13 = (f32[16,1024]{1,0:T(8,128)S(1)}, f32[16,1024]{1,0:T(8,128)S(1)}, u32[]{:S(2)}, u32[]{:S(2)}) collective-permute-start(f32[16,1024]{1,0:T(8,128)S(1)} %broadcast_multiply_fusion), channel_id=1, source_target_pairs={{0,1},{1,0},{2,3},{3,2},{4,5},{5,4},{6,7},{7,6},{8,9},{9,8},{10,11... | collective-permute-start | bytes 196616 | tf_op jit(solution)/shard_map/ppermute | solution.py:232
  160.3 6.8 %collective-permute-start.14 = (f32[16,1024]{1,0:T(8,128)S(1)}, f32[16,1024]{1,0:T(8,128)S(1)}, u32[]{:S(2)}, u32[]{:S(2)}) collective-permute-start(f32[16,1024]{1,0:T(8,128)S(1)} %fusion.8), channel_id=1, source_target_pairs={{0,2},{1,3},{2,0},{3,1},{4,6},{5,7},{6,4},{7,5},{8,10},{9,11},{10,... | collective-permute-start | bytes 196616 | tf_op jit(solution)/shard_map/ppermute | solution.py:232
  167.1 9.7 %collective-permute-start.15 = (f32[16,1024]{1,0:T(8,128)S(1)}, f32[16,1024]{1,0:T(8,128)S(1)}, u32[]{:S(2)}, u32[]{:S(2)}) collective-permute-start(f32[16,1024]{1,0:T(8,128)S(1)} %add.38), channel_id=1, source_target_pairs={{0,4},{4,0},{1,5},{5,1},{2,6},{6,2},{3,7},{7,3},{8,12},{12,8},{9,1... | collective-permute-start | bytes 196616 | tf_op jit(solution)/shard_map/ppermute | solution.py:233

commit v6 on v5

--- a/solution.py
+++ b/solution.py
@@ -158,7 +158,7 @@
             + [pl.BlockSpec((16, 16, SLICE), lambda i, s: (i, 0, 3))] * 8,
             out_specs=pl.BlockSpec((3, 2 * SLICE, ROWS), lambda i, s: (0, i, 0)),
         ),
-        out_shape=pltpu.HBM((3, D, ROWS), jnp.bfloat16),
+        out_shape=jax.ShapeDtypeStruct((3, D, ROWS), jnp.bfloat16),
         compiler_params=pltpu.CompilerParams(vmem_limit_bytes=16 * 2**20),
         cost_estimate=pl.CostEstimate(
             flops=3 * 10**9, bytes_accessed=10 * 2**20, transcendentals=0
@@ -241,21 +241,12 @@
         (columns, query_rows, key_rows, value_rows, upstream)
     )
     plane = lax.all_to_all(columns, PLANE_AXES, 0, 0, tiled=True)
-    core = lax.axis_index("c")
-
-    def both_frames(rows):
-        rows = rows.reshape(CLIP_LEN // 2, 2, PATCH_BLOCK, D)
-        mine = lax.dynamic_index_in_dim(rows, core, 1, keepdims=False)
-        other = swap_cores(lax.dynamic_index_in_dim(rows, 1 - core, 1, keepdims=False))
-        return jnp.stack(
-            [jnp.where(core == 0, mine, other), jnp.where(core == 0, other, mine)], axis=1
-        )
-
     sent = jnp.concatenate(
-        [both_frames(a) for a in (query_rows, key_rows, value_rows, upstream)], axis=3
+        [a.reshape(CLIP_LEN, PATCH_BLOCK, D) for a in (query_rows, key_rows, value_rows, upstream)],
+        axis=2,
     )
     sent, plane = lax.optimization_barrier((sent, plane))
-    moved = lax.all_to_all(sent, ("yl", "zl"), 0, 0, tiled=True).reshape(ROWS, 4 * D)
+    moved = lax.all_to_all(sent, CLIP_AXES, 0, 0, tiled=True).reshape(ROWS, 4 * D)
     moved, own = lax.optimization_barrier((moved, spread_x(plane)))
     attention, keep, send = forward_call(place, moved)
     attention, share, own = lax.optimization_barrier((attention, sum_cores(keep, send), own))

time: 181 us -> 179 us (0.989)
  waiting for transfers between devices: 54.1 us -> 74.5 us
  starting transfers between devices: 88.9 us -> 73.6 us
  local copies, waits for them, and re-layouts: 12.5 us -> 9.36 us
  other arithmetic: 8.21 us -> 5.15 us
    all_to_all x1, waiting for transfers between devices: 9.89 us -> 25.1 us  [on_device(): plane = lax.all_to_all(columns, PLANE_AXES, 0, 0, tiled=True)]
    ppermute x9 -> x5, starting transfers between devices: 21.9 us -> 11.6 us  [swap_cores(): return lax.ppermute(block, 'c', ring(2, 1))]
    all_to_all x1, starting transfers between devices: 12.1 us -> 5.44 us  [on_device(): lax.all_to_all(share.reshape(32, 16, D), PLANE_AXES, 0, 0, tiled=True)]
    another operation x6 -> x0, other arithmetic: 3.13 us -> none  [both_frames(): jnp.stack([jnp.where(core == 0, mine, other), jnp.where(core == 0, other,...]
    squeeze x4 -> x0, local copies, waits for them, and re-layouts: 2.92 us -> none  [both_frames(): lax.dynamic_index_in_dim(rows, 1 - core, 1, keepdims=False)]
    all_to_all x1, waiting for transfers between devices: 0.67 us -> 2.91 us  [on_device(): lax.all_to_all(share.reshape(32, 16, D), PLANE_AXES, 0, 0, tiled=True)]
    unnamed x26 -> x22, local copies, waits for them, and re-layouts: 6.52 us -> 4.48 us
    all_to_all x1, starting transfers between devices: 5.44 us -> 7.44 us  [on_device(): lax.all_to_all(sent, CLIP_AXES, 0, 0, tiled=True).reshape(ROWS, 4 * D)]
  transfers between devices with their start and end apart: 20 -> 16, of which waited for: 12 -> 12; matrix products, arithmetic and copies ran while one was open for 7% -> 4% of each run, Pallas kernels for 5% -> 5%
where the time goes in v6:
time: 179 us; the launch traced here: 176 us
  waiting for transfers between devices  74.5 us (42%)
  starting transfers between devices  73.6 us (41%)
  Pallas kernels  12.7 us (7%)
  local copies, waits for them, and re-layouts  9.36 us (5%)
  other arithmetic  5.15 us (3%)
    all_to_all x1, waiting for transfers between devices, on_device(): plane = lax.all_to_all(columns, PLANE_AXES, 0, 0, tiled=True)  25.1 us
    ppermute x1, waiting for transfers between devices, spread_x(): before = lax.ppermute(plane, 'x', ring(4, 1))  21.1 us
    all_to_all x1, starting transfers between devices, on_device(): plane = lax.all_to_all(columns, PLANE_AXES, 0, 0, tiled=True)  13.5 us
    ppermute x5, starting transfers between devices, swap_cores(): return lax.ppermute(block, 'c', ring(2, 1))  11.6 us
    ppermute x1, waiting for transfers between devices, spread_x(): far_a = lax.ppermute(before[:half], 'x', ring(4, 1))  8.03 us
    ppermute x1, starting transfers between devices, sum_groups(): return share + lax.ppermute(share, 'zh', ring(2, 1))  7.94 us
    ppermute x2, starting transfers between devices, sum_groups(): share = share + lax.ppermute(share, 'x', [(i, i ^ bit) for i in range(4)])  7.79 us
    all_to_all x1, starting transfers between devices, on_device(): lax.all_to_all(sent, CLIP_AXES, 0, 0, tiled=True).reshape(ROWS, 4 * D)  7.44 us
  transfers between devices with their start and end apart: 16, of which 12 were waited for; matrix products, arithmetic and copies ran while one was open for 4% of the time, Pallas kernels for 5%

profile of v6, /device:TPU:1, one launch (start us, length us, event | category | flops | bytes accessed | tf_op | source)
XLA Modules:
  0.0 176.3 jit_solution(16172456743330482615)
XLA Ops:
  0.6 0.0 copy-start
  0.6 0.0 copy-start.6
  0.7 0.0 copy-start.7
  0.7 0.0 copy-start.8
  0.7 0.0 copy-start.9
  0.7 0.9 constant_dynamic-slice_fusion
  1.5 0.0 copy-done
  1.6 1.1 broadcast_in_dim.2
  2.7 13.5 %all-to-all-start = ((bf16[32,16,1024]{2,1,0:T(8,128)(2,1)}), bf16[32,16,1024]{2,1,0:T(8,128)(2,1)S(1)}, u32[]{:S(2)}, u32[]{:S(2)}) async-start(bf16[32,16,1024]{2,1,0:T(8,128)(2,1)} %broadcast_in_dim.2), calls=%async_computation | async-start | bytes 2097152 | tf_op jit(solution)/shard_map/all_to_all | solution.py:243
  16.1 0.0 copy-done.6
  16.2 0.0 copy-done.7
  16.2 0.0 copy-done.8
  16.2 0.0 copy-done.9
  16.2 1.5 pad_maximum_fusion
  17.7 25.1 %all-to-all-done.refs_0_ = bf16[32,16,1024]{2,1,0:T(8,128)(2,1)S(1)} async-done(((bf16[32,16,1024]{2,1,0:T(8,128)(2,1)}), bf16[32,16,1024]{2,1,0:T(8,128)(2,1)S(1)}, u32[]{:S(2)}, u32[]{:S(2)}) %all-to-all-start) | async-done | bytes 1048608 | tf_op jit(solution)/shard_map/all_to_all | solution.py:243
  42.8 7.4 %all-to-all-start.1 = ((bf16[32,8,4096]{2,1,0:T(8,128)(2,1)}), bf16[32,8,4096]{2,1,0:T(8,128)(2,1)S(1)}, u32[]{:S(2)}, u32[]{:S(2)}) async-start(bf16[32,8,4096]{2,1,0:T(8,128)(2,1)} %pad_maximum_fusion), calls=%async_computation.1 | async-start | bytes 4194304 | tf_op jit(solution)/shard_map/all_to_all | solution.py:249
  50.2 3.1 %collective-permute-start.1 = (bf16[32,16,1024]{2,1,0:T(8,128)(2,1)S(1)}, bf16[32,16,1024]{2,1,0:T(8,128)(2,1)S(1)}, u32[]{:S(2)}, u32[]{:S(2)}) collective-permute-start(bf16[32,16,1024]{2,1,0:T(8,128)(2,1)S(1)} %all-to-all-done.refs_0_), channel_id=1, source_target_pairs={{0,1},{1,2},{2,3},{3,0},{4,5},{5,6},{6,7},{7,4},{8,9},{9,10},{10,1... | collective-permute-start | bytes 3145736 | tf_op jit(solution)/shard_map/ppermute | solution.py:220
  53.4 3.4 %collective-permute-start = (bf16[32,16,1024]{2,1,0:T(8,128)(2,1)S(1)}, bf16[32,16,1024]{2,1,0:T(8,128)(2,1)S(1)}, u32[]{:S(2)}, u32[]{:S(2)}) collective-permute-start(bf16[32,16,1024]{2,1,0:T(8,128)(2,1)S(1)} %all-to-all-done.refs_0_), channel_id=1, source_target_pairs={{0,3},{1,0},{2,1},{3,2},{4,7},{5,4},{6,5},{7,6},{8,11},{9,8},{10,9... | collective-permute-start | bytes 3145736 | tf_op jit(solution)/shard_map/ppermute | solution.py:219
  56.7 21.1 %collective-permute-done.1.refs_3_ = bf16[32,16,1024]{2,1,0:T(8,128)(2,1)S(1)} collective-permute-done((bf16[32,16,1024]{2,1,0:T(8,128)(2,1)S(1)}, bf16[32,16,1024]{2,1,0:T(8,128)(2,1)S(1)}, u32[]{:S(2)}, u32[]{:S(2)}) %collective-permute-start.1) | collective-permute-done | bytes 1048608 | tf_op jit(solution)/shard_map/ppermute | solution.py:220
  77.9 0.9 slice.8
  78.8 1.9 %collective-permute-start.2 = (bf16[16,16,1024]{2,1,0:T(8,128)(2,1)}, bf16[16,16,1024]{2,1,0:T(8,128)(2,1)}, u32[]{:S(2)}, u32[]{:S(2)}) collective-permute-start(bf16[16,16,1024]{2,1,0:T(8,128)(2,1)} %slice.8), channel_id=1, source_target_pairs={{0,1},{1,2},{2,3},{3,0},{4,5},{5,6},{6,7},{7,4},{8,9},{9,10},{10,1... | collective-permute-start | bytes 1572872 | tf_op jit(solution)/shard_map/ppermute | solution.py:221
  80.7 0.0 collective-permute-done.refs_1_
  80.7 0.0 copy-done.1
  80.7 0.0 copy-start.3
  80.7 0.9 slice.9
  81.6 0.2 copy-done.3
  81.9 4.6 %collective-permute-start.3 = (bf16[16,16,1024]{2,1,0:T(8,128)(2,1)}, bf16[16,16,1024]{2,1,0:T(8,128)(2,1)}, u32[]{:S(2)}, u32[]{:S(2)}) collective-permute-start(bf16[16,16,1024]{2,1,0:T(8,128)(2,1)} %slice.9), channel_id=1, source_target_pairs={{0,3},{1,0},{2,1},{3,2},{4,7},{5,4},{6,5},{7,6},{8,11},{9,8},{10,9... | collective-permute-start | bytes 1572872 | tf_op jit(solution)/shard_map/ppermute | solution.py:222
  86.4 0.1 pad_add_fusion.place
  86.5 8.0 %collective-permute-done.2 = bf16[16,16,1024]{2,1,0:T(8,128)(2,1)} collective-permute-done((bf16[16,16,1024]{2,1,0:T(8,128)(2,1)}, bf16[16,16,1024]{2,1,0:T(8,128)(2,1)}, u32[]{:S(2)}, u32[]{:S(2)}) %collective-permute-start.2) | collective-permute-done | bytes 524320 | tf_op jit(solution)/shard_map/ppermute | solution.py:221
  94.6 2.1 %collective-permute-done.3 = bf16[16,16,1024]{2,1,0:T(8,128)(2,1)} collective-permute-done((bf16[16,16,1024]{2,1,0:T(8,128)(2,1)}, bf16[16,16,1024]{2,1,0:T(8,128)(2,1)}, u32[]{:S(2)}, u32[]{:S(2)}) %collective-permute-start.3) | collective-permute-done | bytes 524320 | tf_op jit(solution)/shard_map/ppermute | solution.py:222
  96.6 4.3 %all-to-all-done.1 = bf16[32,8,4096]{2,1,0:T(8,128)(2,1)S(1)} async-done(((bf16[32,8,4096]{2,1,0:T(8,128)(2,1)}), bf16[32,8,4096]{2,1,0:T(8,128)(2,1)S(1)}, u32[]{:S(2)}, u32[]{:S(2)}) %all-to-all-start.1) | async-done | bytes 2097184 | tf_op jit(solution)/shard_map/all_to_all | solution.py:249
  101.0 4.6 %attention_and_weight_grad.1 = (f32[16,256,256]{2,1,0:T(8,128)}, bf16[512,1024]{1,0:T(8,128)(2,1)S(1)}, bf16[512,1024]{1,0:T(8,128)(2,1)S(1)}) custom-call(s32[2]{0:T(128)S(1)} %pad_add_fusion.place, bf16[256,4096]{1,0:T(8,128)(2,1)S(1)} %bitcast.11, bf16[256,4096]{1,0:T(8,128)(2,1)S(1)} %bitcast.12, bf16[256,4096]{1,0:T(8,128)(2,1)S(1)} %bitcast.13, ...), custom_call_target="tpu_custom_call" | custom-call | flops 2000000000 | bytes 8388608 | tf_op jit(solution)/shard_map/attention_and_weight_grad/pallas_call | solution.py:86
  105.6 2.8 %collective-permute-start.4 = (bf16[512,1024]{1,0:T(8,128)(2,1)S(1)}, bf16[512,1024]{1,0:T(8,128)(2,1)S(1)}, u32[]{:S(2)}, u32[]{:S(2)}) collective-permute-start(bf16[512,1024]{1,0:T(8,128)(2,1)S(1)} %get-tuple-element.37), channel_id=1, source_target_pairs={{0,8},{8,0},{1,9},{9,1},{2,10},{10,2},{3,11},{11,3},{4,12},{12,4},... | collective-permute-start | bytes 3145736 | tf_op jit(solution)/shard_map/ppermute | solution.py:214
  108.3 2.3 %collective-permute-done.4 = bf16[512,1024]{1,0:T(8,128)(2,1)S(1)} collective-permute-done((bf16[512,1024]{1,0:T(8,128)(2,1)S(1)}, bf16[512,1024]{1,0:T(8,128)(2,1)S(1)}, u32[]{:S(2)}, u32[]{:S(2)}) %collective-permute-start.4) | collective-permute-done | bytes 1048608 | tf_op jit(solution)/shard_map/ppermute | solution.py:214
  110.6 1.5 add_convert_fusion
  112.1 5.4 %all-to-all-start.2 = ((bf16[32,16,1024]{2,1,0:T(8,128)(2,1)}), bf16[32,16,1024]{2,1,0:T(8,128)(2,1)}, u32[]{:S(2)}, u32[]{:S(2)}) async-start(bf16[32,16,1024]{2,1,0:T(8,128)(2,1)} %bitcast.20), calls=%async_computation.2 | async-start | bytes 2097152 | tf_op jit(solution)/shard_map/all_to_all | solution.py:253
  117.6 0.0 copy-start.4
  117.6 0.0 copy-start.2
  117.6 1.2 constant_dynamic-update-slice_fusion.1
  118.8 1.1 constant_dynamic-update-slice_fusion.refs_2_
  119.9 2.6 %collective-permute-start.7 = (bf16[32,16,1024]{2,1,0:T(8,128)(2,1)S(1)}, bf16[32,16,1024]{2,1,0:T(8,128)(2,1)S(1)}, u32[]{:S(2)}, u32[]{:S(2)}) collective-permute-start(bf16[32,16,1024]{2,1,0:T(8,128)(2,1)S(1)} %constant_dynamic-update-slice_fusion.refs_2_), channel_id=1, source_target_pairs={{0,8},{8,0},{1,9},{9,1},{2,10},{10,2},{3,11},{11,3},{4,12},{12,4},... | collective-permute-start | bytes 3145736 | tf_op jit(solution)/shard_map/ppermute | solution.py:214
  122.5 1.9 %collective-permute-start.5 = (bf16[32,16,1024]{2,1,0:T(8,128)(2,1)S(1)}, bf16[32,16,1024]{2,1,0:T(8,128)(2,1)S(1)}, u32[]{:S(2)}, u32[]{:S(2)}) collective-permute-start(bf16[32,16,1024]{2,1,0:T(8,128)(2,1)S(1)} %all-to-all-done.refs_0_), channel_id=1, source_target_pairs={{0,8},{8,0},{1,9},{9,1},{2,10},{10,2},{3,11},{11,3},{4,12},{12,4},... | collective-permute-start | bytes 3145736 | tf_op jit(solution)/shard_map/ppermute | solution.py:214
  124.4 0.0 copy-done.4
  124.4 2.4 %collective-permute-start.6 = (bf16[32,16,1024]{2,1,0:T(8,128)(2,1)S(1)}, bf16[32,16,1024]{2,1,0:T(8,128)(2,1)S(1)}, u32[]{:S(2)}, u32[]{:S(2)}) collective-permute-start(bf16[32,16,1024]{2,1,0:T(8,128)(2,1)S(1)} %copy-done.4), channel_id=1, source_target_pairs={{0,8},{8,0},{1,9},{9,1},{2,10},{10,2},{3,11},{11,3},{4,12},{12,4},... | collective-permute-start | bytes 3145736 | tf_op jit(solution)/shard_map/ppermute | solution.py:214
  126.8 1.9 %collective-permute-start.8 = (bf16[32,16,1024]{2,1,0:T(8,128)(2,1)S(1)}, bf16[32,16,1024]{2,1,0:T(8,128)(2,1)S(1)}, u32[]{:S(2)}, u32[]{:S(2)}) collective-permute-start(bf16[32,16,1024]{2,1,0:T(8,128)(2,1)S(1)} %copy-done.2), channel_id=1, source_target_pairs={{0,8},{8,0},{1,9},{9,1},{2,10},{10,2},{3,11},{11,3},{4,12},{12,4},... | collective-permute-start | bytes 3145736 | tf_op jit(solution)/shard_map/ppermute | solution.py:214
  128.8 0.0 collective-permute-done.7.refs_6_
  128.8 0.0 collective-permute-done.5.refs_4_
  128.8 0.3 collective-permute-done.6.refs_5_
  129.1 2.3 %collective-permute-done.8.refs_7_ = bf16[32,16,1024]{2,1,0:T(8,128)(2,1)S(1)} collective-permute-done((bf16[32,16,1024]{2,1,0:T(8,128)(2,1)S(1)}, bf16[32,16,1024]{2,1,0:T(8,128)(2,1)S(1)}, u32[]{:S(2)}, u32[]{:S(2)}) %collective-permute-start.8) | collective-permute-done | bytes 1048608 | tf_op jit(solution)/shard_map/ppermute | solution.py:214
  131.4 2.2 %copy-done.5 = f32[16,256,256]{2,1,0:T(8,128)S(1)} copy-done((f32[16,256,256]{2,1,0:T(8,128)S(1)}, f32[16,256,256]{2,1,0:T(8,128)}, u32[]{:S(2)}) %copy-start.5) | copy-done | bytes 4194328
  133.6 4.3 %attention_grads.1 = bf16[3,1024,256]{2,1,0:T(8,128)(2,1)S(1)} custom-call(s32[2]{0:T(128)S(1)} %pad_add_fusion.place, f32[16,256,256]{2,1,0:T(8,128)S(1)} %copy-done.5, bf16[256,4096]{1,0:T(8,128)(2,1)S(1)} %bitcast.15, bf16[256,4096]{1,0:T(8,128)(2,1)S(1)} %bitcast.16, bf16[256,4096]{1,0:T(8,128)(2,1)S(1)} %bitcast.17, bf16[256,4096]{1,0:T(8,128)(2,1)S(1)} %bitcast.18, ...), custom_call_target="tpu_custom_call" | custom-call | flops 3000000000 | bytes 10485760 | tf_op jit(solution)/shard_map/attention_grads/pallas_call | solution.py:146
  137.8 3.8 %input_projection.1 = bf16[256,1024]{1,0:T(8,128)(2,1)} custom-call(s32[2]{0:T(128)S(1)} %pad_add_fusion.place, bf16[3072,256]{1,0:T(8,128)(2,1)S(1)} %bitcast.19, bf16[32,16,1024]{2,1,0:T(8,128)(2,1)S(1)} %all-to-all-done.refs_0_, bf16[32,16,1024]{2,1,0:T(8,128)(2,1)S(1)} %copy-done.4, bf16[32,16,1024]{2,1,0:T(8,128)(2,1)S(1)} %constant_dynamic-update-slice_fusion.refs_2_, ...), custom_call_target="tpu_custom_call" | custom-call | flops 2000000000 | bytes 8388608 | tf_op jit(solution)/shard_map/input_projection/pallas_call | solution.py:183
  141.7 2.9 %all-to-all-done.2 = bf16[32,16,1024]{2,1,0:T(8,128)(2,1)} async-done(((bf16[32,16,1024]{2,1,0:T(8,128)(2,1)}), bf16[32,16,1024]{2,1,0:T(8,128)(2,1)}, u32[]{:S(2)}, u32[]{:S(2)}) %all-to-all-start.2) | async-done | bytes 1048608 | tf_op jit(solution)/shard_map/all_to_all | solution.py:253
  144.6 7.0 %all-to-all-start.3 = ((bf16[32,8,1024]{2,1,0:T(8,128)(2,1)}), bf16[32,8,1024]{2,1,0:T(8,128)(2,1)S(1)}, u32[]{:S(2)}, u32[]{:S(2)}) async-start(bf16[32,8,1024]{2,1,0:T(8,128)(2,1)} %bitcast.8), calls=%async_computation.3 | async-start | bytes 1048576 | tf_op jit(solution)/shard_map/all_to_all | solution.py:259
  151.6 1.4 convert_reduce_fusion
  153.0 3.1 %collective-permute-start.9 = (f32[16,1024]{1,0:T(8,128)S(1)}, f32[16,1024]{1,0:T(8,128)S(1)}, u32[]{:S(2)}, u32[]{:S(2)}) collective-permute-start(f32[16,1024]{1,0:T(8,128)S(1)} %broadcast_multiply_fusion), channel_id=1, source_target_pairs={{0,1},{1,0},{2,3},{3,2},{4,5},{5,4},{6,7},{7,6},{8,9},{9,8},{10,11... | collective-permute-start | bytes 196616 | tf_op jit(solution)/shard_map/ppermute | solution.py:232
  156.1 2.2 %collective-permute-done.9 = f32[16,1024]{1,0:T(8,128)S(1)} collective-permute-done((f32[16,1024]{1,0:T(8,128)S(1)}, f32[16,1024]{1,0:T(8,128)S(1)}, u32[]{:S(2)}, u32[]{:S(2)}) %collective-permute-start.9) | collective-permute-done | bytes 65568 | tf_op jit(solution)/shard_map/ppermute | solution.py:232
  158.4 4.7 %collective-permute-start.10 = (f32[16,1024]{1,0:T(8,128)S(1)}, f32[16,1024]{1,0:T(8,128)S(1)}, u32[]{:S(2)}, u32[]{:S(2)}) collective-permute-start(f32[16,1024]{1,0:T(8,128)S(1)} %fusion), channel_id=1, source_target_pairs={{0,2},{1,3},{2,0},{3,1},{4,6},{5,7},{6,4},{7,5},{8,10},{9,11},{10,... | collective-permute-start | bytes 196616 | tf_op jit(solution)/shard_map/ppermute | solution.py:232
  163.0 2.1 %collective-permute-done.10 = f32[16,1024]{1,0:T(8,128)S(1)} collective-permute-done((f32[16,1024]{1,0:T(8,128)S(1)}, f32[16,1024]{1,0:T(8,128)S(1)}, u32[]{:S(2)}, u32[]{:S(2)}) %collective-permute-start.10) | collective-permute-done | bytes 65568 | tf_op jit(solution)/shard_map/ppermute | solution.py:232
  165.2 7.9 %collective-permute-start.11 = (f32[16,1024]{1,0:T(8,128)S(1)}, f32[16,1024]{1,0:T(8,128)S(1)}, u32[]{:S(2)}, u32[]{:S(2)}) collective-permute-start(f32[16,1024]{1,0:T(8,128)S(1)} %add.22), channel_id=1, source_target_pairs={{0,4},{4,0},{1,5},{5,1},{2,6},{6,2},{3,7},{7,3},{8,12},{12,8},{9,1... | collective-permute-start | bytes 196616 | tf_op jit(solution)/shard_map/ppermute | solution.py:233
  173.1 1.7 collective-permute-done.11
  174.9 0.6 add.23
  175.5 0.0 all-to-all-done.3
  175.5 0.8 copy.10
  (8 shorter events, 0.0 us)
Async XLA Ops:
  0.6 0.9 copy-start
  0.6 15.5 %copy-start.6 = (bf16[1,1,256,1024]{3,2,1,0:T(8,128)(2,1)S(1)}, bf16[1,1,256,1024]{3,2,1,0:T(8,128)(2,1)}, u32[]{:S(2)}) copy-start(bf16[1,1,256,1024]{3,2,1,0:T(8,128)(2,1)} %param.9) | copy-start | bytes 1572868
  0.7 15.5 %copy-start.7 = (bf16[1,1,256,1024]{3,2,1,0:T(8,128)(2,1)S(1)}, bf16[1,1,256,1024]{3,2,1,0:T(8,128)(2,1)}, u32[]{:S(2)}) copy-start(bf16[1,1,256,1024]{3,2,1,0:T(8,128)(2,1)} %param.8) | copy-start | bytes 1572868
  0.7 15.5 %copy-start.8 = (bf16[1,1,256,1024]{3,2,1,0:T(8,128)(2,1)S(1)}, bf16[1,1,256,1024]{3,2,1,0:T(8,128)(2,1)}, u32[]{:S(2)}) copy-start(bf16[1,1,256,1024]{3,2,1,0:T(8,128)(2,1)} %param.7) | copy-start | bytes 1572868
  0.7 15.5 %copy-start.9 = (bf16[1,1,256,1024]{3,2,1,0:T(8,128)(2,1)S(1)}, bf16[1,1,256,1024]{3,2,1,0:T(8,128)(2,1)}, u32[]{:S(2)}) copy-start(bf16[1,1,256,1024]{3,2,1,0:T(8,128)(2,1)} %param.6) | copy-start | bytes 1572868
  2.7 40.1 %all-to-all-start = ((bf16[32,16,1024]{2,1,0:T(8,128)(2,1)}), bf16[32,16,1024]{2,1,0:T(8,128)(2,1)S(1)}, u32[]{:S(2)}, u32[]{:S(2)}) async-start(bf16[32,16,1024]{2,1,0:T(8,128)(2,1)} %broadcast_in_dim.2), calls=%async_computation | async-start | bytes 2097152 | tf_op jit(solution)/shard_map/all_to_all | solution.py:243
  42.8 58.2 %all-to-all-start.1 = ((bf16[32,8,4096]{2,1,0:T(8,128)(2,1)}), bf16[32,8,4096]{2,1,0:T(8,128)(2,1)S(1)}, u32[]{:S(2)}, u32[]{:S(2)}) async-start(bf16[32,8,4096]{2,1,0:T(8,128)(2,1)} %pad_maximum_fusion), calls=%async_computation.1 | async-start | bytes 4194304 | tf_op jit(solution)/shard_map/all_to_all | solution.py:249
  50.2 27.6 %collective-permute-start.1 = (bf16[32,16,1024]{2,1,0:T(8,128)(2,1)S(1)}, bf16[32,16,1024]{2,1,0:T(8,128)(2,1)S(1)}, u32[]{:S(2)}, u32[]{:S(2)}) collective-permute-start(bf16[32,16,1024]{2,1,0:T(8,128)(2,1)S(1)} %all-to-all-done.refs_0_), channel_id=1, source_target_pairs={{0,1},{1,2},{2,3},{3,0},{4,5},{5,6},{6,7},{7,4},{8,9},{9,10},{10,1... | collective-permute-start | bytes 3145736 | tf_op jit(solution)/shard_map/ppermute | solution.py:220
  53.4 27.3 %collective-permute-start = (bf16[32,16,1024]{2,1,0:T(8,128)(2,1)S(1)}, bf16[32,16,1024]{2,1,0:T(8,128)(2,1)S(1)}, u32[]{:S(2)}, u32[]{:S(2)}) collective-permute-start(bf16[32,16,1024]{2,1,0:T(8,128)(2,1)S(1)} %all-to-all-done.refs_0_), channel_id=1, source_target_pairs={{0,3},{1,0},{2,1},{3,2},{4,7},{5,4},{6,5},{7,6},{8,11},{9,8},{10,9... | collective-permute-start | bytes 3145736 | tf_op jit(solution)/shard_map/ppermute | solution.py:219
  77.9 2.8 %copy-start.1 = (bf16[32,16,1024]{2,1,0:T(8,128)(2,1)}, bf16[32,16,1024]{2,1,0:T(8,128)(2,1)S(1)}, u32[]{:S(2)}) copy-start(bf16[32,16,1024]{2,1,0:T(8,128)(2,1)S(1)} %collective-permute-done.1.refs_3_) | copy-start | bytes 3145732
  78.8 15.8 %collective-permute-start.2 = (bf16[16,16,1024]{2,1,0:T(8,128)(2,1)}, bf16[16,16,1024]{2,1,0:T(8,128)(2,1)}, u32[]{:S(2)}, u32[]{:S(2)}) collective-permute-start(bf16[16,16,1024]{2,1,0:T(8,128)(2,1)} %slice.8), channel_id=1, source_target_pairs={{0,1},{1,2},{2,3},{3,0},{4,5},{5,6},{6,7},{7,4},{8,9},{9,10},{10,1... | collective-permute-start | bytes 1572872 | tf_op jit(solution)/shard_map/ppermute | solution.py:221
  80.7 1.2 copy-start.3
  81.9 14.8 %collective-permute-start.3 = (bf16[16,16,1024]{2,1,0:T(8,128)(2,1)}, bf16[16,16,1024]{2,1,0:T(8,128)(2,1)}, u32[]{:S(2)}, u32[]{:S(2)}) collective-permute-start(bf16[16,16,1024]{2,1,0:T(8,128)(2,1)} %slice.9), channel_id=1, source_target_pairs={{0,3},{1,0},{2,1},{3,2},{4,7},{5,4},{6,5},{7,6},{8,11},{9,8},{10,9... | collective-permute-start | bytes 1572872 | tf_op jit(solution)/shard_map/ppermute | solution.py:222
  105.6 5.0 %collective-permute-start.4 = (bf16[512,1024]{1,0:T(8,128)(2,1)S(1)}, bf16[512,1024]{1,0:T(8,128)(2,1)S(1)}, u32[]{:S(2)}, u32[]{:S(2)}) collective-permute-start(bf16[512,1024]{1,0:T(8,128)(2,1)S(1)} %get-tuple-element.37), channel_id=1, source_target_pairs={{0,8},{8,0},{1,9},{9,1},{2,10},{10,2},{3,11},{11,3},{4,12},{12,4},... | collective-permute-start | bytes 3145736 | tf_op jit(solution)/shard_map/ppermute | solution.py:214
  112.1 32.5 %all-to-all-start.2 = ((bf16[32,16,1024]{2,1,0:T(8,128)(2,1)}), bf16[32,16,1024]{2,1,0:T(8,128)(2,1)}, u32[]{:S(2)}, u32[]{:S(2)}) async-start(bf16[32,16,1024]{2,1,0:T(8,128)(2,1)} %bitcast.20), calls=%async_computation.2 | async-start | bytes 2097152 | tf_op jit(solution)/shard_map/all_to_all | solution.py:253
  117.6 6.8 %copy-start.4 = (bf16[32,16,1024]{2,1,0:T(8,128)(2,1)S(1)}, bf16[32,16,1024]{2,1,0:T(8,128)(2,1)}, u32[]{:S(2)}) copy-start(bf16[32,16,1024]{2,1,0:T(8,128)(2,1)} %copy-done.3) | copy-start | bytes 3145732
  117.6 9.3 %copy-start.2 = (bf16[32,16,1024]{2,1,0:T(8,128)(2,1)S(1)}, bf16[32,16,1024]{2,1,0:T(8,128)(2,1)}, u32[]{:S(2)}) copy-start(bf16[32,16,1024]{2,1,0:T(8,128)(2,1)} %copy-done.1) | copy-start | bytes 3145732
  119.9 8.9 %collective-permute-start.7 = (bf16[32,16,1024]{2,1,0:T(8,128)(2,1)S(1)}, bf16[32,16,1024]{2,1,0:T(8,128)(2,1)S(1)}, u32[]{:S(2)}, u32[]{:S(2)}) collective-permute-start(bf16[32,16,1024]{2,1,0:T(8,128)(2,1)S(1)} %constant_dynamic-update-slice_fusion.refs_2_), channel_id=1, source_target_pairs={{0,8},{8,0},{1,9},{9,1},{2,10},{10,2},{3,11},{11,3},{4,12},{12,4},... | collective-permute-start | bytes 3145736 | tf_op jit(solution)/shard_map/ppermute | solution.py:214
  122.5 6.3 %collective-permute-start.5 = (bf16[32,16,1024]{2,1,0:T(8,128)(2,1)S(1)}, bf16[32,16,1024]{2,1,0:T(8,128)(2,1)S(1)}, u32[]{:S(2)}, u32[]{:S(2)}) collective-permute-start(bf16[32,16,1024]{2,1,0:T(8,128)(2,1)S(1)} %all-to-all-done.refs_0_), channel_id=1, source_target_pairs={{0,8},{8,0},{1,9},{9,1},{2,10},{10,2},{3,11},{11,3},{4,12},{12,4},... | collective-permute-start | bytes 3145736 | tf_op jit(solution)/shard_map/ppermute | solution.py:214
  124.4 4.7 %collective-permute-start.6 = (bf16[32,16,1024]{2,1,0:T(8,128)(2,1)S(1)}, bf16[32,16,1024]{2,1,0:T(8,128)(2,1)S(1)}, u32[]{:S(2)}, u32[]{:S(2)}) collective-permute-start(bf16[32,16,1024]{2,1,0:T(8,128)(2,1)S(1)} %copy-done.4), channel_id=1, source_target_pairs={{0,8},{8,0},{1,9},{9,1},{2,10},{10,2},{3,11},{11,3},{4,12},{12,4},... | collective-permute-start | bytes 3145736 | tf_op jit(solution)/shard_map/ppermute | solution.py:214
  126.8 4.6 %collective-permute-start.8 = (bf16[32,16,1024]{2,1,0:T(8,128)(2,1)S(1)}, bf16[32,16,1024]{2,1,0:T(8,128)(2,1)S(1)}, u32[]{:S(2)}, u32[]{:S(2)}) collective-permute-start(bf16[32,16,1024]{2,1,0:T(8,128)(2,1)S(1)} %copy-done.2), channel_id=1, source_target_pairs={{0,8},{8,0},{1,9},{9,1},{2,10},{10,2},{3,11},{11,3},{4,12},{12,4},... | collective-permute-start | bytes 3145736 | tf_op jit(solution)/shard_map/ppermute | solution.py:214
  131.4 2.2 %copy-start.5 = (f32[16,256,256]{2,1,0:T(8,128)S(1)}, f32[16,256,256]{2,1,0:T(8,128)}, u32[]{:S(2)}) copy-start(f32[16,256,256]{2,1,0:T(8,128)} %get-tuple-element.43.attention_ref) | copy-start | bytes 12582916
  144.6 30.9 %all-to-all-start.3 = ((bf16[32,8,1024]{2,1,0:T(8,128)(2,1)}), bf16[32,8,1024]{2,1,0:T(8,128)(2,1)S(1)}, u32[]{:S(2)}, u32[]{:S(2)}) async-start(bf16[32,8,1024]{2,1,0:T(8,128)(2,1)} %bitcast.8), calls=%async_computation.3 | async-start | bytes 1048576 | tf_op jit(solution)/shard_map/all_to_all | solution.py:259
  153.0 5.4 %collective-permute-start.9 = (f32[16,1024]{1,0:T(8,128)S(1)}, f32[16,1024]{1,0:T(8,128)S(1)}, u32[]{:S(2)}, u32[]{:S(2)}) collective-permute-start(f32[16,1024]{1,0:T(8,128)S(1)} %broadcast_multiply_fusion), channel_id=1, source_target_pairs={{0,1},{1,0},{2,3},{3,2},{4,5},{5,4},{6,7},{7,6},{8,9},{9,8},{10,11... | collective-permute-start | bytes 196616 | tf_op jit(solution)/shard_map/ppermute | solution.py:232
  158.4 6.8 %collective-permute-start.10 = (f32[16,1024]{1,0:T(8,128)S(1)}, f32[16,1024]{1,0:T(8,128)S(1)}, u32[]{:S(2)}, u32[]{:S(2)}) collective-permute-start(f32[16,1024]{1,0:T(8,128)S(1)} %fusion), channel_id=1, source_target_pairs={{0,2},{1,3},{2,0},{3,1},{4,6},{5,7},{6,4},{7,5},{8,10},{9,11},{10,... | collective-permute-start | bytes 196616 | tf_op jit(solution)/shard_map/ppermute | solution.py:232
  165.2 9.7 %collective-permute-start.11 = (f32[16,1024]{1,0:T(8,128)S(1)}, f32[16,1024]{1,0:T(8,128)S(1)}, u32[]{:S(2)}, u32[]{:S(2)}) collective-permute-start(f32[16,1024]{1,0:T(8,128)S(1)} %add.22), channel_id=1, source_target_pairs={{0,4},{4,0},{1,5},{5,1},{2,6},{6,2},{3,7},{7,3},{8,12},{12,8},{9,1... | collective-permute-start | bytes 196616 | tf_op jit(solution)/shard_map/ppermute | solution.py:233

commit v7 on v6

--- a/solution.py
+++ b/solution.py
@@ -227,10 +227,27 @@
     return (keep.astype(jnp.float32) + swap_cores(send).astype(jnp.float32)).astype(jnp.bfloat16)
 
 
-def sum_groups(share):
+def write_kernel(i_ref, o_ref):
+    o_ref[...] = i_ref[...]
+
+
+def write_out(rows):
+    block = pl.BlockSpec((64, D), lambda i: (i, 0))
+    return pl.pallas_call(
+        write_kernel,
+        grid=(4,),
+        in_specs=[block],
+        out_specs=block,
+        out_shape=jax.ShapeDtypeStruct(rows.shape, rows.dtype),
+        compiler_params=pltpu.CompilerParams(vmem_limit_bytes=8 * 2**20),
+        name="write_out",
+    )(rows)
+
+
+def sum_x(share):
     for bit in (1, 2):
         share = share + lax.ppermute(share, "x", [(i, i ^ bit) for i in range(4)])
-    return share + lax.ppermute(share, "zh", ring(2, 1))
+    return share
 
 
 def on_device(query_rows, key_rows, value_rows, upstream, input_weights, output_weight):
@@ -257,7 +274,11 @@
     result = projection_call(place, grads, pieces).reshape(CLIP_LEN, PATCH_BLOCK, D)
     result, share = lax.optimization_barrier((result, share))
     input_gradient = lax.all_to_all(result, CLIP_AXES, 0, 0, tiled=True)
-    weight_gradient = sum_groups(jnp.sum(share.astype(jnp.float32), axis=0) * factor)
+    share = sum_x(jnp.sum(share.astype(jnp.float32), axis=0) * factor)
+    other = lax.ppermute(share, "zh", ring(2, 1))
+    input_gradient = write_out(input_gradient.reshape(ROWS, D))
+    input_gradient, other = lax.optimization_barrier((input_gradient, other))
+    weight_gradient = share + other
     return (input_gradient.reshape(query_rows.shape), weight_gradient)
 
 

time: 179 us -> 178 us (level)
    unnamed x22 -> x21, local copies, waits for them, and re-layouts: 4.48 us -> 3.68 us
where the time goes in v7:
time: 178 us; the launch traced here: 176 us
  starting transfers between devices  73.6 us (41%)
  waiting for transfers between devices  73.1 us (41%)
  Pallas kernels  14.1 us (8%)
  local copies, waits for them, and re-layouts  8.57 us (5%)
  other arithmetic  5.15 us (3%)
    all_to_all x1, waiting for transfers between devices, on_device(): plane = lax.all_to_all(columns, PLANE_AXES, 0, 0, tiled=True)  25.1 us
    ppermute x1, waiting for transfers between devices, spread_x(): before = lax.ppermute(plane, 'x', ring(4, 1))  21.1 us
    all_to_all x1, starting transfers between devices, on_device(): plane = lax.all_to_all(columns, PLANE_AXES, 0, 0, tiled=True)  13.5 us
    ppermute x5, starting transfers between devices, swap_cores(): return lax.ppermute(block, 'c', ring(2, 1))  11.6 us
    ppermute x1, waiting for transfers between devices, spread_x(): far_a = lax.ppermute(before[:half], 'x', ring(4, 1))  8.03 us
    ppermute x1, starting transfers between devices, on_device(): other = lax.ppermute(share, 'zh', ring(2, 1))  7.94 us
    ppermute x2, starting transfers between devices, sum_x(): share = share + lax.ppermute(share, 'x', [(i, i ^ bit) for i in range(4)])  7.79 us
    all_to_all x1, starting transfers between devices, on_device(): lax.all_to_all(sent, CLIP_AXES, 0, 0, tiled=True).reshape(ROWS, 4 * D)  7.44 us
  transfers between devices with their start and end apart: 16, of which 12 were waited for; matrix products, arithmetic and copies ran while one was open for 4% of the time, Pallas kernels for 5%

profile of v7, /device:TPU:1, one launch (start us, length us, event | category | flops | bytes accessed | tf_op | source)
XLA Modules:
  0.0 175.5 jit_solution(12097530258558698867)
XLA Ops:
  0.6 0.0 copy-start
  0.6 0.0 copy-start.6
  0.7 0.0 copy-start.7
  0.7 0.0 copy-start.8
  0.7 0.0 copy-start.9
  0.7 0.9 constant_dynamic-slice_fusion
  1.5 0.0 copy-done
  1.6 1.1 broadcast_in_dim.2
  2.7 13.5 %all-to-all-start = ((bf16[32,16,1024]{2,1,0:T(8,128)(2,1)}), bf16[32,16,1024]{2,1,0:T(8,128)(2,1)S(1)}, u32[]{:S(2)}, u32[]{:S(2)}) async-start(bf16[32,16,1024]{2,1,0:T(8,128)(2,1)} %broadcast_in_dim.2), calls=%async_computation | async-start | bytes 2097152 | tf_op jit(solution)/shard_map/all_to_all | solution.py:260
  16.1 0.0 copy-done.6
  16.2 0.0 copy-done.7
  16.2 0.0 copy-done.8
  16.2 0.0 copy-done.9
  16.2 1.5 pad_maximum_fusion
  17.7 25.1 %all-to-all-done.refs_0_ = bf16[32,16,1024]{2,1,0:T(8,128)(2,1)S(1)} async-done(((bf16[32,16,1024]{2,1,0:T(8,128)(2,1)}), bf16[32,16,1024]{2,1,0:T(8,128)(2,1)S(1)}, u32[]{:S(2)}, u32[]{:S(2)}) %all-to-all-start) | async-done | bytes 1048608 | tf_op jit(solution)/shard_map/all_to_all | solution.py:260
  42.8 7.4 %all-to-all-start.1 = ((bf16[32,8,4096]{2,1,0:T(8,128)(2,1)}), bf16[32,8,4096]{2,1,0:T(8,128)(2,1)S(1)}, u32[]{:S(2)}, u32[]{:S(2)}) async-start(bf16[32,8,4096]{2,1,0:T(8,128)(2,1)} %pad_maximum_fusion), calls=%async_computation.1 | async-start | bytes 4194304 | tf_op jit(solution)/shard_map/all_to_all | solution.py:266
  50.2 3.1 %collective-permute-start.1 = (bf16[32,16,1024]{2,1,0:T(8,128)(2,1)S(1)}, bf16[32,16,1024]{2,1,0:T(8,128)(2,1)S(1)}, u32[]{:S(2)}, u32[]{:S(2)}) collective-permute-start(bf16[32,16,1024]{2,1,0:T(8,128)(2,1)S(1)} %all-to-all-done.refs_0_), channel_id=1, source_target_pairs={{0,1},{1,2},{2,3},{3,0},{4,5},{5,6},{6,7},{7,4},{8,9},{9,10},{10,1... | collective-permute-start | bytes 3145736 | tf_op jit(solution)/shard_map/ppermute | solution.py:220
  53.4 3.4 %collective-permute-start = (bf16[32,16,1024]{2,1,0:T(8,128)(2,1)S(1)}, bf16[32,16,1024]{2,1,0:T(8,128)(2,1)S(1)}, u32[]{:S(2)}, u32[]{:S(2)}) collective-permute-start(bf16[32,16,1024]{2,1,0:T(8,128)(2,1)S(1)} %all-to-all-done.refs_0_), channel_id=1, source_target_pairs={{0,3},{1,0},{2,1},{3,2},{4,7},{5,4},{6,5},{7,6},{8,11},{9,8},{10,9... | collective-permute-start | bytes 3145736 | tf_op jit(solution)/shard_map/ppermute | solution.py:219
  56.7 21.1 %collective-permute-done.1.refs_3_ = bf16[32,16,1024]{2,1,0:T(8,128)(2,1)S(1)} collective-permute-done((bf16[32,16,1024]{2,1,0:T(8,128)(2,1)S(1)}, bf16[32,16,1024]{2,1,0:T(8,128)(2,1)S(1)}, u32[]{:S(2)}, u32[]{:S(2)}) %collective-permute-start.1) | collective-permute-done | bytes 1048608 | tf_op jit(solution)/shard_map/ppermute | solution.py:220
  77.9 0.9 slice.8
  78.8 1.9 %collective-permute-start.2 = (bf16[16,16,1024]{2,1,0:T(8,128)(2,1)}, bf16[16,16,1024]{2,1,0:T(8,128)(2,1)}, u32[]{:S(2)}, u32[]{:S(2)}) collective-permute-start(bf16[16,16,1024]{2,1,0:T(8,128)(2,1)} %slice.8), channel_id=1, source_target_pairs={{0,1},{1,2},{2,3},{3,0},{4,5},{5,6},{6,7},{7,4},{8,9},{9,10},{10,1... | collective-permute-start | bytes 1572872 | tf_op jit(solution)/shard_map/ppermute | solution.py:221
  80.7 0.0 collective-permute-done.refs_1_
  80.7 0.0 copy-done.1
  80.7 0.0 copy-start.3
  80.7 0.9 slice.9
  81.6 0.2 copy-done.3
  81.9 4.6 %collective-permute-start.3 = (bf16[16,16,1024]{2,1,0:T(8,128)(2,1)}, bf16[16,16,1024]{2,1,0:T(8,128)(2,1)}, u32[]{:S(2)}, u32[]{:S(2)}) collective-permute-start(bf16[16,16,1024]{2,1,0:T(8,128)(2,1)} %slice.9), channel_id=1, source_target_pairs={{0,3},{1,0},{2,1},{3,2},{4,7},{5,4},{6,5},{7,6},{8,11},{9,8},{10,9... | collective-permute-start | bytes 1572872 | tf_op jit(solution)/shard_map/ppermute | solution.py:222
  86.4 0.1 pad_add_fusion.place
  86.5 8.0 %collective-permute-done.2 = bf16[16,16,1024]{2,1,0:T(8,128)(2,1)} collective-permute-done((bf16[16,16,1024]{2,1,0:T(8,128)(2,1)}, bf16[16,16,1024]{2,1,0:T(8,128)(2,1)}, u32[]{:S(2)}, u32[]{:S(2)}) %collective-permute-start.2) | collective-permute-done | bytes 524320 | tf_op jit(solution)/shard_map/ppermute | solution.py:221
  94.6 2.1 %collective-permute-done.3 = bf16[16,16,1024]{2,1,0:T(8,128)(2,1)} collective-permute-done((bf16[16,16,1024]{2,1,0:T(8,128)(2,1)}, bf16[16,16,1024]{2,1,0:T(8,128)(2,1)}, u32[]{:S(2)}, u32[]{:S(2)}) %collective-permute-start.3) | collective-permute-done | bytes 524320 | tf_op jit(solution)/shard_map/ppermute | solution.py:222
  96.6 4.3 %all-to-all-done.1 = bf16[32,8,4096]{2,1,0:T(8,128)(2,1)S(1)} async-done(((bf16[32,8,4096]{2,1,0:T(8,128)(2,1)}), bf16[32,8,4096]{2,1,0:T(8,128)(2,1)S(1)}, u32[]{:S(2)}, u32[]{:S(2)}) %all-to-all-start.1) | async-done | bytes 2097184 | tf_op jit(solution)/shard_map/all_to_all | solution.py:266
  101.0 4.6 %attention_and_weight_grad.1 = (f32[16,256,256]{2,1,0:T(8,128)}, bf16[512,1024]{1,0:T(8,128)(2,1)S(1)}, bf16[512,1024]{1,0:T(8,128)(2,1)S(1)}) custom-call(s32[2]{0:T(128)S(1)} %pad_add_fusion.place, bf16[256,4096]{1,0:T(8,128)(2,1)S(1)} %bitcast.12, bf16[256,4096]{1,0:T(8,128)(2,1)S(1)} %bitcast.13, bf16[256,4096]{1,0:T(8,128)(2,1)S(1)} %bitcast.14, ...), custom_call_target="tpu_custom_call" | custom-call | flops 2000000000 | bytes 8388608 | tf_op jit(solution)/shard_map/attention_and_weight_grad/pallas_call | solution.py:86
  105.6 2.8 %collective-permute-start.4 = (bf16[512,1024]{1,0:T(8,128)(2,1)S(1)}, bf16[512,1024]{1,0:T(8,128)(2,1)S(1)}, u32[]{:S(2)}, u32[]{:S(2)}) collective-permute-start(bf16[512,1024]{1,0:T(8,128)(2,1)S(1)} %get-tuple-element.39), channel_id=1, source_target_pairs={{0,8},{8,0},{1,9},{9,1},{2,10},{10,2},{3,11},{11,3},{4,12},{12,4},... | collective-permute-start | bytes 3145736 | tf_op jit(solution)/shard_map/ppermute | solution.py:214
  108.3 2.3 %collective-permute-done.4 = bf16[512,1024]{1,0:T(8,128)(2,1)S(1)} collective-permute-done((bf16[512,1024]{1,0:T(8,128)(2,1)S(1)}, bf16[512,1024]{1,0:T(8,128)(2,1)S(1)}, u32[]{:S(2)}, u32[]{:S(2)}) %collective-permute-start.4) | collective-permute-done | bytes 1048608 | tf_op jit(solution)/shard_map/ppermute | solution.py:214
  110.6 1.5 add_convert_fusion
  112.1 5.4 %all-to-all-start.2 = ((bf16[32,16,1024]{2,1,0:T(8,128)(2,1)}), bf16[32,16,1024]{2,1,0:T(8,128)(2,1)}, u32[]{:S(2)}, u32[]{:S(2)}) async-start(bf16[32,16,1024]{2,1,0:T(8,128)(2,1)} %bitcast.22), calls=%async_computation.2 | async-start | bytes 2097152 | tf_op jit(solution)/shard_map/all_to_all | solution.py:270
  117.6 0.0 copy-start.4
  117.6 0.0 copy-start.2
  117.6 1.2 constant_dynamic-update-slice_fusion.1
  118.8 1.1 constant_dynamic-update-slice_fusion.refs_2_
  119.9 2.6 %collective-permute-start.7 = (bf16[32,16,1024]{2,1,0:T(8,128)(2,1)S(1)}, bf16[32,16,1024]{2,1,0:T(8,128)(2,1)S(1)}, u32[]{:S(2)}, u32[]{:S(2)}) collective-permute-start(bf16[32,16,1024]{2,1,0:T(8,128)(2,1)S(1)} %constant_dynamic-update-slice_fusion.refs_2_), channel_id=1, source_target_pairs={{0,8},{8,0},{1,9},{9,1},{2,10},{10,2},{3,11},{11,3},{4,12},{12,4},... | collective-permute-start | bytes 3145736 | tf_op jit(solution)/shard_map/ppermute | solution.py:214
  122.5 1.9 %collective-permute-start.5 = (bf16[32,16,1024]{2,1,0:T(8,128)(2,1)S(1)}, bf16[32,16,1024]{2,1,0:T(8,128)(2,1)S(1)}, u32[]{:S(2)}, u32[]{:S(2)}) collective-permute-start(bf16[32,16,1024]{2,1,0:T(8,128)(2,1)S(1)} %all-to-all-done.refs_0_), channel_id=1, source_target_pairs={{0,8},{8,0},{1,9},{9,1},{2,10},{10,2},{3,11},{11,3},{4,12},{12,4},... | collective-permute-start | bytes 3145736 | tf_op jit(solution)/shard_map/ppermute | solution.py:214
  124.4 0.0 copy-done.4
  124.4 2.4 %collective-permute-start.6 = (bf16[32,16,1024]{2,1,0:T(8,128)(2,1)S(1)}, bf16[32,16,1024]{2,1,0:T(8,128)(2,1)S(1)}, u32[]{:S(2)}, u32[]{:S(2)}) collective-permute-start(bf16[32,16,1024]{2,1,0:T(8,128)(2,1)S(1)} %copy-done.4), channel_id=1, source_target_pairs={{0,8},{8,0},{1,9},{9,1},{2,10},{10,2},{3,11},{11,3},{4,12},{12,4},... | collective-permute-start | bytes 3145736 | tf_op jit(solution)/shard_map/ppermute | solution.py:214
  126.8 1.9 %collective-permute-start.8 = (bf16[32,16,1024]{2,1,0:T(8,128)(2,1)S(1)}, bf16[32,16,1024]{2,1,0:T(8,128)(2,1)S(1)}, u32[]{:S(2)}, u32[]{:S(2)}) collective-permute-start(bf16[32,16,1024]{2,1,0:T(8,128)(2,1)S(1)} %copy-done.2), channel_id=1, source_target_pairs={{0,8},{8,0},{1,9},{9,1},{2,10},{10,2},{3,11},{11,3},{4,12},{12,4},... | collective-permute-start | bytes 3145736 | tf_op jit(solution)/shard_map/ppermute | solution.py:214
  128.8 0.0 collective-permute-done.7.refs_6_
  128.8 0.0 collective-permute-done.5.refs_4_
  128.8 0.3 collective-permute-done.6.refs_5_
  129.1 2.3 %collective-permute-done.8.refs_7_ = bf16[32,16,1024]{2,1,0:T(8,128)(2,1)S(1)} collective-permute-done((bf16[32,16,1024]{2,1,0:T(8,128)(2,1)S(1)}, bf16[32,16,1024]{2,1,0:T(8,128)(2,1)S(1)}, u32[]{:S(2)}, u32[]{:S(2)}) %collective-permute-start.8) | collective-permute-done | bytes 1048608 | tf_op jit(solution)/shard_map/ppermute | solution.py:214
  131.4 2.2 %copy-done.5 = f32[16,256,256]{2,1,0:T(8,128)S(1)} copy-done((f32[16,256,256]{2,1,0:T(8,128)S(1)}, f32[16,256,256]{2,1,0:T(8,128)}, u32[]{:S(2)}) %copy-start.5) | copy-done | bytes 4194328
  133.6 4.3 %attention_grads.1 = bf16[3,1024,256]{2,1,0:T(8,128)(2,1)S(1)} custom-call(s32[2]{0:T(128)S(1)} %pad_add_fusion.place, f32[16,256,256]{2,1,0:T(8,128)S(1)} %copy-done.5, bf16[256,4096]{1,0:T(8,128)(2,1)S(1)} %bitcast.16, bf16[256,4096]{1,0:T(8,128)(2,1)S(1)} %bitcast.17, bf16[256,4096]{1,0:T(8,128)(2,1)S(1)} %bitcast.18, bf16[256,4096]{1,0:T(8,128)(2,1)S(1)} %bitcast.19, ...), custom_call_target="tpu_custom_call" | custom-call | flops 3000000000 | bytes 10485760 | tf_op jit(solution)/shard_map/attention_grads/pallas_call | solution.py:146
  137.8 3.8 %input_projection.1 = bf16[256,1024]{1,0:T(8,128)(2,1)} custom-call(s32[2]{0:T(128)S(1)} %pad_add_fusion.place, bf16[3072,256]{1,0:T(8,128)(2,1)S(1)} %bitcast.20, bf16[32,16,1024]{2,1,0:T(8,128)(2,1)S(1)} %all-to-all-done.refs_0_, bf16[32,16,1024]{2,1,0:T(8,128)(2,1)S(1)} %copy-done.4, bf16[32,16,1024]{2,1,0:T(8,128)(2,1)S(1)} %constant_dynamic-update-slice_fusion.refs_2_, ...), custom_call_target="tpu_custom_call" | custom-call | flops 2000000000 | bytes 8388608 | tf_op jit(solution)/shard_map/input_projection/pallas_call | solution.py:183
  141.7 2.9 %all-to-all-done.2 = bf16[32,16,1024]{2,1,0:T(8,128)(2,1)} async-done(((bf16[32,16,1024]{2,1,0:T(8,128)(2,1)}), bf16[32,16,1024]{2,1,0:T(8,128)(2,1)}, u32[]{:S(2)}, u32[]{:S(2)}) %all-to-all-start.2) | async-done | bytes 1048608 | tf_op jit(solution)/shard_map/all_to_all | solution.py:270
  144.6 7.0 %all-to-all-start.3 = ((bf16[32,8,1024]{2,1,0:T(8,128)(2,1)}), bf16[32,8,1024]{2,1,0:T(8,128)(2,1)S(1)}, u32[]{:S(2)}, u32[]{:S(2)}) async-start(bf16[32,8,1024]{2,1,0:T(8,128)(2,1)} %bitcast.8), calls=%async_computation.3 | async-start | bytes 1048576 | tf_op jit(solution)/shard_map/all_to_all | solution.py:276
  151.6 1.4 convert_reduce_fusion
  153.0 3.1 %collective-permute-start.9 = (f32[16,1024]{1,0:T(8,128)S(1)}, f32[16,1024]{1,0:T(8,128)S(1)}, u32[]{:S(2)}, u32[]{:S(2)}) collective-permute-start(f32[16,1024]{1,0:T(8,128)S(1)} %broadcast_multiply_fusion), channel_id=1, source_target_pairs={{0,1},{1,0},{2,3},{3,2},{4,5},{5,4},{6,7},{7,6},{8,9},{9,8},{10,11... | collective-permute-start | bytes 196616 | tf_op jit(solution)/shard_map/ppermute | solution.py:249
  156.1 2.2 %collective-permute-done.9 = f32[16,1024]{1,0:T(8,128)S(1)} collective-permute-done((f32[16,1024]{1,0:T(8,128)S(1)}, f32[16,1024]{1,0:T(8,128)S(1)}, u32[]{:S(2)}, u32[]{:S(2)}) %collective-permute-start.9) | collective-permute-done | bytes 65568 | tf_op jit(solution)/shard_map/ppermute | solution.py:249
  158.4 4.7 %collective-permute-start.10 = (f32[16,1024]{1,0:T(8,128)S(1)}, f32[16,1024]{1,0:T(8,128)S(1)}, u32[]{:S(2)}, u32[]{:S(2)}) collective-permute-start(f32[16,1024]{1,0:T(8,128)S(1)} %fusion), channel_id=1, source_target_pairs={{0,2},{1,3},{2,0},{3,1},{4,6},{5,7},{6,4},{7,5},{8,10},{9,11},{10,... | collective-permute-start | bytes 196616 | tf_op jit(solution)/shard_map/ppermute | solution.py:249
  163.0 2.1 %collective-permute-done.10 = f32[16,1024]{1,0:T(8,128)S(1)} collective-permute-done((f32[16,1024]{1,0:T(8,128)S(1)}, f32[16,1024]{1,0:T(8,128)S(1)}, u32[]{:S(2)}, u32[]{:S(2)}) %collective-permute-start.10) | collective-permute-done | bytes 65568 | tf_op jit(solution)/shard_map/ppermute | solution.py:249
  165.2 7.9 %collective-permute-start.11 = (f32[16,1024]{1,0:T(8,128)S(1)}, f32[16,1024]{1,0:T(8,128)S(1)}, u32[]{:S(2)}, u32[]{:S(2)}) collective-permute-start(f32[16,1024]{1,0:T(8,128)S(1)} %add.22), channel_id=1, source_target_pairs={{0,4},{4,0},{1,5},{5,1},{2,6},{6,2},{3,7},{7,3},{8,12},{12,8},{9,1... | collective-permute-start | bytes 196616 | tf_op jit(solution)/shard_map/ppermute | solution.py:278
  173.1 0.0 all-to-all-done.3
  173.2 1.4 write_out.1
  174.6 0.3 collective-permute-done.11
  174.9 0.6 add.23
  (8 shorter events, 0.0 us)
Async XLA Ops:
  0.6 0.9 copy-start
  0.6 15.5 %copy-start.6 = (bf16[1,1,256,1024]{3,2,1,0:T(8,128)(2,1)S(1)}, bf16[1,1,256,1024]{3,2,1,0:T(8,128)(2,1)}, u32[]{:S(2)}) copy-start(bf16[1,1,256,1024]{3,2,1,0:T(8,128)(2,1)} %param.9) | copy-start | bytes 1572868
  0.7 15.5 %copy-start.7 = (bf16[1,1,256,1024]{3,2,1,0:T(8,128)(2,1)S(1)}, bf16[1,1,256,1024]{3,2,1,0:T(8,128)(2,1)}, u32[]{:S(2)}) copy-start(bf16[1,1,256,1024]{3,2,1,0:T(8,128)(2,1)} %param.8) | copy-start | bytes 1572868
  0.7 15.5 %copy-start.8 = (bf16[1,1,256,1024]{3,2,1,0:T(8,128)(2,1)S(1)}, bf16[1,1,256,1024]{3,2,1,0:T(8,128)(2,1)}, u32[]{:S(2)}) copy-start(bf16[1,1,256,1024]{3,2,1,0:T(8,128)(2,1)} %param.7) | copy-start | bytes 1572868
  0.7 15.5 %copy-start.9 = (bf16[1,1,256,1024]{3,2,1,0:T(8,128)(2,1)S(1)}, bf16[1,1,256,1024]{3,2,1,0:T(8,128)(2,1)}, u32[]{:S(2)}) copy-start(bf16[1,1,256,1024]{3,2,1,0:T(8,128)(2,1)} %param.6) | copy-start | bytes 1572868
  2.7 40.1 %all-to-all-start = ((bf16[32,16,1024]{2,1,0:T(8,128)(2,1)}), bf16[32,16,1024]{2,1,0:T(8,128)(2,1)S(1)}, u32[]{:S(2)}, u32[]{:S(2)}) async-start(bf16[32,16,1024]{2,1,0:T(8,128)(2,1)} %broadcast_in_dim.2), calls=%async_computation | async-start | bytes 2097152 | tf_op jit(solution)/shard_map/all_to_all | solution.py:260
  42.8 58.2 %all-to-all-start.1 = ((bf16[32,8,4096]{2,1,0:T(8,128)(2,1)}), bf16[32,8,4096]{2,1,0:T(8,128)(2,1)S(1)}, u32[]{:S(2)}, u32[]{:S(2)}) async-start(bf16[32,8,4096]{2,1,0:T(8,128)(2,1)} %pad_maximum_fusion), calls=%async_computation.1 | async-start | bytes 4194304 | tf_op jit(solution)/shard_map/all_to_all | solution.py:266
  50.2 27.6 %collective-permute-start.1 = (bf16[32,16,1024]{2,1,0:T(8,128)(2,1)S(1)}, bf16[32,16,1024]{2,1,0:T(8,128)(2,1)S(1)}, u32[]{:S(2)}, u32[]{:S(2)}) collective-permute-start(bf16[32,16,1024]{2,1,0:T(8,128)(2,1)S(1)} %all-to-all-done.refs_0_), channel_id=1, source_target_pairs={{0,1},{1,2},{2,3},{3,0},{4,5},{5,6},{6,7},{7,4},{8,9},{9,10},{10,1... | collective-permute-start | bytes 3145736 | tf_op jit(solution)/shard_map/ppermute | solution.py:220
  53.4 27.3 %collective-permute-start = (bf16[32,16,1024]{2,1,0:T(8,128)(2,1)S(1)}, bf16[32,16,1024]{2,1,0:T(8,128)(2,1)S(1)}, u32[]{:S(2)}, u32[]{:S(2)}) collective-permute-start(bf16[32,16,1024]{2,1,0:T(8,128)(2,1)S(1)} %all-to-all-done.refs_0_), channel_id=1, source_target_pairs={{0,3},{1,0},{2,1},{3,2},{4,7},{5,4},{6,5},{7,6},{8,11},{9,8},{10,9... | collective-permute-start | bytes 3145736 | tf_op jit(solution)/shard_map/ppermute | solution.py:219
  77.9 2.8 %copy-start.1 = (bf16[32,16,1024]{2,1,0:T(8,128)(2,1)}, bf16[32,16,1024]{2,1,0:T(8,128)(2,1)S(1)}, u32[]{:S(2)}) copy-start(bf16[32,16,1024]{2,1,0:T(8,128)(2,1)S(1)} %collective-permute-done.1.refs_3_) | copy-start | bytes 3145732
  78.8 15.8 %collective-permute-start.2 = (bf16[16,16,1024]{2,1,0:T(8,128)(2,1)}, bf16[16,16,1024]{2,1,0:T(8,128)(2,1)}, u32[]{:S(2)}, u32[]{:S(2)}) collective-permute-start(bf16[16,16,1024]{2,1,0:T(8,128)(2,1)} %slice.8), channel_id=1, source_target_pairs={{0,1},{1,2},{2,3},{3,0},{4,5},{5,6},{6,7},{7,4},{8,9},{9,10},{10,1... | collective-permute-start | bytes 1572872 | tf_op jit(solution)/shard_map/ppermute | solution.py:221
  80.7 1.2 copy-start.3
  81.9 14.8 %collective-permute-start.3 = (bf16[16,16,1024]{2,1,0:T(8,128)(2,1)}, bf16[16,16,1024]{2,1,0:T(8,128)(2,1)}, u32[]{:S(2)}, u32[]{:S(2)}) collective-permute-start(bf16[16,16,1024]{2,1,0:T(8,128)(2,1)} %slice.9), channel_id=1, source_target_pairs={{0,3},{1,0},{2,1},{3,2},{4,7},{5,4},{6,5},{7,6},{8,11},{9,8},{10,9... | collective-permute-start | bytes 1572872 | tf_op jit(solution)/shard_map/ppermute | solution.py:222
  105.6 5.0 %collective-permute-start.4 = (bf16[512,1024]{1,0:T(8,128)(2,1)S(1)}, bf16[512,1024]{1,0:T(8,128)(2,1)S(1)}, u32[]{:S(2)}, u32[]{:S(2)}) collective-permute-start(bf16[512,1024]{1,0:T(8,128)(2,1)S(1)} %get-tuple-element.39), channel_id=1, source_target_pairs={{0,8},{8,0},{1,9},{9,1},{2,10},{10,2},{3,11},{11,3},{4,12},{12,4},... | collective-permute-start | bytes 3145736 | tf_op jit(solution)/shard_map/ppermute | solution.py:214
  112.1 32.5 %all-to-all-start.2 = ((bf16[32,16,1024]{2,1,0:T(8,128)(2,1)}), bf16[32,16,1024]{2,1,0:T(8,128)(2,1)}, u32[]{:S(2)}, u32[]{:S(2)}) async-start(bf16[32,16,1024]{2,1,0:T(8,128)(2,1)} %bitcast.22), calls=%async_computation.2 | async-start | bytes 2097152 | tf_op jit(solution)/shard_map/all_to_all | solution.py:270
  117.6 6.8 %copy-start.4 = (bf16[32,16,1024]{2,1,0:T(8,128)(2,1)S(1)}, bf16[32,16,1024]{2,1,0:T(8,128)(2,1)}, u32[]{:S(2)}) copy-start(bf16[32,16,1024]{2,1,0:T(8,128)(2,1)} %copy-done.3) | copy-start | bytes 3145732
  117.6 9.3 %copy-start.2 = (bf16[32,16,1024]{2,1,0:T(8,128)(2,1)S(1)}, bf16[32,16,1024]{2,1,0:T(8,128)(2,1)}, u32[]{:S(2)}) copy-start(bf16[32,16,1024]{2,1,0:T(8,128)(2,1)} %copy-done.1) | copy-start | bytes 3145732
  119.9 8.9 %collective-permute-start.7 = (bf16[32,16,1024]{2,1,0:T(8,128)(2,1)S(1)}, bf16[32,16,1024]{2,1,0:T(8,128)(2,1)S(1)}, u32[]{:S(2)}, u32[]{:S(2)}) collective-permute-start(bf16[32,16,1024]{2,1,0:T(8,128)(2,1)S(1)} %constant_dynamic-update-slice_fusion.refs_2_), channel_id=1, source_target_pairs={{0,8},{8,0},{1,9},{9,1},{2,10},{10,2},{3,11},{11,3},{4,12},{12,4},... | collective-permute-start | bytes 3145736 | tf_op jit(solution)/shard_map/ppermute | solution.py:214
  122.5 6.3 %collective-permute-start.5 = (bf16[32,16,1024]{2,1,0:T(8,128)(2,1)S(1)}, bf16[32,16,1024]{2,1,0:T(8,128)(2,1)S(1)}, u32[]{:S(2)}, u32[]{:S(2)}) collective-permute-start(bf16[32,16,1024]{2,1,0:T(8,128)(2,1)S(1)} %all-to-all-done.refs_0_), channel_id=1, source_target_pairs={{0,8},{8,0},{1,9},{9,1},{2,10},{10,2},{3,11},{11,3},{4,12},{12,4},... | collective-permute-start | bytes 3145736 | tf_op jit(solution)/shard_map/ppermute | solution.py:214
  124.4 4.7 %collective-permute-start.6 = (bf16[32,16,1024]{2,1,0:T(8,128)(2,1)S(1)}, bf16[32,16,1024]{2,1,0:T(8,128)(2,1)S(1)}, u32[]{:S(2)}, u32[]{:S(2)}) collective-permute-start(bf16[32,16,1024]{2,1,0:T(8,128)(2,1)S(1)} %copy-done.4), channel_id=1, source_target_pairs={{0,8},{8,0},{1,9},{9,1},{2,10},{10,2},{3,11},{11,3},{4,12},{12,4},... | collective-permute-start | bytes 3145736 | tf_op jit(solution)/shard_map/ppermute | solution.py:214
  126.8 4.6 %collective-permute-start.8 = (bf16[32,16,1024]{2,1,0:T(8,128)(2,1)S(1)}, bf16[32,16,1024]{2,1,0:T(8,128)(2,1)S(1)}, u32[]{:S(2)}, u32[]{:S(2)}) collective-permute-start(bf16[32,16,1024]{2,1,0:T(8,128)(2,1)S(1)} %copy-done.2), channel_id=1, source_target_pairs={{0,8},{8,0},{1,9},{9,1},{2,10},{10,2},{3,11},{11,3},{4,12},{12,4},... | collective-permute-start | bytes 3145736 | tf_op jit(solution)/shard_map/ppermute | solution.py:214
  131.4 2.2 %copy-start.5 = (f32[16,256,256]{2,1,0:T(8,128)S(1)}, f32[16,256,256]{2,1,0:T(8,128)}, u32[]{:S(2)}) copy-start(f32[16,256,256]{2,1,0:T(8,128)} %get-tuple-element.45.attention_ref) | copy-start | bytes 12582916
  144.6 28.6 %all-to-all-start.3 = ((bf16[32,8,1024]{2,1,0:T(8,128)(2,1)}), bf16[32,8,1024]{2,1,0:T(8,128)(2,1)S(1)}, u32[]{:S(2)}, u32[]{:S(2)}) async-start(bf16[32,8,1024]{2,1,0:T(8,128)(2,1)} %bitcast.8), calls=%async_computation.3 | async-start | bytes 1048576 | tf_op jit(solution)/shard_map/all_to_all | solution.py:276
  153.0 5.4 %collective-permute-start.9 = (f32[16,1024]{1,0:T(8,128)S(1)}, f32[16,1024]{1,0:T(8,128)S(1)}, u32[]{:S(2)}, u32[]{:S(2)}) collective-permute-start(f32[16,1024]{1,0:T(8,128)S(1)} %broadcast_multiply_fusion), channel_id=1, source_target_pairs={{0,1},{1,0},{2,3},{3,2},{4,5},{5,4},{6,7},{7,6},{8,9},{9,8},{10,11... | collective-permute-start | bytes 196616 | tf_op jit(solution)/shard_map/ppermute | solution.py:249
  158.4 6.8 %collective-permute-start.10 = (f32[16,1024]{1,0:T(8,128)S(1)}, f32[16,1024]{1,0:T(8,128)S(1)}, u32[]{:S(2)}, u32[]{:S(2)}) collective-permute-start(f32[16,1024]{1,0:T(8,128)S(1)} %fusion), channel_id=1, source_target_pairs={{0,2},{1,3},{2,0},{3,1},{4,6},{5,7},{6,4},{7,5},{8,10},{9,11},{10,... | collective-permute-start | bytes 196616 | tf_op jit(solution)/shard_map/ppermute | solution.py:249
  165.2 9.7 %collective-permute-start.11 = (f32[16,1024]{1,0:T(8,128)S(1)}, f32[16,1024]{1,0:T(8,128)S(1)}, u32[]{:S(2)}, u32[]{:S(2)}) collective-permute-start(f32[16,1024]{1,0:T(8,128)S(1)} %add.22), channel_id=1, source_target_pairs={{0,4},{4,0},{1,5},{5,1},{2,6},{6,2},{3,7},{7,3},{8,12},{12,8},{9,1... | collective-permute-start | bytes 196616 | tf_op jit(solution)/shard_map/ppermute | solution.py:278

commit v8 on v7

--- a/solution.py
+++ b/solution.py
@@ -1,3 +1,4 @@
+import functools
 import math
 
 import jax
@@ -223,8 +224,38 @@
     return [plane, after, far_a, far_b, before]
 
 
+def add_kernel(a_ref, b_ref, o_ref):
+    total = a_ref[...].astype(jnp.float32) + b_ref[...].astype(jnp.float32)
+    o_ref[...] = total.astype(jnp.bfloat16)
+
+
 def sum_cores(keep, send):
-    return (keep.astype(jnp.float32) + swap_cores(send).astype(jnp.float32)).astype(jnp.bfloat16)
+    block = pl.BlockSpec((256, D), lambda i: (i, 0))
+    return pl.pallas_call(
+        add_kernel,
+        grid=(2,),
+        in_specs=[block, block],
+        out_specs=block,
+        out_shape=jax.ShapeDtypeStruct(keep.shape, keep.dtype),
+        compiler_params=pltpu.CompilerParams(vmem_limit_bytes=8 * 2**20),
+        name="sum_cores",
+    )(keep, swap_cores(send))
+
+
+def shares_kernel(factor, s_ref, o_ref):
+    o_ref[...] = jnp.sum(s_ref[...].astype(jnp.float32), axis=0) * factor
+
+
+def sum_shares(shares, factor):
+    return pl.pallas_call(
+        functools.partial(shares_kernel, factor),
+        grid=(2,),
+        in_specs=[pl.BlockSpec((32, 16, D // 2), lambda i: (0, 0, i))],
+        out_specs=pl.BlockSpec((16, D // 2), lambda i: (0, i)),
+        out_shape=jax.ShapeDtypeStruct((16, D), jnp.float32),
+        compiler_params=pltpu.CompilerParams(vmem_limit_bytes=8 * 2**20),
+        name="sum_shares",
+    )(shares)
 
 
 def write_kernel(i_ref, o_ref):
@@ -274,7 +305,7 @@
     result = projection_call(place, grads, pieces).reshape(CLIP_LEN, PATCH_BLOCK, D)
     result, share = lax.optimization_barrier((result, share))
     input_gradient = lax.all_to_all(result, CLIP_AXES, 0, 0, tiled=True)
-    share = sum_x(jnp.sum(share.astype(jnp.float32), axis=0) * factor)
+    share = sum_x(sum_shares(share, factor))
     other = lax.ppermute(share, "zh", ring(2, 1))
     input_gradient = write_out(input_gradient.reshape(ROWS, D))
     input_gradient, other = lax.optimization_barrier((input_gradient, other))

time: 178 us -> 178 us (level)
  waiting for transfers between devices: 73.1 us -> 69.4 us
  local copies, waits for them, and re-layouts: 8.57 us -> 11.9 us
    unnamed x21 -> x15, local copies, waits for them, and re-layouts: 3.68 us -> 7.17 us
    all_to_all x1, waiting for transfers between devices: 2.91 us -> 0.42 us  [on_device(): lax.all_to_all(share.reshape(32, 16, D), PLANE_AXES, 0, 0, tiled=True)]
  transfers between devices with their start and end apart: 16 -> 16, of which waited for: 12 -> 12; matrix products, arithmetic and copies ran while one was open for 4% -> 4% of each run, Pallas kernels for 5% -> 6%
where the time goes in v8:
time: 178 us; the launch traced here: 176 us
  starting transfers between devices  74 us (42%)
  waiting for transfers between devices  69.4 us (39%)
  Pallas kernels  15.7 us (9%)
  local copies, waits for them, and re-layouts  11.9 us (7%)
  other arithmetic  3.78 us (2%)
    all_to_all x1, waiting for transfers between devices, on_device(): plane = lax.all_to_all(columns, PLANE_AXES, 0, 0, tiled=True)  23.6 us
    ppermute x1, waiting for transfers between devices, spread_x(): before = lax.ppermute(plane, 'x', ring(4, 1))  21.1 us
    all_to_all x1, starting transfers between devices, on_device(): plane = lax.all_to_all(columns, PLANE_AXES, 0, 0, tiled=True)  13.5 us
    ppermute x5, starting transfers between devices, swap_cores(): return lax.ppermute(block, 'c', ring(2, 1))  11.6 us
    ppermute x1, waiting for transfers between devices, spread_x(): far_a = lax.ppermute(before[:half], 'x', ring(4, 1))  8.05 us
    ppermute x1, starting transfers between devices, on_device(): other = lax.ppermute(share, 'zh', ring(2, 1))  7.94 us
    ppermute x2, starting transfers between devices, sum_x(): share = share + lax.ppermute(share, 'x', [(i, i ^ bit) for i in range(4)])  7.78 us
    all_to_all x1, starting transfers between devices, on_device(): lax.all_to_all(sent, CLIP_AXES, 0, 0, tiled=True).reshape(ROWS, 4 * D)  7.44 us
  transfers between devices with their start and end apart: 16, of which 12 were waited for; matrix products, arithmetic and copies ran while one was open for 4% of the time, Pallas kernels for 6%

profile of v8, /device:TPU:1, one launch (start us, length us, event | category | flops | bytes accessed | tf_op | source)
XLA Modules:
  0.0 175.6 jit_solution(16911787641852553845)
XLA Ops:
  0.6 0.0 copy-start
  0.7 0.7 constant_dynamic-slice_fusion
  1.4 0.1 copy-done
  1.5 1.1 broadcast_in_dim.2
  2.7 13.5 %all-to-all-start = ((bf16[32,16,1024]{2,1,0:T(8,128)(2,1)}), bf16[32,16,1024]{2,1,0:T(8,128)(2,1)S(1)}, u32[]{:S(2)}, u32[]{:S(2)}) async-start(bf16[32,16,1024]{2,1,0:T(8,128)(2,1)} %broadcast_in_dim.2), calls=%async_computation | async-start | bytes 2097152 | tf_op jit(solution)/shard_map/all_to_all | solution.py:291
  16.1 3.0 %pad_maximum_fusion = bf16[32,8,4096]{2,1,0:T(8,128)(2,1)} fusion(bf16[32,8,1024]{2,1,0:T(8,128)(2,1)} %bitcast.24, bf16[32,8,1024]{2,1,0:T(8,128)(2,1)} %bitcast.25, bf16[32,8,1024]{2,1,0:T(8,128)(2,1)} %bitcast.26, bf16[32,8,1024]{2,1,0:T(8,128)(2,1)} %bitcast.27), kind=kLoop, calls=%fused_computation | loop fusion | flops 8388608 | bytes 4194304 | tf_op jit(solution)/shard_map/concatenate | solution.py:292
  19.2 23.6 %all-to-all-done.refs_0_ = bf16[32,16,1024]{2,1,0:T(8,128)(2,1)S(1)} async-done(((bf16[32,16,1024]{2,1,0:T(8,128)(2,1)}), bf16[32,16,1024]{2,1,0:T(8,128)(2,1)S(1)}, u32[]{:S(2)}, u32[]{:S(2)}) %all-to-all-start) | async-done | bytes 1048608 | tf_op jit(solution)/shard_map/all_to_all | solution.py:291
  42.8 7.4 %all-to-all-start.1 = ((bf16[32,8,4096]{2,1,0:T(8,128)(2,1)}), bf16[32,8,4096]{2,1,0:T(8,128)(2,1)S(1)}, u32[]{:S(2)}, u32[]{:S(2)}) async-start(bf16[32,8,4096]{2,1,0:T(8,128)(2,1)} %pad_maximum_fusion), calls=%async_computation.1 | async-start | bytes 4194304 | tf_op jit(solution)/shard_map/all_to_all | solution.py:297
  50.2 3.1 %collective-permute-start.1 = (bf16[32,16,1024]{2,1,0:T(8,128)(2,1)S(1)}, bf16[32,16,1024]{2,1,0:T(8,128)(2,1)S(1)}, u32[]{:S(2)}, u32[]{:S(2)}) collective-permute-start(bf16[32,16,1024]{2,1,0:T(8,128)(2,1)S(1)} %all-to-all-done.refs_0_), channel_id=1, source_target_pairs={{0,1},{1,2},{2,3},{3,0},{4,5},{5,6},{6,7},{7,4},{8,9},{9,10},{10,1... | collective-permute-start | bytes 3145736 | tf_op jit(solution)/shard_map/ppermute | solution.py:221
  53.3 3.4 %collective-permute-start = (bf16[32,16,1024]{2,1,0:T(8,128)(2,1)S(1)}, bf16[32,16,1024]{2,1,0:T(8,128)(2,1)S(1)}, u32[]{:S(2)}, u32[]{:S(2)}) collective-permute-start(bf16[32,16,1024]{2,1,0:T(8,128)(2,1)S(1)} %all-to-all-done.refs_0_), channel_id=1, source_target_pairs={{0,3},{1,0},{2,1},{3,2},{4,7},{5,4},{6,5},{7,6},{8,11},{9,8},{10,9... | collective-permute-start | bytes 3145736 | tf_op jit(solution)/shard_map/ppermute | solution.py:220
  56.7 21.1 %collective-permute-done.1.refs_3_ = bf16[32,16,1024]{2,1,0:T(8,128)(2,1)S(1)} collective-permute-done((bf16[32,16,1024]{2,1,0:T(8,128)(2,1)S(1)}, bf16[32,16,1024]{2,1,0:T(8,128)(2,1)S(1)}, u32[]{:S(2)}, u32[]{:S(2)}) %collective-permute-start.1) | collective-permute-done | bytes 1048608 | tf_op jit(solution)/shard_map/ppermute | solution.py:221
  77.8 0.0 copy-start.1
  77.8 0.9 slice.8
  78.7 1.9 %collective-permute-start.2 = (bf16[16,16,1024]{2,1,0:T(8,128)(2,1)}, bf16[16,16,1024]{2,1,0:T(8,128)(2,1)}, u32[]{:S(2)}, u32[]{:S(2)}) collective-permute-start(bf16[16,16,1024]{2,1,0:T(8,128)(2,1)} %slice.8), channel_id=1, source_target_pairs={{0,1},{1,2},{2,3},{3,0},{4,5},{5,6},{6,7},{7,4},{8,9},{9,10},{10,1... | collective-permute-start | bytes 1572872 | tf_op jit(solution)/shard_map/ppermute | solution.py:222
  80.7 0.0 collective-permute-done.refs_1_
  80.7 0.0 copy-done.1
  80.7 0.0 copy-start.3
  80.7 0.9 slice.9
  81.6 0.2 copy-done.3
  81.8 4.6 %collective-permute-start.3 = (bf16[16,16,1024]{2,1,0:T(8,128)(2,1)}, bf16[16,16,1024]{2,1,0:T(8,128)(2,1)}, u32[]{:S(2)}, u32[]{:S(2)}) collective-permute-start(bf16[16,16,1024]{2,1,0:T(8,128)(2,1)} %slice.9), channel_id=1, source_target_pairs={{0,3},{1,0},{2,1},{3,2},{4,7},{5,4},{6,5},{7,6},{8,11},{9,8},{10,9... | collective-permute-start | bytes 1572872 | tf_op jit(solution)/shard_map/ppermute | solution.py:223
  86.4 0.1 pad_add_fusion.place
  86.5 8.0 %collective-permute-done.2 = bf16[16,16,1024]{2,1,0:T(8,128)(2,1)} collective-permute-done((bf16[16,16,1024]{2,1,0:T(8,128)(2,1)}, bf16[16,16,1024]{2,1,0:T(8,128)(2,1)}, u32[]{:S(2)}, u32[]{:S(2)}) %collective-permute-start.2) | collective-permute-done | bytes 524320 | tf_op jit(solution)/shard_map/ppermute | solution.py:222
  94.5 2.1 %collective-permute-done.3 = bf16[16,16,1024]{2,1,0:T(8,128)(2,1)} collective-permute-done((bf16[16,16,1024]{2,1,0:T(8,128)(2,1)}, bf16[16,16,1024]{2,1,0:T(8,128)(2,1)}, u32[]{:S(2)}, u32[]{:S(2)}) %collective-permute-start.3) | collective-permute-done | bytes 524320 | tf_op jit(solution)/shard_map/ppermute | solution.py:223
  96.6 4.4 %all-to-all-done.1 = bf16[32,8,4096]{2,1,0:T(8,128)(2,1)S(1)} async-done(((bf16[32,8,4096]{2,1,0:T(8,128)(2,1)}), bf16[32,8,4096]{2,1,0:T(8,128)(2,1)S(1)}, u32[]{:S(2)}, u32[]{:S(2)}) %all-to-all-start.1) | async-done | bytes 2097184 | tf_op jit(solution)/shard_map/all_to_all | solution.py:297
  100.9 4.6 %attention_and_weight_grad.1 = (f32[16,256,256]{2,1,0:T(8,128)}, bf16[512,1024]{1,0:T(8,128)(2,1)S(1)}, bf16[512,1024]{1,0:T(8,128)(2,1)S(1)}) custom-call(s32[2]{0:T(128)S(1)} %pad_add_fusion.place, bf16[256,4096]{1,0:T(8,128)(2,1)S(1)} %bitcast.12, bf16[256,4096]{1,0:T(8,128)(2,1)S(1)} %bitcast.13, bf16[256,4096]{1,0:T(8,128)(2,1)S(1)} %bitcast.14, ...), custom_call_target="tpu_custom_call" | custom-call | flops 2000000000 | bytes 8388608 | tf_op jit(solution)/shard_map/attention_and_weight_grad/pallas_call | solution.py:87
  105.5 2.8 %collective-permute-start.4 = (bf16[512,1024]{1,0:T(8,128)(2,1)S(1)}, bf16[512,1024]{1,0:T(8,128)(2,1)S(1)}, u32[]{:S(2)}, u32[]{:S(2)}) collective-permute-start(bf16[512,1024]{1,0:T(8,128)(2,1)S(1)} %get-tuple-element.39), channel_id=1, source_target_pairs={{0,8},{8,0},{1,9},{9,1},{2,10},{10,2},{3,11},{11,3},{4,12},{12,4},... | collective-permute-start | bytes 3145736 | tf_op jit(solution)/shard_map/ppermute | solution.py:215
  108.3 2.3 %collective-permute-done.4.b_ref = bf16[512,1024]{1,0:T(8,128)(2,1)S(1)} collective-permute-done((bf16[512,1024]{1,0:T(8,128)(2,1)S(1)}, bf16[512,1024]{1,0:T(8,128)(2,1)S(1)}, u32[]{:S(2)}, u32[]{:S(2)}) %collective-permute-start.4) | collective-permute-done | bytes 1048608 | tf_op jit(solution)/shard_map/ppermute | solution.py:215
  110.6 0.3 sum_cores.1
  110.8 0.0 copy-start.6
  110.9 1.1 copy-done.6
  111.9 5.4 %all-to-all-start.2 = ((bf16[32,16,1024]{2,1,0:T(8,128)(2,1)}), bf16[32,16,1024]{2,1,0:T(8,128)(2,1)}, u32[]{:S(2)}, u32[]{:S(2)}) async-start(bf16[32,16,1024]{2,1,0:T(8,128)(2,1)} %bitcast.21), calls=%async_computation.2 | async-start | bytes 2097152 | tf_op jit(solution)/shard_map/all_to_all | solution.py:301
  117.4 1.1 constant_dynamic-update-slice_fusion.1
  118.5 1.1 constant_dynamic-update-slice_fusion.refs_2_
  119.5 2.6 %collective-permute-start.7 = (bf16[32,16,1024]{2,1,0:T(8,128)(2,1)S(1)}, bf16[32,16,1024]{2,1,0:T(8,128)(2,1)S(1)}, u32[]{:S(2)}, u32[]{:S(2)}) collective-permute-start(bf16[32,16,1024]{2,1,0:T(8,128)(2,1)S(1)} %constant_dynamic-update-slice_fusion.refs_2_), channel_id=1, source_target_pairs={{0,8},{8,0},{1,9},{9,1},{2,10},{10,2},{3,11},{11,3},{4,12},{12,4},... | collective-permute-start | bytes 3145736 | tf_op jit(solution)/shard_map/ppermute | solution.py:215
  122.1 1.9 %collective-permute-start.5 = (bf16[32,16,1024]{2,1,0:T(8,128)(2,1)S(1)}, bf16[32,16,1024]{2,1,0:T(8,128)(2,1)S(1)}, u32[]{:S(2)}, u32[]{:S(2)}) collective-permute-start(bf16[32,16,1024]{2,1,0:T(8,128)(2,1)S(1)} %all-to-all-done.refs_0_), channel_id=1, source_target_pairs={{0,8},{8,0},{1,9},{9,1},{2,10},{10,2},{3,11},{11,3},{4,12},{12,4},... | collective-permute-start | bytes 3145736 | tf_op jit(solution)/shard_map/ppermute | solution.py:215
  124.0 2.4 %collective-permute-start.6 = (bf16[32,16,1024]{2,1,0:T(8,128)(2,1)}, bf16[32,16,1024]{2,1,0:T(8,128)(2,1)S(1)}, u32[]{:S(2)}, u32[]{:S(2)}) collective-permute-start(bf16[32,16,1024]{2,1,0:T(8,128)(2,1)} %copy-done.3), channel_id=1, source_target_pairs={{0,8},{8,0},{1,9},{9,1},{2,10},{10,2},{3,11},{11,3},{4,12},{12,4},... | collective-permute-start | bytes 3145736 | tf_op jit(solution)/shard_map/ppermute | solution.py:215
  126.5 1.9 %collective-permute-start.8 = (bf16[32,16,1024]{2,1,0:T(8,128)(2,1)}, bf16[32,16,1024]{2,1,0:T(8,128)(2,1)S(1)}, u32[]{:S(2)}, u32[]{:S(2)}) collective-permute-start(bf16[32,16,1024]{2,1,0:T(8,128)(2,1)} %copy-done.1), channel_id=1, source_target_pairs={{0,8},{8,0},{1,9},{9,1},{2,10},{10,2},{3,11},{11,3},{4,12},{12,4},... | collective-permute-start | bytes 3145736 | tf_op jit(solution)/shard_map/ppermute | solution.py:215
  128.4 0.0 collective-permute-done.7.refs_6_
  128.4 0.0 collective-permute-done.5.refs_4_
  128.4 0.5 collective-permute-done.6.refs_5_
  128.9 2.3 %collective-permute-done.8.refs_7_ = bf16[32,16,1024]{2,1,0:T(8,128)(2,1)S(1)} collective-permute-done((bf16[32,16,1024]{2,1,0:T(8,128)(2,1)}, bf16[32,16,1024]{2,1,0:T(8,128)(2,1)S(1)}, u32[]{:S(2)}, u32[]{:S(2)}) %collective-permute-start.8) | collective-permute-done | bytes 1048608 | tf_op jit(solution)/shard_map/ppermute | solution.py:215
  131.2 0.0 copy-start.2
  131.2 1.2 copy-done.2
  132.4 0.0 copy-start.4
  132.5 1.2 copy-done.4
  133.7 0.0 copy-start.5
  133.7 2.2 %copy-done.5 = f32[16,256,256]{2,1,0:T(8,128)S(1)} copy-done((f32[16,256,256]{2,1,0:T(8,128)S(1)}, f32[16,256,256]{2,1,0:T(8,128)}, u32[]{:S(2)}) %copy-start.5) | copy-done | bytes 4194328
  135.9 4.3 %attention_grads.1 = bf16[3,1024,256]{2,1,0:T(8,128)(2,1)S(1)} custom-call(s32[2]{0:T(128)S(1)} %pad_add_fusion.place, f32[16,256,256]{2,1,0:T(8,128)S(1)} %copy-done.5, bf16[256,4096]{1,0:T(8,128)(2,1)S(1)} %bitcast.16, bf16[256,4096]{1,0:T(8,128)(2,1)S(1)} %bitcast.17, bf16[256,4096]{1,0:T(8,128)(2,1)S(1)} %bitcast.18, bf16[256,4096]{1,0:T(8,128)(2,1)S(1)} %bitcast.19, ...), custom_call_target="tpu_custom_call" | custom-call | flops 3000000000 | bytes 10485760 | tf_op jit(solution)/shard_map/attention_grads/pallas_call | solution.py:147
  140.1 3.8 %input_projection.1 = bf16[256,1024]{1,0:T(8,128)(2,1)} custom-call(s32[2]{0:T(128)S(1)} %pad_add_fusion.place, bf16[3072,256]{1,0:T(8,128)(2,1)S(1)} %bitcast.20, bf16[32,16,1024]{2,1,0:T(8,128)(2,1)S(1)} %all-to-all-done.refs_0_, bf16[32,16,1024]{2,1,0:T(8,128)(2,1)S(1)} %copy-done.4, bf16[32,16,1024]{2,1,0:T(8,128)(2,1)S(1)} %constant_dynamic-update-slice_fusion.refs_2_, ...), custom_call_target="tpu_custom_call" | custom-call | flops 2000000000 | bytes 8388608 | tf_op jit(solution)/shard_map/input_projection/pallas_call | solution.py:184
  144.0 0.4 all-to-all-done.2.s_ref
  144.4 7.4 %all-to-all-start.3 = ((bf16[32,8,1024]{2,1,0:T(8,128)(2,1)}), bf16[32,8,1024]{2,1,0:T(8,128)(2,1)S(1)}, u32[]{:S(2)}, u32[]{:S(2)}) async-start(bf16[32,8,1024]{2,1,0:T(8,128)(2,1)} %bitcast.8), calls=%async_computation.3 | async-start | bytes 1048576 | tf_op jit(solution)/shard_map/all_to_all | solution.py:307
  151.8 1.3 sum_shares.1
  153.1 3.1 %collective-permute-start.9 = (f32[16,1024]{1,0:T(8,128)S(1)}, f32[16,1024]{1,0:T(8,128)S(1)}, u32[]{:S(2)}, u32[]{:S(2)}) collective-permute-start(f32[16,1024]{1,0:T(8,128)S(1)} %sum_shares.1), channel_id=1, source_target_pairs={{0,1},{1,0},{2,3},{3,2},{4,5},{5,4},{6,7},{7,6},{8,9},{9,8},{10,11... | collective-permute-start | bytes 196616 | tf_op jit(solution)/shard_map/ppermute | solution.py:280
  156.2 2.2 %collective-permute-done.9 = f32[16,1024]{1,0:T(8,128)S(1)} collective-permute-done((f32[16,1024]{1,0:T(8,128)S(1)}, f32[16,1024]{1,0:T(8,128)S(1)}, u32[]{:S(2)}, u32[]{:S(2)}) %collective-permute-start.9) | collective-permute-done | bytes 65568 | tf_op jit(solution)/shard_map/ppermute | solution.py:280
  158.5 4.7 %collective-permute-start.10 = (f32[16,1024]{1,0:T(8,128)S(1)}, f32[16,1024]{1,0:T(8,128)S(1)}, u32[]{:S(2)}, u32[]{:S(2)}) collective-permute-start(f32[16,1024]{1,0:T(8,128)S(1)} %add.17), channel_id=1, source_target_pairs={{0,2},{1,3},{2,0},{3,1},{4,6},{5,7},{6,4},{7,5},{8,10},{9,11},{10,... | collective-permute-start | bytes 196616 | tf_op jit(solution)/shard_map/ppermute | solution.py:280
  163.2 2.1 %collective-permute-done.10 = f32[16,1024]{1,0:T(8,128)S(1)} collective-permute-done((f32[16,1024]{1,0:T(8,128)S(1)}, f32[16,1024]{1,0:T(8,128)S(1)}, u32[]{:S(2)}, u32[]{:S(2)}) %collective-permute-start.10) | collective-permute-done | bytes 65568 | tf_op jit(solution)/shard_map/ppermute | solution.py:280
  165.3 7.9 %collective-permute-start.11 = (f32[16,1024]{1,0:T(8,128)S(1)}, f32[16,1024]{1,0:T(8,128)S(1)}, u32[]{:S(2)}, u32[]{:S(2)}) collective-permute-start(f32[16,1024]{1,0:T(8,128)S(1)} %add.18), channel_id=1, source_target_pairs={{0,4},{4,0},{1,5},{5,1},{2,6},{6,2},{3,7},{7,3},{8,12},{12,8},{9,1... | collective-permute-start | bytes 196616 | tf_op jit(solution)/shard_map/ppermute | solution.py:309
  173.3 0.0 all-to-all-done.3
  173.3 1.4 write_out.1
  174.7 0.3 collective-permute-done.11
  175.0 0.6 add.19
  (4 shorter events, 0.0 us)
Async XLA Ops:
  0.6 0.9 copy-start
  2.7 40.1 %all-to-all-start = ((bf16[32,16,1024]{2,1,0:T(8,128)(2,1)}), bf16[32,16,1024]{2,1,0:T(8,128)(2,1)S(1)}, u32[]{:S(2)}, u32[]{:S(2)}) async-start(bf16[32,16,1024]{2,1,0:T(8,128)(2,1)} %broadcast_in_dim.2), calls=%async_computation | async-start | bytes 2097152 | tf_op jit(solution)/shard_map/all_to_all | solution.py:291
  42.8 58.2 %all-to-all-start.1 = ((bf16[32,8,4096]{2,1,0:T(8,128)(2,1)}), bf16[32,8,4096]{2,1,0:T(8,128)(2,1)S(1)}, u32[]{:S(2)}, u32[]{:S(2)}) async-start(bf16[32,8,4096]{2,1,0:T(8,128)(2,1)} %pad_maximum_fusion), calls=%async_computation.1 | async-start | bytes 4194304 | tf_op jit(solution)/shard_map/all_to_all | solution.py:297
  50.2 27.6 %collective-permute-start.1 = (bf16[32,16,1024]{2,1,0:T(8,128)(2,1)S(1)}, bf16[32,16,1024]{2,1,0:T(8,128)(2,1)S(1)}, u32[]{:S(2)}, u32[]{:S(2)}) collective-permute-start(bf16[32,16,1024]{2,1,0:T(8,128)(2,1)S(1)} %all-to-all-done.refs_0_), channel_id=1, source_target_pairs={{0,1},{1,2},{2,3},{3,0},{4,5},{5,6},{6,7},{7,4},{8,9},{9,10},{10,1... | collective-permute-start | bytes 3145736 | tf_op jit(solution)/shard_map/ppermute | solution.py:221
  53.3 27.3 %collective-permute-start = (bf16[32,16,1024]{2,1,0:T(8,128)(2,1)S(1)}, bf16[32,16,1024]{2,1,0:T(8,128)(2,1)S(1)}, u32[]{:S(2)}, u32[]{:S(2)}) collective-permute-start(bf16[32,16,1024]{2,1,0:T(8,128)(2,1)S(1)} %all-to-all-done.refs_0_), channel_id=1, source_target_pairs={{0,3},{1,0},{2,1},{3,2},{4,7},{5,4},{6,5},{7,6},{8,11},{9,8},{10,9... | collective-permute-start | bytes 3145736 | tf_op jit(solution)/shard_map/ppermute | solution.py:220
  77.8 2.8 %copy-start.1 = (bf16[32,16,1024]{2,1,0:T(8,128)(2,1)}, bf16[32,16,1024]{2,1,0:T(8,128)(2,1)S(1)}, u32[]{:S(2)}) copy-start(bf16[32,16,1024]{2,1,0:T(8,128)(2,1)S(1)} %collective-permute-done.1.refs_3_) | copy-start | bytes 3145732
  78.7 15.8 %collective-permute-start.2 = (bf16[16,16,1024]{2,1,0:T(8,128)(2,1)}, bf16[16,16,1024]{2,1,0:T(8,128)(2,1)}, u32[]{:S(2)}, u32[]{:S(2)}) collective-permute-start(bf16[16,16,1024]{2,1,0:T(8,128)(2,1)} %slice.8), channel_id=1, source_target_pairs={{0,1},{1,2},{2,3},{3,0},{4,5},{5,6},{6,7},{7,4},{8,9},{9,10},{10,1... | collective-permute-start | bytes 1572872 | tf_op jit(solution)/shard_map/ppermute | solution.py:222
  80.7 1.1 copy-start.3
  81.8 14.8 %collective-permute-start.3 = (bf16[16,16,1024]{2,1,0:T(8,128)(2,1)}, bf16[16,16,1024]{2,1,0:T(8,128)(2,1)}, u32[]{:S(2)}, u32[]{:S(2)}) collective-permute-start(bf16[16,16,1024]{2,1,0:T(8,128)(2,1)} %slice.9), channel_id=1, source_target_pairs={{0,3},{1,0},{2,1},{3,2},{4,7},{5,4},{6,5},{7,6},{8,11},{9,8},{10,9... | collective-permute-start | bytes 1572872 | tf_op jit(solution)/shard_map/ppermute | solution.py:223
  105.5 5.0 %collective-permute-start.4 = (bf16[512,1024]{1,0:T(8,128)(2,1)S(1)}, bf16[512,1024]{1,0:T(8,128)(2,1)S(1)}, u32[]{:S(2)}, u32[]{:S(2)}) collective-permute-start(bf16[512,1024]{1,0:T(8,128)(2,1)S(1)} %get-tuple-element.39), channel_id=1, source_target_pairs={{0,8},{8,0},{1,9},{9,1},{2,10},{10,2},{3,11},{11,3},{4,12},{12,4},... | collective-permute-start | bytes 3145736 | tf_op jit(solution)/shard_map/ppermute | solution.py:215
  110.8 1.1 copy-start.6
  111.9 32.5 %all-to-all-start.2 = ((bf16[32,16,1024]{2,1,0:T(8,128)(2,1)}), bf16[32,16,1024]{2,1,0:T(8,128)(2,1)}, u32[]{:S(2)}, u32[]{:S(2)}) async-start(bf16[32,16,1024]{2,1,0:T(8,128)(2,1)} %bitcast.21), calls=%async_computation.2 | async-start | bytes 2097152 | tf_op jit(solution)/shard_map/all_to_all | solution.py:301
  119.5 8.8 %collective-permute-start.7 = (bf16[32,16,1024]{2,1,0:T(8,128)(2,1)S(1)}, bf16[32,16,1024]{2,1,0:T(8,128)(2,1)S(1)}, u32[]{:S(2)}, u32[]{:S(2)}) collective-permute-start(bf16[32,16,1024]{2,1,0:T(8,128)(2,1)S(1)} %constant_dynamic-update-slice_fusion.refs_2_), channel_id=1, source_target_pairs={{0,8},{8,0},{1,9},{9,1},{2,10},{10,2},{3,11},{11,3},{4,12},{12,4},... | collective-permute-start | bytes 3145736 | tf_op jit(solution)/shard_map/ppermute | solution.py:215
  122.1 6.3 %collective-permute-start.5 = (bf16[32,16,1024]{2,1,0:T(8,128)(2,1)S(1)}, bf16[32,16,1024]{2,1,0:T(8,128)(2,1)S(1)}, u32[]{:S(2)}, u32[]{:S(2)}) collective-permute-start(bf16[32,16,1024]{2,1,0:T(8,128)(2,1)S(1)} %all-to-all-done.refs_0_), channel_id=1, source_target_pairs={{0,8},{8,0},{1,9},{9,1},{2,10},{10,2},{3,11},{11,3},{4,12},{12,4},... | collective-permute-start | bytes 3145736 | tf_op jit(solution)/shard_map/ppermute | solution.py:215
  124.0 4.9 %collective-permute-start.6 = (bf16[32,16,1024]{2,1,0:T(8,128)(2,1)}, bf16[32,16,1024]{2,1,0:T(8,128)(2,1)S(1)}, u32[]{:S(2)}, u32[]{:S(2)}) collective-permute-start(bf16[32,16,1024]{2,1,0:T(8,128)(2,1)} %copy-done.3), channel_id=1, source_target_pairs={{0,8},{8,0},{1,9},{9,1},{2,10},{10,2},{3,11},{11,3},{4,12},{12,4},... | collective-permute-start | bytes 3145736 | tf_op jit(solution)/shard_map/ppermute | solution.py:215
  126.5 4.8 %collective-permute-start.8 = (bf16[32,16,1024]{2,1,0:T(8,128)(2,1)}, bf16[32,16,1024]{2,1,0:T(8,128)(2,1)S(1)}, u32[]{:S(2)}, u32[]{:S(2)}) collective-permute-start(bf16[32,16,1024]{2,1,0:T(8,128)(2,1)} %copy-done.1), channel_id=1, source_target_pairs={{0,8},{8,0},{1,9},{9,1},{2,10},{10,2},{3,11},{11,3},{4,12},{12,4},... | collective-permute-start | bytes 3145736 | tf_op jit(solution)/shard_map/ppermute | solution.py:215
  131.2 1.2 copy-start.2
  132.4 1.2 copy-start.4
  133.7 2.2 %copy-start.5 = (f32[16,256,256]{2,1,0:T(8,128)S(1)}, f32[16,256,256]{2,1,0:T(8,128)}, u32[]{:S(2)}) copy-start(f32[16,256,256]{2,1,0:T(8,128)} %get-tuple-element.45.attention_ref) | copy-start | bytes 12582916
  144.4 28.9 %all-to-all-start.3 = ((bf16[32,8,1024]{2,1,0:T(8,128)(2,1)}), bf16[32,8,1024]{2,1,0:T(8,128)(2,1)S(1)}, u32[]{:S(2)}, u32[]{:S(2)}) async-start(bf16[32,8,1024]{2,1,0:T(8,128)(2,1)} %bitcast.8), calls=%async_computation.3 | async-start | bytes 1048576 | tf_op jit(solution)/shard_map/all_to_all | solution.py:307
  153.1 5.4 %collective-permute-start.9 = (f32[16,1024]{1,0:T(8,128)S(1)}, f32[16,1024]{1,0:T(8,128)S(1)}, u32[]{:S(2)}, u32[]{:S(2)}) collective-permute-start(f32[16,1024]{1,0:T(8,128)S(1)} %sum_shares.1), channel_id=1, source_target_pairs={{0,1},{1,0},{2,3},{3,2},{4,5},{5,4},{6,7},{7,6},{8,9},{9,8},{10,11... | collective-permute-start | bytes 196616 | tf_op jit(solution)/shard_map/ppermute | solution.py:280
  158.5 6.8 %collective-permute-start.10 = (f32[16,1024]{1,0:T(8,128)S(1)}, f32[16,1024]{1,0:T(8,128)S(1)}, u32[]{:S(2)}, u32[]{:S(2)}) collective-permute-start(f32[16,1024]{1,0:T(8,128)S(1)} %add.17), channel_id=1, source_target_pairs={{0,2},{1,3},{2,0},{3,1},{4,6},{5,7},{6,4},{7,5},{8,10},{9,11},{10,... | collective-permute-start | bytes 196616 | tf_op jit(solution)/shard_map/ppermute | solution.py:280
  165.3 9.7 %collective-permute-start.11 = (f32[16,1024]{1,0:T(8,128)S(1)}, f32[16,1024]{1,0:T(8,128)S(1)}, u32[]{:S(2)}, u32[]{:S(2)}) collective-permute-start(f32[16,1024]{1,0:T(8,128)S(1)} %add.18), channel_id=1, source_target_pairs={{0,4},{4,0},{1,5},{5,1},{2,6},{6,2},{3,7},{7,3},{8,12},{12,8},{9,1... | collective-permute-start | bytes 196616 | tf_op jit(solution)/shard_map/ppermute | solution.py:309
